TPU v7x, 128 devices: a whole 4x4x4 slice. The times are simulated.
128 devices in a mesh: row: 8 (over x, z_hi), col: 16 (over y, z_lo, core).
Axes of the slice: x: 4, y: 4, z: 4 (z_hi: 2, z_lo: 2; z = z_hi * 2 + z_lo), core: 2. Of those that a mesh axis runs over, the one named last changes fastest.
Arguments:
- features: bfloat16 [65536, 128], P(('col', 'row')), may hold values from -6 to 6
- weight: bfloat16 [128, 256], replicated, may hold values from -0.5 to 0.5
- bias: float32 [256], replicated, may hold values from -3 to 3
- tile_values: bfloat16 [8, 16, 704, 128, 128], P('row', 'col'), may hold values from -0.0390625 to 0.0390625
- tile_rows: int32 [8, 16, 704], P('row', 'col'), may hold values from 0 to 63
- tile_cols: int32 [8, 16, 704], P('row', 'col'), may hold values from 0 to 31
- tile_count: int32 [8, 16], P('row', 'col'), may hold values from 88 to 704, as said below
- upstream: bfloat16 [65536, 256], P(('row', 'col')), may hold values from -6 to 6
Outputs:
- activated: bfloat16 [65536, 256], P(('row', 'col'))
- feature_grad: bfloat16 [65536, 128], P(('col', 'row'))
- weight_grad: float32 [128, 256], replicated
- bias_grad: float32 [256], replicated
Inputs may be any that keep to these rules, and one draw needn't show every extreme that they name: Each device uses only its first tile_count slots; some devices use all 704.
All inputs are finite; a program needn't handle non-finite values.
Results may differ from a plain program's by a relative error of at most 0.0075.
Values may be sent and summed in bfloat16 or wider, within the bound.
No kernel may reach another device: no remote copies, remote signals or barrier semaphores. Data moves between devices by JAX's collectives and lax.ppermute only.
A program may use at most 256 MiB of HBM per device.

v0:
```python
import jax
import jax.numpy as jnp
from jax import lax
from jax.sharding import PartitionSpec as P


def tile_products(values, source, index, transposed):
    num_src = source.shape[0]
    select = (index[:, None] == jnp.arange(num_src, dtype=jnp.int32)[None, :]).astype(jnp.bfloat16)
    flat_src = source.reshape(num_src, -1)
    picked = jnp.dot(select, flat_src, preferred_element_type=jnp.float32).astype(jnp.bfloat16)
    picked = picked.reshape((index.shape[0],) + source.shape[1:])
    if transposed:
        return jnp.einsum("tba,tbf->taf", values, picked, preferred_element_type=jnp.float32)
    return jnp.einsum("tab,tbf->taf", values, picked, preferred_element_type=jnp.float32)


def accumulate(products, target, live, first_tile, num_out):
    local = target - first_tile
    inside = live & (local >= 0) & (local < num_out)
    placed = jnp.where(inside, local, num_out)
    onehot = (jnp.arange(num_out, dtype=jnp.int32)[:, None] == placed[None, :]).astype(jnp.float32)
    flat_prod = products.reshape(products.shape[0], -1)
    summed = jnp.dot(
        onehot, flat_prod, precision=lax.Precision.HIGHEST, preferred_element_type=jnp.float32
    )
    return summed.reshape((num_out,) + products.shape[1:])


def shards(features, weight, bias, tile_values, tile_rows, tile_cols, tile_count, upstream):
    tile_side = tile_values.shape[3]
    width_in = features.shape[1]
    values = tile_values[0, 0]
    rows = tile_rows[0, 0]
    cols = tile_cols[0, 0]
    count = tile_count[0, 0]
    node_rows = features.shape[0]
    row_tiles = node_rows * lax.axis_size("col") // tile_side
    col_tiles = node_rows * lax.axis_size("row") // tile_side
    slots = jnp.arange(values.shape[0], dtype=jnp.int32)
    live = slots < count
    gathered = lax.all_gather(features, "row", axis=0, tiled=True)
    source = gathered.reshape(col_tiles, tile_side, width_in)
    forward_prod = tile_products(values, source, cols, False)
    partial_value = accumulate(forward_prod, rows, live, 0, row_tiles)
    partial_value = partial_value.reshape(row_tiles * tile_side, width_in)
    summed = lax.psum_scatter(partial_value, "col", scatter_dimension=0, tiled=True)
    s_half = summed.astype(jnp.bfloat16)
    pre = jnp.dot(s_half, weight, preferred_element_type=jnp.float32) + bias
    activated = jax.nn.gelu(pre, approximate=True).astype(jnp.bfloat16)
    unused_out, pullback = jax.vjp(lambda v: jax.nn.gelu(v, approximate=True), pre)
    grad_pre = pullback(upstream.astype(jnp.float32))[0].astype(jnp.bfloat16)
    weight_term = jnp.dot(s_half.T, grad_pre, preferred_element_type=jnp.float32)
    bias_term = jnp.sum(grad_pre.astype(jnp.float32), axis=0)
    weight_grad, bias_grad = lax.psum((weight_term, bias_term), ("row", "col"))
    grad_agg = jnp.dot(grad_pre, weight.T, preferred_element_type=jnp.float32).astype(jnp.bfloat16)
    block = lax.all_gather(grad_agg, "col", axis=0, tiled=True)
    back_source = block.reshape(row_tiles, tile_side, width_in)
    back_prod = tile_products(values, back_source, rows, True)
    back_partial = accumulate(back_prod, cols, live, 0, col_tiles)
    back_partial = back_partial.reshape(col_tiles * tile_side, width_in)
    feature_grad = lax.psum_scatter(back_partial, "row", scatter_dimension=0, tiled=True).astype(
        jnp.bfloat16
    )
    return (activated, feature_grad, weight_grad, bias_grad)


def solution(mesh):
    in_specs = (
        P(("col", "row"), None),
        P(),
        P(),
        P("row", "col", None, None, None),
        P("row", "col", None),
        P("row", "col", None),
        P("row", "col"),
        P(("row", "col"), None),
    )
    out_specs = (P(("row", "col"), None), P(("col", "row"), None), P(), P())
    return jax.shard_map(shards, mesh=mesh, in_specs=in_specs, out_specs=out_specs, check_vma=False)
```

profile of v0, /device:TPU:0, one launch (start us, length us, event | category | flops | bytes accessed | tf_op | source)
XLA Modules:
  0.0 734.4 jit_solution(17161399045825978746)
XLA Ops:
  7.2 0.0 copy-start
  7.2 0.0 all-gather.3.cloned.1.call-start
  7.2 0.7 all-gather.3.cloned.1.call-update
  7.9 0.0 reduce-scatter.3.cloned.1.call-start
  8.6 0.7 reduce
  9.3 0.7 reduce.1
  10.0 0.6 fusion.38
  10.6 49.6 %all-gather.3.cloned.1.call-done = bf16[4096,128]{1,0:T(8,128)(2,1)} async-done(((bf16[512,128]{1,0:T(8,128)(2,1)}), bf16[4096,128]{1,0:T(8,128)(2,1)}) %all-gather.3.cloned.1.call-update) | async-done | bytes 1048592 | tf_op jit(solution)/shard_map/all_gather | solution.py:42
  60.2 1.5 reshape_reshape.12
  61.8 10.9 %fusion.16 = bf16[88,8,128,128]{3,1,2,0:T(8,128)(2,1)} fusion(bf16[32,16384]{1,0:T(8,128)(2,1)S(1)} %reshape_reshape.12, s32[704]{0:T(1024)S(1)} %reduce.1), kind=kOutput, calls=%fused_computation.14 | convolution fusion | flops 749754368 | bytes 24120064 | tf_op jit(solution)/shard_map/dot_general | solution.py:11
  72.7 21.9 %copy.20 = bf16[88,8,128,128]{3,2,1,0:T(8,128)(2,1)} copy(bf16[88,8,128,128]{3,1,2,0:T(8,128)(2,1)} %fusion.16) | data formatting | bytes 46137344
  94.6 37.5 %fusion.10 = f32[704,128,128]{1,2,0:T(8,128)} fusion(bf16[704,128,128]{2,1,0:T(8,128)(2,1)} %bitcast.39, bf16[1,1,704,128,128]{4,3,2,1,0:T(8,128)(2,1)} %param.11), kind=kOutput, calls=%fused_computation.12 | convolution fusion | flops 2952790016 | bytes 92274688 | tf_op jit(solution)/shard_map/tab,tbf->taf/dot_general | solution.py:15
  132.1 45.5 %copy.15 = f32[704,128,128]{2,1,0:T(8,128)} copy(f32[704,128,128]{1,2,0:T(8,128)} %fusion.10) | data formatting | bytes 92274688 | tf_op jit(solution)/shard_map/tab,tbf->taf/dot_general | solution.py:15
  177.6 0.0 copy-start.4
  177.6 0.0 copy-start.5
  177.6 58.6 %fusion.3 = f32[64,16384]{1,0:T(8,128)} fusion(f32[88,8,128,128]{3,2,1,0:T(8,128)} %bitcast.38, s32[704]{0:T(1024)S(1)} %get-tuple-element.7), kind=kOutput, calls=%fused_computation.3 | convolution fusion | flops 8858415104 | bytes 50334464 | tf_op jit(solution)/shard_map/dot_general | solution.py:24
  236.3 4.9 reshape_reshape.13
  241.2 0.0 reduce-scatter.3.cloned.1.call-update
  241.2 0.0 all-gather.5.cloned.1.call-start
  241.3 66.3 %reduce-scatter.3.cloned.1.call-done = f32[512,128]{1,0:T(8,128)} async-done(((f32[8192,128]{1,0:T(8,128)}), f32[512,128]{1,0:T(8,128)}) %reduce-scatter.3.cloned.1.call-update) | async-done | bytes 262160 | tf_op jit(solution)/shard_map/reduce_scatter | solution.py:47
  307.6 0.0 copy-done
  307.6 0.0 copy-done.4
  307.6 0.0 copy-done.5
  307.6 2.2 convert_reduce_fusion
  309.8 0.9 convolution_convert_fusion.2
  310.7 0.0 all-gather.5.cloned.1.call-update
  310.7 0.0 reduce-scatter.5.cloned.1.call-start
  310.8 32.5 %all-gather.5.cloned.1.call-done = bf16[8192,128]{1,0:T(8,128)(2,1)} async-done(((bf16[512,128]{1,0:T(8,128)(2,1)}), bf16[8192,128]{1,0:T(8,128)(2,1)}) %all-gather.5.cloned.1.call-update) | async-done | bytes 2097168 | tf_op jit(solution)/shard_map/all_gather | solution.py:57
  343.3 3.0 reshape_reshape.14
  346.3 10.9 %fusion.17 = bf16[88,8,128,128]{3,1,2,0:T(8,128)(2,1)} fusion(bf16[64,16384]{1,0:T(8,128)(2,1)S(1)} %reshape_reshape.14, s32[704]{0:T(1024)S(1)} %reduce), kind=kOutput, calls=%fused_computation.15 | convolution fusion | flops 1487974400 | bytes 25168640 | tf_op jit(solution)/shard_map/dot_general | solution.py:11
  357.1 21.9 %copy.22 = bf16[88,8,128,128]{3,2,1,0:T(8,128)(2,1)} copy(bf16[88,8,128,128]{3,1,2,0:T(8,128)(2,1)} %fusion.17) | data formatting | bytes 46137344
  379.1 28.8 %fusion.13 = f32[704,128,128]{1,2,0:T(8,128)} fusion(bf16[704,128,128]{2,1,0:T(8,128)(2,1)} %bitcast.40, bf16[1,1,704,128,128]{4,3,2,1,0:T(8,128)(2,1)} %param.11), kind=kOutput, calls=%fused_computation.13 | convolution fusion | flops 2952790016 | bytes 92274688 | tf_op jit(solution)/shard_map/tba,tbf->taf/dot_general | solution.py:14
  407.8 0.0 copy-start.3
  407.8 45.5 %copy.17 = f32[704,128,128]{2,1,0:T(8,128)} copy(f32[704,128,128]{1,2,0:T(8,128)} %fusion.13) | data formatting | bytes 92274688 | tf_op jit(solution)/shard_map/tba,tbf->taf/dot_general | solution.py:14
  453.4 0.0 copy-done.3
  453.4 0.0 copy-start.2
  453.4 0.0 copy-start.1
  453.4 50.6 %fusion = f32[32,16384]{1,0:T(8,128)S(1)} fusion(f32[88,8,128,128]{3,2,1,0:T(8,128)} %bitcast.37, s32[704]{0:T(1024)S(1)} %copy-done.3), kind=kOutput, calls=%fused_computation | convolution fusion | flops 4429207552 | bytes 48237312 | tf_op jit(solution)/shard_map/dot_general | solution.py:24
  504.0 1.5 reshape_reshape.15
  505.5 0.0 reduce-scatter.5.cloned.1.call-update
  505.5 0.0 all-reduce.2.cloned.1.call-start
  505.6 0.0 copy-done.2
  505.6 0.9 fusion.31
  506.5 0.0 all-reduce.2.cloned.1.call-update
  506.5 68.6 %psum.15 = f32[256]{0:T(256)} all-reduce(f32[256]{0:T(256)S(1)} %get-tuple-element.4), channel_id=1, replica_groups=mesh['row'=8,'col'=16] {'row','col'}, use_global_device_ids=true, to_apply=%region_4.5 | all-reduce | flops 256 | bytes 2048 | tf_op jit(solution)/shard_map/psum | solution.py:55
  575.0 6.5 reduce-scatter.5.cloned.1.call-done
  581.6 1.6 convert_element_type.38
  583.2 142.8 %all-reduce.2.cloned.1.call-done = f32[128,256]{1,0:T(8,128)} async-done(((f32[128,256]{1,0:T(8,128)}), f32[128,256]{1,0:T(8,128)}) %all-reduce.2.cloned.1.call-update) | async-done | bytes 131088 | tf_op jit(solution)/shard_map/psum | solution.py:55
  726.0 1.6 copy.34
  727.5 0.0 copy-done.1
Async XLA Ops:
  7.2 300.4 %copy-start = (bf16[128,256]{1,0:T(8,128)(2,1)S(1)}, bf16[128,256]{1,0:T(8,128)(2,1)}, u32[]{:S(2)}) copy-start(bf16[128,256]{1,0:T(8,128)(2,1)} %param.9) | copy-start | bytes 196612
  7.2 53.1 %all-gather.3.cloned.1.call-start = ((), (), s32[]{:S(2)}) async-start(), calls=%async_computation.2 | async-start | bytes 1179648 | tf_op jit(solution)/shard_map/all_gather | solution.py:42
  7.9 299.7 %reduce-scatter.3.cloned.1.call-start = ((), (), s32[]{:S(2)}) async-start(), calls=%async_computation.3 | async-start | bytes 4456448 | tf_op jit(solution)/shard_map/reduce_scatter | solution.py:47
  177.6 130.0 %copy-start.4 = (bf16[512,256]{1,0:T(8,128)(2,1)S(1)}, bf16[512,256]{1,0:T(8,128)(2,1)}, u32[]{:S(2)}) copy-start(bf16[512,256]{1,0:T(8,128)(2,1)} %param.15) | copy-start | bytes 786436
  177.6 130.0 %copy-start.5 = (f32[256]{0:T(256)S(1)}, f32[256]{0:T(256)}, u32[]{:S(2)}) copy-start(f32[256]{0:T(256)} %param.10) | copy-start | bytes 3076
  241.2 102.0 %all-gather.5.cloned.1.call-start = ((), (), s32[]{:S(2)}) async-start(), calls=%async_computation.4 | async-start | bytes 2228224 | tf_op jit(solution)/shard_map/all_gather | solution.py:57
  310.7 270.8 %reduce-scatter.5.cloned.1.call-start = ((), (), s32[]{:S(2)}) async-start(), calls=%async_computation.5 | async-start | bytes 2359296 | tf_op jit(solution)/shard_map/reduce_scatter | solution.py:62
  407.8 45.5 %copy-start.3 = (s32[704]{0:T(1024)S(1)}, s32[704]{0:T(1024)}, u32[]{:S(2)}) copy-start(s32[704]{0:T(1024)} %get-tuple-element.8) | copy-start | bytes 8452
  453.4 52.2 %copy-start.2 = (f32[512,128]{1,0:T(8,128)S(1)}, f32[512,128]{1,0:T(8,128)}, u32[]{:S(2)}) copy-start(f32[512,128]{1,0:T(8,128)} %reduce-scatter.3.cloned.1.call-done) | copy-start | bytes 786436
  453.4 274.1 %copy-start.1 = (bf16[128,256]{1,0:T(8,128)(2,1)S(1)}, bf16[128,256]{1,0:T(8,128)(2,1)}, u32[]{:S(2)}) copy-start(bf16[128,256]{1,0:T(8,128)(2,1)} %param.9) | copy-start | bytes 196612
  505.5 220.4 %all-reduce.2.cloned.1.call-start = ((), (), s32[]{:S(2)}) async-start(), calls=%async_computation.6 | async-start | bytes 262144 | tf_op jit(solution)/shard_map/psum | solution.py:55
Sparse Core Ops, SparseCore 0:
  10.4 49.8 all-gather.2
  241.3 66.2 reduce-scatter.2
  310.9 32.3 all-gather.4
  505.6 75.9 reduce-scatter.4
  587.5 138.4 all-reduce.1
where the time goes:
time: 742 us; the launch traced here: 734 us
  waiting for transfers between devices  298 us (40%)
  matrix products  201 us (27%)
  local copies, waits for them, and re-layouts  148 us (20%)
  blocking collectives  68.6 us (9%)
  between operations  14.9 us (2%)
    psum x1, waiting for transfers between devices, shards(): weight_grad, bias_grad = lax.psum((weight_term, bias_term), ('row', 'col'))  143 us
    dot_general x2, matrix products, accumulate(): jnp.dot(onehot, flat_prod, precision=lax.Precision.HIGHEST, preferred_ele...  109 us
    psum x1, blocking collectives, shards(): weight_grad, bias_grad = lax.psum((weight_term, bias_term), ('row', 'col'))  68.6 us
    reduce_scatter x1, waiting for transfers between devices, shards(): lax.psum_scatter(partial_value, 'col', scatter_dimension=0, tiled=True)  66.3 us
    all_gather x1, waiting for transfers between devices, shards(): gathered = lax.all_gather(features, 'row', axis=0, tiled=True)  49.6 us
    dot_general x1, local copies, waits for them, and re-layouts, tile_products(): jnp.einsum('tba,tbf->taf', values, picked, preferred_element_type=jnp.flo...  45.5 us
    dot_general x1, local copies, waits for them, and re-layouts, tile_products(): jnp.einsum('tab,tbf->taf', values, picked, preferred_element_type=jnp.flo...  45.5 us
    unnamed x15, local copies, waits for them, and re-layouts  45.5 us
  transfers between devices with their start and end apart: 5, of which 5 were waited for; matrix products, arithmetic and copies ran while one was open for 1% of the time, Pallas kernels for 0%

commit v1 on v0

v1 whole, which is shorter than its diff:
```python
import functools

import jax
import jax.numpy as jnp
from jax import lax
from jax.experimental import pallas as pl
from jax.experimental.pallas import tpu as pltpu
from jax.sharding import PartitionSpec as P

HALF = jnp.bfloat16
FULL = jnp.float32


def swap(array, axis, distance):
    size = lax.axis_size(axis)
    return lax.ppermute(array, axis, [(j, j ^ distance) for j in range(size)])


def tile_kernel(chunk, num_pieces, flip, live_ref, source_ref, target_ref, *refs):
    values_hbm = refs[0]
    pieces = refs[1 : 1 + num_pieces]
    outs = refs[1 + num_pieces : -4]
    source, values, total, sems = refs[-4:]
    num_chunks = values.shape[0] // chunk

    def copy(i):
        span = pl.ds(i * chunk, chunk)
        return pltpu.make_async_copy(values_hbm.at[span], values.at[span], sems.at[i])

    live_chunks = live_ref[0]
    for i in range(num_chunks):

        @pl.when(i < live_chunks)
        def _():
            copy(i).start()

    first = 0
    for piece in pieces:
        source[pl.ds(first, piece.shape[0])] = piece[...]
        first += piece.shape[0]
    total[...] = jnp.zeros_like(total)

    def step(i, carry):
        copy(i).wait()
        products = []
        for u in range(chunk):
            slot = i * chunk + u
            picked = source[source_ref[slot]]
            pair = (picked, values[slot]) if flip else (values[slot], picked)
            products.append(jnp.dot(*pair, preferred_element_type=FULL))
        for u in range(chunk):
            total[target_ref[i * chunk + u]] += products[u]
        return carry

    lax.fori_loop(0, live_chunks, step, 0)
    first = 0
    for out in outs:
        out[...] = total[pl.ds(first, out.shape[0])].astype(out.dtype)
        first += out.shape[0]


def tile_sums(values, pieces, source_index, target_index, count, out_types, flip):
    slots, side, _ = values.shape
    chunk = max(d for d in range(1, 65) if slots % d == 0)
    num_source = sum(piece.shape[0] for piece in pieces)
    num_out = sum(n for n, _ in out_types)
    width = pieces[0].shape[2]
    target_index = jnp.where(jnp.arange(slots, dtype=jnp.int32) < count, target_index, num_out)
    live_chunks = ((count + chunk - 1) // chunk).reshape(1)
    smem = pl.BlockSpec(memory_space=pltpu.SMEM)
    vmem = pl.BlockSpec(memory_space=pltpu.VMEM)
    return pl.pallas_call(
        functools.partial(tile_kernel, chunk, len(pieces), flip),
        out_shape=[jax.ShapeDtypeStruct((n, side, width), kind) for n, kind in out_types],
        in_specs=[smem] * 3 + [pl.BlockSpec(memory_space=pl.ANY)] + [vmem] * len(pieces),
        out_specs=[vmem] * len(out_types),
        scratch_shapes=[
            pltpu.VMEM((num_source, side, width), HALF),
            pltpu.VMEM((slots, side, side), HALF),
            pltpu.VMEM((num_out + 1, side, width), FULL),
            pltpu.SemaphoreType.DMA((slots // chunk,)),
        ],
        compiler_params=pltpu.CompilerParams(vmem_limit_bytes=42 * 2**20),
    )(live_chunks, source_index, target_index, values, *pieces)


def all_sum(array):
    half = array.shape[0] // 2
    low, high = array[:half], array[half:]
    odd = lax.axis_index("col") % 2 == 1
    array = jnp.where(odd, high, low) + swap(jnp.where(odd, low, high), "col", 1)
    array = array + swap(array, "col", 2)
    array = (array + swap(array, "col", 4)) + (swap(array, "col", 8) + swap(array, "col", 12))
    array = array + swap(array, "row", 1)
    array = (array + swap(array, "row", 2)) + (swap(array, "row", 4) + swap(array, "row", 6))
    other = swap(array, "col", 1)
    return jnp.concatenate([jnp.where(odd, other, array), jnp.where(odd, array, other)], axis=0)


def shards(features, weight, bias, tile_values, tile_rows, tile_cols, tile_count, upstream):
    side = tile_values.shape[3]
    width = features.shape[1]
    hidden = weight.shape[1]
    nodes = features.shape[0]
    per = nodes // side
    values = tile_values[0, 0]
    rows = tile_rows[0, 0]
    cols = tile_cols[0, 0]
    count = tile_count[0, 0]
    my_row = lax.axis_index("row")
    my_col = lax.axis_index("col")
    row_owner = (rows // per) ^ my_col
    row_place = (row_owner % 2) * (lax.axis_size("col") // 2 * per) + (row_owner // 2) * per + rows % per
    col_place = ((cols // per) ^ my_row) * per + cols % per

    own = features.reshape(per, side, width)
    pair = jnp.concatenate([own, swap(own, "row", 1)], axis=0)
    pieces = [pair] + [swap(pair, "row", d) for d in (2, 4, 6)]
    half_tiles = lax.axis_size("col") // 2 * per
    keep, send = tile_sums(
        values, pieces, col_place, row_place, count, [(half_tiles, FULL), (half_tiles, HALF)], False
    )

    block = (keep + swap(send, "col", 1).astype(FULL)).astype(HALF).reshape(4, 2 * per, side, width)
    total = block[0].astype(FULL)
    for other in [swap(block[d], "col", 4 * d) for d in (1, 2, 3)]:
        total = total + other.astype(FULL)
    away = swap(total[per:].astype(HALF), "col", 2)
    s_half = (total[:per] + away.astype(FULL)).astype(HALF).reshape(nodes, width)

    pre = jnp.dot(s_half, weight, preferred_element_type=FULL) + bias
    activated = jax.nn.gelu(pre, approximate=True).astype(HALF)
    _, pullback = jax.vjp(lambda v: jax.nn.gelu(v, approximate=True), pre)
    grad_pre = pullback(upstream.astype(FULL))[0].astype(HALF)
    grad_tiles = grad_pre.reshape(per, side, hidden)
    grad_agg = jnp.einsum("fh,tbh->tfb", weight, grad_tiles, preferred_element_type=FULL).astype(HALF)

    pair = jnp.concatenate([grad_agg, swap(grad_agg, "col", 2)], axis=0)
    near = [pair] + [swap(pair, "col", d) for d in (4, 8, 12)]
    far = [swap(piece, "col", 1) for piece in near]
    (back,) = tile_sums(
        values, near + far, row_place, col_place, count, [(lax.axis_size("row") * per, HALF)], True
    )

    weight_term = jnp.dot(s_half.T, grad_pre, preferred_element_type=FULL)
    bias_term = jnp.sum(grad_pre.astype(FULL), axis=0)
    terms = jnp.concatenate([weight_term, jnp.broadcast_to(bias_term[None], (16, hidden))], axis=0)
    terms = all_sum(terms)
    weight_grad, bias_grad = terms[:width], terms[width]

    back = back.reshape(4, 2 * per, side, side)
    total = back[0].astype(FULL)
    for other in [swap(back[d], "row", 2 * d) for d in (1, 2, 3)]:
        total = total + other.astype(FULL)
    away = swap(total[per:].astype(HALF), "row", 1)
    total = total[:per] + away.astype(FULL)
    feature_grad = jnp.swapaxes(total, 1, 2).astype(HALF).reshape(nodes, width)
    return (activated, feature_grad, weight_grad, bias_grad)


def solution(mesh):
    in_specs = (
        P(("col", "row"), None),
        P(),
        P(),
        P("row", "col", None, None, None),
        P("row", "col", None),
        P("row", "col", None),
        P("row", "col"),
        P(("row", "col"), None),
    )
    out_specs = (P(("row", "col"), None), P(("col", "row"), None), P(), P())
    return jax.shard_map(shards, mesh=mesh, in_specs=in_specs, out_specs=out_specs, check_vma=False)
```

time: 742 us -> 129 us (0.17)
  waiting for transfers between devices: 298 us -> 56.4 us
  matrix products: 201 us -> 1.74 us
  local copies, waits for them, and re-layouts: 148 us -> 1.52 us
  blocking collectives: 68.6 us -> 0 us
  starting transfers between devices: 0.2 us -> 40.4 us
  Pallas kernels: 0 us -> 23.3 us
  between operations: 14.9 us -> 1.56 us
    dot_general x9 -> x3, matrix products: 201 us -> 1.74 us  [the longest x1 1.29 us: shards(): pre = jnp.dot(s_half, weight, preferred_element_type=FULL) + bias]
    psum x1 -> x0, waiting for transfers between devices: 143 us -> none  [shards(): weight_grad, bias_grad = lax.psum((weight_term, bias_term), ('row', 'col'))]
    dot_general x2 -> x0, local copies, waits for them, and re-layouts: 91.1 us -> none  [the longest x1 45.5 us: tile_products(): jnp.einsum('tba,tbf->taf', values, picked, preferred_element_type=jnp.flo...]
    all_gather x2 -> x0, waiting for transfers between devices: 82.1 us -> none  [the longest x1 49.6 us: shards(): gathered = lax.all_gather(features, 'row', axis=0, tiled=True)]
    reduce_scatter x2 -> x0, waiting for transfers between devices: 72.9 us -> none  [the longest x1 66.3 us: shards(): lax.psum_scatter(partial_value, 'col', scatter_dimension=0, tiled=True)]
    psum x1 -> x0, blocking collectives: 68.6 us -> none  [shards(): weight_grad, bias_grad = lax.psum((weight_term, bias_term), ('row', 'col'))]
    ppermute x0 -> x31, waiting for transfers between devices: none -> 56.4 us  [swap(): return lax.ppermute(array, axis, [(j, j ^ distance) for j in range(size)])]
    unnamed x15 -> x6, local copies, waits for them, and re-layouts: 45.5 us -> 0.02 us
  transfers between devices with their start and end apart: 5 -> 31, of which waited for: 5 -> 16; matrix products, arithmetic and copies ran while one was open for 1% -> 2% of each run, Pallas kernels for 0% -> 9%
where the time goes in v1:
time: 129 us
  waiting for transfers between devices  56.4 us (44%)
  starting transfers between devices  40.4 us (31%)
  Pallas kernels  23.3 us (18%)
  other arithmetic  3.8 us (3%)
  matrix products  1.74 us (1%)
  between operations  1.56 us (1%)
  local copies, waits for them, and re-layouts  1.52 us (1%)
    ppermute x31, waiting for transfers between devices, swap(): return lax.ppermute(array, axis, [(j, j ^ distance) for j in range(size)])  56.4 us
    ppermute x31, starting transfers between devices, swap(): return lax.ppermute(array, axis, [(j, j ^ distance) for j in range(size)])  40.4 us
    pallas_call x2, Pallas kernels, tile_sums(): pl.pallas_call(functools.partial(tile_kernel, chunk, len(pieces), flip),...  23.3 us
  transfers between devices with their start and end apart: 31, of which 16 were waited for; matrix products, arithmetic and copies ran while one was open for 2% of the time, Pallas kernels for 9%

profile of v1, /device:TPU:0, one launch (start us, length us, event | category | flops | bytes accessed | tf_op | source)
XLA Modules:
  0.0 128.8 jit_solution(10515903235568588627)
XLA Ops:
  0.6 0.0 copy-start
  0.6 4.0 %collective-permute-start = (bf16[4,128,128]{2,1,0:T(8,128)(2,1)}, bf16[4,128,128]{2,1,0:T(8,128)(2,1)S(1)}, u32[]{:S(2)}, u32[]{:S(2)}) collective-permute-start(bf16[4,128,128]{2,1,0:T(8,128)(2,1)} %bitcast.28), channel_id=1, source_target_pairs={{0,16},{16,0},{32,48},{48,32},{64,80},{80,64},{96,112},{112,96},{1... | collective-permute-start | bytes 393224 | tf_op jit(solution)/shard_map/ppermute | solution.py:16
  4.7 3.7 %collective-permute-done = bf16[4,128,128]{2,1,0:T(8,128)(2,1)S(1)} collective-permute-done((bf16[4,128,128]{2,1,0:T(8,128)(2,1)}, bf16[4,128,128]{2,1,0:T(8,128)(2,1)S(1)}, u32[]{:S(2)}, u32[]{:S(2)}) %collective-permute-start) | collective-permute-done | bytes 131104 | tf_op jit(solution)/shard_map/ppermute | solution.py:16
  8.4 0.9 pad_maximum_fusion.refs_1_
  9.3 2.8 %collective-permute-start.3 = (bf16[8,128,128]{2,1,0:T(8,128)(2,1)S(1)}, bf16[8,128,128]{2,1,0:T(8,128)(2,1)S(1)}, u32[]{:S(2)}, u32[]{:S(2)}) collective-permute-start(bf16[8,128,128]{2,1,0:T(8,128)(2,1)S(1)} %pad_maximum_fusion.refs_1_), channel_id=1, source_target_pairs={{0,96},{16,112},{32,64},{48,80},{64,32},{80,48},{96,0},{112,16},{1... | collective-permute-start | bytes 786440 | tf_op jit(solution)/shard_map/ppermute | solution.py:16
  12.2 0.8 collective-permute-start.2
  13.0 0.5 collective-permute-start.1
  14.2 0.7 reduce.1
  14.9 0.7 reduce
  15.6 8.1 %collective-permute-done.3.refs_4_ = bf16[8,128,128]{2,1,0:T(8,128)(2,1)S(1)} collective-permute-done((bf16[8,128,128]{2,1,0:T(8,128)(2,1)S(1)}, bf16[8,128,128]{2,1,0:T(8,128)(2,1)S(1)}, u32[]{:S(2)}, u32[]{:S(2)}) %collective-permute-start.3) | collective-permute-done | bytes 262176 | tf_op jit(solution)/shard_map/ppermute | solution.py:16
  23.7 0.0 collective-permute-done.2.refs_3_
  23.7 0.6 collective-permute-done.1.refs_2_
  24.3 11.8 %shard_map.111 = (f32[32,128,128]{2,1,0:T(8,128)S(1)}, bf16[32,128,128]{2,1,0:T(8,128)(2,1)S(1)}) custom-call(s32[1]{0:T(128)} %bitcast.1.live_ref, s32[704]{0:T(1024)S(1)} %get-tuple-element.11.source_ref, s32[704]{0:T(1024)S(1)} %get-tuple-element.23.target_ref, bf16[704,128,128]{2,1,0:T(8,128)(2,1)} %bitcast.22, ...), custom_call_target="tpu_custom_call" | custom-call | tf_op jit(solution)/shard_map/pallas_call | solution.py:72
  36.2 0.1 collective-permute-start.4
  36.3 2.6 %collective-permute-done.4 = bf16[32,128,128]{2,1,0:T(8,128)(2,1)S(1)} collective-permute-done((bf16[32,128,128]{2,1,0:T(8,128)(2,1)S(1)}, bf16[32,128,128]{2,1,0:T(8,128)(2,1)S(1)}, u32[]{:S(2)}, u32[]{:S(2)}) %collective-permute-start.4) | collective-permute-done | bytes 1048608 | tf_op jit(solution)/shard_map/ppermute | solution.py:16
  38.9 0.3 add_convert_fusion
  39.2 0.0 copy-start.1
  39.2 0.0 copy-start.2
  39.3 0.1 fusion.39
  39.3 0.1 collective-permute-start.5
  39.4 2.9 %collective-permute-start.7 = (bf16[8,128,128]{2,1,0:T(8,128)(2,1)S(1)}, bf16[8,128,128]{2,1,0:T(8,128)(2,1)S(1)}, u32[]{:S(2)}, u32[]{:S(2)}) collective-permute-start(bf16[8,128,128]{2,1,0:T(8,128)(2,1)S(1)} %get-tuple-element.18), channel_id=1, source_target_pairs={{0,12},{1,13},{2,14},{3,15},{4,8},{5,9},{6,10},{7,11},{8,4},{9,5},... | collective-permute-start | bytes 786440 | tf_op jit(solution)/shard_map/ppermute | solution.py:16
  42.3 1.2 collective-permute-start.6
  43.5 5.1 %collective-permute-done.5 = bf16[8,128,128]{2,1,0:T(8,128)(2,1)S(1)} collective-permute-done((bf16[8,128,128]{2,1,0:T(8,128)(2,1)S(1)}, bf16[8,128,128]{2,1,0:T(8,128)(2,1)S(1)}, u32[]{:S(2)}, u32[]{:S(2)}) %collective-permute-start.5) | collective-permute-done | bytes 262176 | tf_op jit(solution)/shard_map/ppermute | solution.py:16
  48.5 6.1 %collective-permute-done.7 = bf16[8,128,128]{2,1,0:T(8,128)(2,1)S(1)} collective-permute-done((bf16[8,128,128]{2,1,0:T(8,128)(2,1)S(1)}, bf16[8,128,128]{2,1,0:T(8,128)(2,1)S(1)}, u32[]{:S(2)}, u32[]{:S(2)}) %collective-permute-start.7) | collective-permute-done | bytes 262176 | tf_op jit(solution)/shard_map/ppermute | solution.py:16
  54.7 0.1 convert_add_fusion.1
  54.8 1.4 %collective-permute-start.8 = (bf16[4,128,128]{2,1,0:T(8,128)(2,1)S(1)}, bf16[4,128,128]{2,1,0:T(8,128)(2,1)S(1)}, u32[]{:S(2)}, u32[]{:S(2)}) collective-permute-start(bf16[4,128,128]{2,1,0:T(8,128)(2,1)S(1)} %slice.103), channel_id=1, source_target_pairs={{0,2},{1,3},{2,0},{3,1},{4,6},{5,7},{6,4},{7,5},{8,10},{9,11},{10,... | collective-permute-start | bytes 393224 | tf_op jit(solution)/shard_map/ppermute | solution.py:16
  56.2 3.6 %collective-permute-done.8 = bf16[4,128,128]{2,1,0:T(8,128)(2,1)S(1)} collective-permute-done((bf16[4,128,128]{2,1,0:T(8,128)(2,1)S(1)}, bf16[4,128,128]{2,1,0:T(8,128)(2,1)S(1)}, u32[]{:S(2)}, u32[]{:S(2)}) %collective-permute-start.8) | collective-permute-done | bytes 131104 | tf_op jit(solution)/shard_map/ppermute | solution.py:16
  60.0 1.3 %convert_reduce_fusion = (f32[256]{0:T(256)S(1)}, bf16[512,256]{1,0:T(8,128)(2,1)S(1)}, bf16[512,256]{1,0:T(8,128)(2,1)}) fusion(bf16[512,256]{1,0:T(8,128)(2,1)S(1)} %copy-done.1, f32[256]{0:T(256)S(1)} %copy-done.2, bf16[512,128]{1,0:T(8,128)(2,1)S(1)} %bitcast.25, bf16[128,256]{1,0:T(8,128)(2,1)S(1)} %copy-done), kind=kOutput, calls=%fused_computation.18 | convolution fusion | flops 36962048 | bytes 985088 | tf_op jit(solution)/shard_map/dot_general | solution.py:131
  61.2 0.2 fusion.40
  61.5 0.2 fusion
  61.7 1.4 %collective-permute-start.9 = (bf16[4,128,128]{2,1,0:T(8,128)(2,1)S(1)}, bf16[4,128,128]{2,1,0:T(8,128)(2,1)S(1)}, u32[]{:S(2)}, u32[]{:S(2)}) collective-permute-start(bf16[4,128,128]{2,1,0:T(8,128)(2,1)S(1)} %fusion), channel_id=1, source_target_pairs={{0,2},{1,3},{2,0},{3,1},{4,6},{5,7},{6,4},{7,5},{8,10},{9,11},{10,... | collective-permute-start | bytes 393224 | tf_op jit(solution)/shard_map/ppermute | solution.py:16
  63.1 0.1 collective-permute-start.21
  63.2 3.5 %collective-permute-done.9 = bf16[4,128,128]{2,1,0:T(8,128)(2,1)S(1)} collective-permute-done((bf16[4,128,128]{2,1,0:T(8,128)(2,1)S(1)}, bf16[4,128,128]{2,1,0:T(8,128)(2,1)S(1)}, u32[]{:S(2)}, u32[]{:S(2)}) %collective-permute-start.9) | collective-permute-done | bytes 131104 | tf_op jit(solution)/shard_map/ppermute | solution.py:16
  66.8 2.6 %collective-permute-start.12 = (bf16[8,128,128]{2,1,0:T(8,128)(2,1)S(1)}, bf16[8,128,128]{2,1,0:T(8,128)(2,1)S(1)}, u32[]{:S(2)}, u32[]{:S(2)}) collective-permute-start(bf16[8,128,128]{2,1,0:T(8,128)(2,1)S(1)} %pad_maximum_fusion.1.refs_1_), channel_id=1, source_target_pairs={{0,12},{1,13},{2,14},{3,15},{4,8},{5,9},{6,10},{7,11},{8,4},{9,5},... | collective-permute-start | bytes 786440 | tf_op jit(solution)/shard_map/ppermute | solution.py:16
  69.4 0.0 collective-permute-start.11
  69.4 1.5 %collective-permute-start.10 = (bf16[8,128,128]{2,1,0:T(8,128)(2,1)S(1)}, bf16[8,128,128]{2,1,0:T(8,128)(2,1)S(1)}, u32[]{:S(2)}, u32[]{:S(2)}) collective-permute-start(bf16[8,128,128]{2,1,0:T(8,128)(2,1)S(1)} %pad_maximum_fusion.1.refs_1_), channel_id=1, source_target_pairs={{0,4},{1,5},{2,6},{3,7},{4,0},{5,1},{6,2},{7,3},{8,12},{9,13},{10,... | collective-permute-start | bytes 786440 | tf_op jit(solution)/shard_map/ppermute | solution.py:16
  71.0 0.0 collective-permute-done.21
  71.0 1.4 %collective-permute-start.22 = (f32[72,256]{1,0:T(8,128)S(1)}, f32[72,256]{1,0:T(8,128)S(1)}, u32[]{:S(2)}, u32[]{:S(2)}) collective-permute-start(f32[72,256]{1,0:T(8,128)S(1)} %select_add_fusion), channel_id=1, source_target_pairs={{0,2},{1,3},{2,0},{3,1},{4,6},{5,7},{6,4},{7,5},{8,10},{9,11},{10,... | collective-permute-start | bytes 221192 | tf_op jit(solution)/shard_map/ppermute | solution.py:16
  72.4 3.0 %collective-permute-done.22 = f32[72,256]{1,0:T(8,128)S(1)} collective-permute-done((f32[72,256]{1,0:T(8,128)S(1)}, f32[72,256]{1,0:T(8,128)S(1)}, u32[]{:S(2)}, u32[]{:S(2)}) %collective-permute-start.22) | collective-permute-done | bytes 73760 | tf_op jit(solution)/shard_map/ppermute | solution.py:16
  75.4 2.6 %collective-permute-start.25 = (f32[72,256]{1,0:T(8,128)S(1)}, f32[72,256]{1,0:T(8,128)S(1)}, u32[]{:S(2)}, u32[]{:S(2)}) collective-permute-start(f32[72,256]{1,0:T(8,128)S(1)} %add.128), channel_id=1, source_target_pairs={{0,12},{1,13},{2,14},{3,15},{4,8},{5,9},{6,10},{7,11},{8,4},{9,5},... | collective-permute-start | bytes 221192 | tf_op jit(solution)/shard_map/ppermute | solution.py:16
  78.1 3.2 %collective-permute-done.25 = f32[72,256]{1,0:T(8,128)S(1)} collective-permute-done((f32[72,256]{1,0:T(8,128)S(1)}, f32[72,256]{1,0:T(8,128)S(1)}, u32[]{:S(2)}, u32[]{:S(2)}) %collective-permute-start.25) | collective-permute-done | bytes 73760 | tf_op jit(solution)/shard_map/ppermute | solution.py:16
  81.3 3.2 %collective-permute-done.24 = f32[72,256]{1,0:T(8,128)S(1)} collective-permute-done((f32[72,256]{1,0:T(8,128)S(1)}, f32[72,256]{1,0:T(8,128)S(1)}, u32[]{:S(2)}, u32[]{:S(2)}) %collective-permute-start.24) | collective-permute-done | bytes 73760 | tf_op jit(solution)/shard_map/ppermute | solution.py:16
  84.5 0.5 collective-permute-start.16
  85.0 0.1 collective-permute-start.15
  85.1 0.4 collective-permute-start.14
  85.5 0.1 collective-permute-done.23
  85.6 3.7 %collective-permute-start.26 = (f32[72,256]{1,0:T(8,128)S(1)}, f32[72,256]{1,0:T(8,128)S(1)}, u32[]{:S(2)}, u32[]{:S(2)}) collective-permute-start(f32[72,256]{1,0:T(8,128)S(1)} %add_add_fusion.1), channel_id=1, source_target_pairs={{0,16},{16,0},{32,48},{48,32},{64,80},{80,64},{96,112},{112,96},{1... | collective-permute-start | bytes 221192 | tf_op jit(solution)/shard_map/ppermute | solution.py:16
  89.3 2.3 %collective-permute-done.26 = f32[72,256]{1,0:T(8,128)S(1)} collective-permute-done((f32[72,256]{1,0:T(8,128)S(1)}, f32[72,256]{1,0:T(8,128)S(1)}, u32[]{:S(2)}, u32[]{:S(2)}) %collective-permute-start.26) | collective-permute-done | bytes 73760 | tf_op jit(solution)/shard_map/ppermute | solution.py:16
  91.6 4.0 %collective-permute-start.29 = (f32[72,256]{1,0:T(8,128)S(1)}, f32[72,256]{1,0:T(8,128)S(1)}, u32[]{:S(2)}, u32[]{:S(2)}) collective-permute-start(f32[72,256]{1,0:T(8,128)S(1)} %add.132), channel_id=1, source_target_pairs={{0,96},{16,112},{32,64},{48,80},{64,32},{80,48},{96,0},{112,16},{1... | collective-permute-start | bytes 221192 | tf_op jit(solution)/shard_map/ppermute | solution.py:16
  95.6 1.3 %collective-permute-start.28 = (f32[72,256]{1,0:T(8,128)S(1)}, f32[72,256]{1,0:T(8,128)S(1)}, u32[]{:S(2)}, u32[]{:S(2)}) collective-permute-start(f32[72,256]{1,0:T(8,128)S(1)} %add.132), channel_id=1, source_target_pairs={{0,64},{16,80},{32,96},{48,112},{64,0},{80,16},{96,32},{112,48},{1... | collective-permute-start | bytes 221192 | tf_op jit(solution)/shard_map/ppermute | solution.py:16
  96.9 11.5 %shard_map.112 = bf16[32,128,128]{2,1,0:T(8,128)(2,1)S(1)} custom-call(s32[1]{0:T(128)} %bitcast.1.live_ref, s32[704]{0:T(1024)S(1)} %get-tuple-element.24.source_ref, s32[704]{0:T(1024)S(1)} %get-tuple-element.10.target_ref, bf16[704,128,128]{2,1,0:T(8,128)(2,1)} %bitcast.23, bf16[8,128,128]{2,1,0:T(8,128)(2,1)S(1)} %pad_maximum_fusion.1.refs_1_, ...), custom_call_target="tpu_custom_call" | custom-call | tf_op jit(solution)/shard_map/pallas_call | solution.py:72
  108.4 0.1 fusion.38
  108.5 0.1 collective-permute-start.17
  108.6 0.6 collective-permute-start.19
  109.2 3.5 %collective-permute-start.18 = (bf16[8,128,128]{2,1,0:T(8,128)(2,1)S(1)}, bf16[8,128,128]{2,1,0:T(8,128)(2,1)S(1)}, u32[]{:S(2)}, u32[]{:S(2)}) collective-permute-start(bf16[8,128,128]{2,1,0:T(8,128)(2,1)S(1)} %get-tuple-element.16), channel_id=1, source_target_pairs={{0,64},{16,80},{32,96},{48,112},{64,0},{80,16},{96,32},{112,48},{1... | collective-permute-start | bytes 786440 | tf_op jit(solution)/shard_map/ppermute | solution.py:16
  112.7 0.1 collective-permute-start.30
  112.8 3.8 %collective-permute-done.17 = bf16[8,128,128]{2,1,0:T(8,128)(2,1)S(1)} collective-permute-done((bf16[8,128,128]{2,1,0:T(8,128)(2,1)S(1)}, bf16[8,128,128]{2,1,0:T(8,128)(2,1)S(1)}, u32[]{:S(2)}, u32[]{:S(2)}) %collective-permute-start.17) | collective-permute-done | bytes 262176 | tf_op jit(solution)/shard_map/ppermute | solution.py:16
  116.6 4.6 %collective-permute-done.19 = bf16[8,128,128]{2,1,0:T(8,128)(2,1)S(1)} collective-permute-done((bf16[8,128,128]{2,1,0:T(8,128)(2,1)S(1)}, bf16[8,128,128]{2,1,0:T(8,128)(2,1)S(1)}, u32[]{:S(2)}, u32[]{:S(2)}) %collective-permute-start.19) | collective-permute-done | bytes 262176 | tf_op jit(solution)/shard_map/ppermute | solution.py:16
  121.2 0.1 convert_add_fusion
  121.4 2.6 %collective-permute-start.20 = (bf16[4,128,128]{2,1,0:T(8,128)(2,1)S(1)}, bf16[4,128,128]{2,1,0:T(8,128)(2,1)S(1)}, u32[]{:S(2)}, u32[]{:S(2)}) collective-permute-start(bf16[4,128,128]{2,1,0:T(8,128)(2,1)S(1)} %slice.102), channel_id=1, source_target_pairs={{0,16},{16,0},{32,48},{48,32},{64,80},{80,64},{96,112},{112,96},{1... | collective-permute-start | bytes 393224 | tf_op jit(solution)/shard_map/ppermute | solution.py:16
  124.0 0.6 slice.87
  124.6 0.7 pad_maximum_fusion.2
  125.2 2.7 %collective-permute-done.20 = bf16[4,128,128]{2,1,0:T(8,128)(2,1)S(1)} collective-permute-done((bf16[4,128,128]{2,1,0:T(8,128)(2,1)S(1)}, bf16[4,128,128]{2,1,0:T(8,128)(2,1)S(1)}, u32[]{:S(2)}, u32[]{:S(2)}) %collective-permute-start.20) | collective-permute-done | bytes 131104 | tf_op jit(solution)/shard_map/ppermute | solution.py:16
  128.0 0.8 copy.14
  (34 shorter events, 0.3 us)
Async XLA Ops:
  0.6 59.3 %copy-start = (bf16[128,256]{1,0:T(8,128)(2,1)S(1)}, bf16[128,256]{1,0:T(8,128)(2,1)}, u32[]{:S(2)}) copy-start(bf16[128,256]{1,0:T(8,128)(2,1)} %param.9) | copy-start | bytes 196612
  0.6 7.7 %collective-permute-start = (bf16[4,128,128]{2,1,0:T(8,128)(2,1)}, bf16[4,128,128]{2,1,0:T(8,128)(2,1)S(1)}, u32[]{:S(2)}, u32[]{:S(2)}) collective-permute-start(bf16[4,128,128]{2,1,0:T(8,128)(2,1)} %bitcast.28), channel_id=1, source_target_pairs={{0,16},{16,0},{32,48},{48,32},{64,80},{80,64},{96,112},{112,96},{1... | collective-permute-start | bytes 393224 | tf_op jit(solution)/shard_map/ppermute | solution.py:16
  9.3 14.4 %collective-permute-start.3 = (bf16[8,128,128]{2,1,0:T(8,128)(2,1)S(1)}, bf16[8,128,128]{2,1,0:T(8,128)(2,1)S(1)}, u32[]{:S(2)}, u32[]{:S(2)}) collective-permute-start(bf16[8,128,128]{2,1,0:T(8,128)(2,1)S(1)} %pad_maximum_fusion.refs_1_), channel_id=1, source_target_pairs={{0,96},{16,112},{32,64},{48,80},{64,32},{80,48},{96,0},{112,16},{1... | collective-permute-start | bytes 786440 | tf_op jit(solution)/shard_map/ppermute | solution.py:16
  12.2 11.6 %collective-permute-start.2 = (bf16[8,128,128]{2,1,0:T(8,128)(2,1)S(1)}, bf16[8,128,128]{2,1,0:T(8,128)(2,1)S(1)}, u32[]{:S(2)}, u32[]{:S(2)}) collective-permute-start(bf16[8,128,128]{2,1,0:T(8,128)(2,1)S(1)} %pad_maximum_fusion.refs_1_), channel_id=1, source_target_pairs={{0,64},{16,80},{32,96},{48,112},{64,0},{80,16},{96,32},{112,48},{1... | collective-permute-start | bytes 786440 | tf_op jit(solution)/shard_map/ppermute | solution.py:16
  13.0 11.4 %collective-permute-start.1 = (bf16[8,128,128]{2,1,0:T(8,128)(2,1)S(1)}, bf16[8,128,128]{2,1,0:T(8,128)(2,1)S(1)}, u32[]{:S(2)}, u32[]{:S(2)}) collective-permute-start(bf16[8,128,128]{2,1,0:T(8,128)(2,1)S(1)} %pad_maximum_fusion.refs_1_), channel_id=1, source_target_pairs={{0,32},{16,48},{32,0},{48,16},{64,96},{80,112},{96,64},{112,80},{1... | collective-permute-start | bytes 786440 | tf_op jit(solution)/shard_map/ppermute | solution.py:16
  36.2 2.7 %collective-permute-start.4 = (bf16[32,128,128]{2,1,0:T(8,128)(2,1)S(1)}, bf16[32,128,128]{2,1,0:T(8,128)(2,1)S(1)}, u32[]{:S(2)}, u32[]{:S(2)}) collective-permute-start(bf16[32,128,128]{2,1,0:T(8,128)(2,1)S(1)} %get-tuple-element.7), channel_id=1, source_target_pairs={{0,1},{1,0},{2,3},{3,2},{4,5},{5,4},{6,7},{7,6},{8,9},{9,8},{10,11... | collective-permute-start | bytes 3145736 | tf_op jit(solution)/shard_map/ppermute | solution.py:16
  39.2 20.7 %copy-start.1 = (bf16[512,256]{1,0:T(8,128)(2,1)S(1)}, bf16[512,256]{1,0:T(8,128)(2,1)}, u32[]{:S(2)}) copy-start(bf16[512,256]{1,0:T(8,128)(2,1)} %param.15) | copy-start | bytes 786436
  39.2 20.7 %copy-start.2 = (f32[256]{0:T(256)S(1)}, f32[256]{0:T(256)}, u32[]{:S(2)}) copy-start(f32[256]{0:T(256)} %param.10) | copy-start | bytes 3076
  39.3 9.2 %collective-permute-start.5 = (bf16[8,128,128]{2,1,0:T(8,128)(2,1)S(1)}, bf16[8,128,128]{2,1,0:T(8,128)(2,1)S(1)}, u32[]{:S(2)}, u32[]{:S(2)}) collective-permute-start(bf16[8,128,128]{2,1,0:T(8,128)(2,1)S(1)} %get-tuple-element.17), channel_id=1, source_target_pairs={{0,4},{1,5},{2,6},{3,7},{4,0},{5,1},{6,2},{7,3},{8,12},{9,13},{10,... | collective-permute-start | bytes 786440 | tf_op jit(solution)/shard_map/ppermute | solution.py:16
  39.4 15.3 %collective-permute-start.7 = (bf16[8,128,128]{2,1,0:T(8,128)(2,1)S(1)}, bf16[8,128,128]{2,1,0:T(8,128)(2,1)S(1)}, u32[]{:S(2)}, u32[]{:S(2)}) collective-permute-start(bf16[8,128,128]{2,1,0:T(8,128)(2,1)S(1)} %get-tuple-element.18), channel_id=1, source_target_pairs={{0,12},{1,13},{2,14},{3,15},{4,8},{5,9},{6,10},{7,11},{8,4},{9,5},... | collective-permute-start | bytes 786440 | tf_op jit(solution)/shard_map/ppermute | solution.py:16
  42.3 12.3 %collective-permute-start.6 = (bf16[8,128,128]{2,1,0:T(8,128)(2,1)S(1)}, bf16[8,128,128]{2,1,0:T(8,128)(2,1)S(1)}, u32[]{:S(2)}, u32[]{:S(2)}) collective-permute-start(bf16[8,128,128]{2,1,0:T(8,128)(2,1)S(1)} %get-tuple-element.19), channel_id=1, source_target_pairs={{0,8},{1,9},{2,10},{3,11},{4,12},{5,13},{6,14},{7,15},{8,0},{9,1},... | collective-permute-start | bytes 786440 | tf_op jit(solution)/shard_map/ppermute | solution.py:16
  54.8 5.0 %collective-permute-start.8 = (bf16[4,128,128]{2,1,0:T(8,128)(2,1)S(1)}, bf16[4,128,128]{2,1,0:T(8,128)(2,1)S(1)}, u32[]{:S(2)}, u32[]{:S(2)}) collective-permute-start(bf16[4,128,128]{2,1,0:T(8,128)(2,1)S(1)} %slice.103), channel_id=1, source_target_pairs={{0,2},{1,3},{2,0},{3,1},{4,6},{5,7},{6,4},{7,5},{8,10},{9,11},{10,... | collective-permute-start | bytes 393224 | tf_op jit(solution)/shard_map/ppermute | solution.py:16
  61.7 5.0 %collective-permute-start.9 = (bf16[4,128,128]{2,1,0:T(8,128)(2,1)S(1)}, bf16[4,128,128]{2,1,0:T(8,128)(2,1)S(1)}, u32[]{:S(2)}, u32[]{:S(2)}) collective-permute-start(bf16[4,128,128]{2,1,0:T(8,128)(2,1)S(1)} %fusion), channel_id=1, source_target_pairs={{0,2},{1,3},{2,0},{3,1},{4,6},{5,7},{6,4},{7,5},{8,10},{9,11},{10,... | collective-permute-start | bytes 393224 | tf_op jit(solution)/shard_map/ppermute | solution.py:16
  63.1 7.8 %collective-permute-start.21 = (f32[72,256]{1,0:T(8,128)S(1)}, f32[72,256]{1,0:T(8,128)S(1)}, u32[]{:S(2)}, u32[]{:S(2)}) collective-permute-start(f32[72,256]{1,0:T(8,128)S(1)} %slice_select_fusion), channel_id=1, source_target_pairs={{0,1},{1,0},{2,3},{3,2},{4,5},{5,4},{6,7},{7,6},{8,9},{9,8},{10,11... | collective-permute-start | bytes 221192 | tf_op jit(solution)/shard_map/ppermute | solution.py:16
  66.8 17.7 %collective-permute-start.12 = (bf16[8,128,128]{2,1,0:T(8,128)(2,1)S(1)}, bf16[8,128,128]{2,1,0:T(8,128)(2,1)S(1)}, u32[]{:S(2)}, u32[]{:S(2)}) collective-permute-start(bf16[8,128,128]{2,1,0:T(8,128)(2,1)S(1)} %pad_maximum_fusion.1.refs_1_), channel_id=1, source_target_pairs={{0,12},{1,13},{2,14},{3,15},{4,8},{5,9},{6,10},{7,11},{8,4},{9,5},... | collective-permute-start | bytes 786440 | tf_op jit(solution)/shard_map/ppermute | solution.py:16
  69.4 15.6 %collective-permute-start.11 = (bf16[8,128,128]{2,1,0:T(8,128)(2,1)S(1)}, bf16[8,128,128]{2,1,0:T(8,128)(2,1)S(1)}, u32[]{:S(2)}, u32[]{:S(2)}) collective-permute-start(bf16[8,128,128]{2,1,0:T(8,128)(2,1)S(1)} %pad_maximum_fusion.1.refs_1_), channel_id=1, source_target_pairs={{0,8},{1,9},{2,10},{3,11},{4,12},{5,13},{6,14},{7,15},{8,0},{9,1},... | collective-permute-start | bytes 786440 | tf_op jit(solution)/shard_map/ppermute | solution.py:16
  69.4 15.7 %collective-permute-start.10 = (bf16[8,128,128]{2,1,0:T(8,128)(2,1)S(1)}, bf16[8,128,128]{2,1,0:T(8,128)(2,1)S(1)}, u32[]{:S(2)}, u32[]{:S(2)}) collective-permute-start(bf16[8,128,128]{2,1,0:T(8,128)(2,1)S(1)} %pad_maximum_fusion.1.refs_1_), channel_id=1, source_target_pairs={{0,4},{1,5},{2,6},{3,7},{4,0},{5,1},{6,2},{7,3},{8,12},{9,13},{10,... | collective-permute-start | bytes 786440 | tf_op jit(solution)/shard_map/ppermute | solution.py:16
  71.0 4.4 %collective-permute-start.22 = (f32[72,256]{1,0:T(8,128)S(1)}, f32[72,256]{1,0:T(8,128)S(1)}, u32[]{:S(2)}, u32[]{:S(2)}) collective-permute-start(f32[72,256]{1,0:T(8,128)S(1)} %select_add_fusion), channel_id=1, source_target_pairs={{0,2},{1,3},{2,0},{3,1},{4,6},{5,7},{6,4},{7,5},{8,10},{9,11},{10,... | collective-permute-start | bytes 221192 | tf_op jit(solution)/shard_map/ppermute | solution.py:16
  75.4 5.8 %collective-permute-start.25 = (f32[72,256]{1,0:T(8,128)S(1)}, f32[72,256]{1,0:T(8,128)S(1)}, u32[]{:S(2)}, u32[]{:S(2)}) collective-permute-start(f32[72,256]{1,0:T(8,128)S(1)} %add.128), channel_id=1, source_target_pairs={{0,12},{1,13},{2,14},{3,15},{4,8},{5,9},{6,10},{7,11},{8,4},{9,5},... | collective-permute-start | bytes 221192 | tf_op jit(solution)/shard_map/ppermute | solution.py:16
  78.1 6.4 %collective-permute-start.24 = (f32[72,256]{1,0:T(8,128)S(1)}, f32[72,256]{1,0:T(8,128)S(1)}, u32[]{:S(2)}, u32[]{:S(2)}) collective-permute-start(f32[72,256]{1,0:T(8,128)S(1)} %add.128), channel_id=1, source_target_pairs={{0,8},{1,9},{2,10},{3,11},{4,12},{5,13},{6,14},{7,15},{8,0},{9,1},... | collective-permute-start | bytes 221192 | tf_op jit(solution)/shard_map/ppermute | solution.py:16
  81.3 4.4 %collective-permute-start.23 = (f32[72,256]{1,0:T(8,128)S(1)}, f32[72,256]{1,0:T(8,128)S(1)}, u32[]{:S(2)}, u32[]{:S(2)}) collective-permute-start(f32[72,256]{1,0:T(8,128)S(1)} %add.128), channel_id=1, source_target_pairs={{0,4},{1,5},{2,6},{3,7},{4,0},{5,1},{6,2},{7,3},{8,12},{9,13},{10,... | collective-permute-start | bytes 221192 | tf_op jit(solution)/shard_map/ppermute | solution.py:16
  84.5 11.1 %collective-permute-start.13 = (bf16[8,128,128]{2,1,0:T(8,128)(2,1)S(1)}, bf16[8,128,128]{2,1,0:T(8,128)(2,1)S(1)}, u32[]{:S(2)}, u32[]{:S(2)}) collective-permute-start(bf16[8,128,128]{2,1,0:T(8,128)(2,1)S(1)} %pad_maximum_fusion.1.refs_1_), channel_id=1, source_target_pairs={{0,1},{1,0},{2,3},{3,2},{4,5},{5,4},{6,7},{7,6},{8,9},{9,8},{10,11... | collective-permute-start | bytes 786440 | tf_op jit(solution)/shard_map/ppermute | solution.py:16
  84.5 12.4 %collective-permute-start.16 = (bf16[8,128,128]{2,1,0:T(8,128)(2,1)S(1)}, bf16[8,128,128]{2,1,0:T(8,128)(2,1)S(1)}, u32[]{:S(2)}, u32[]{:S(2)}) collective-permute-start(bf16[8,128,128]{2,1,0:T(8,128)(2,1)S(1)} %collective-permute-done.12.refs_4_), channel_id=1, source_target_pairs={{0,1},{1,0},{2,3},{3,2},{4,5},{5,4},{6,7},{7,6},{8,9},{9,8},{10,11... | collective-permute-start | bytes 786440 | tf_op jit(solution)/shard_map/ppermute | solution.py:16
  85.0 11.9 %collective-permute-start.15 = (bf16[8,128,128]{2,1,0:T(8,128)(2,1)S(1)}, bf16[8,128,128]{2,1,0:T(8,128)(2,1)S(1)}, u32[]{:S(2)}, u32[]{:S(2)}) collective-permute-start(bf16[8,128,128]{2,1,0:T(8,128)(2,1)S(1)} %collective-permute-done.11.refs_3_), channel_id=1, source_target_pairs={{0,1},{1,0},{2,3},{3,2},{4,5},{5,4},{6,7},{7,6},{8,9},{9,8},{10,11... | collective-permute-start | bytes 786440 | tf_op jit(solution)/shard_map/ppermute | solution.py:16
  85.1 11.8 %collective-permute-start.14 = (bf16[8,128,128]{2,1,0:T(8,128)(2,1)S(1)}, bf16[8,128,128]{2,1,0:T(8,128)(2,1)S(1)}, u32[]{:S(2)}, u32[]{:S(2)}) collective-permute-start(bf16[8,128,128]{2,1,0:T(8,128)(2,1)S(1)} %collective-permute-done.10.refs_2_), channel_id=1, source_target_pairs={{0,1},{1,0},{2,3},{3,2},{4,5},{5,4},{6,7},{7,6},{8,9},{9,8},{10,11... | collective-permute-start | bytes 786440 | tf_op jit(solution)/shard_map/ppermute | solution.py:16
  85.6 6.0 %collective-permute-start.26 = (f32[72,256]{1,0:T(8,128)S(1)}, f32[72,256]{1,0:T(8,128)S(1)}, u32[]{:S(2)}, u32[]{:S(2)}) collective-permute-start(f32[72,256]{1,0:T(8,128)S(1)} %add_add_fusion.1), channel_id=1, source_target_pairs={{0,16},{16,0},{32,48},{48,32},{64,80},{80,64},{96,112},{112,96},{1... | collective-permute-start | bytes 221192 | tf_op jit(solution)/shard_map/ppermute | solution.py:16
  91.6 17.6 %collective-permute-start.29 = (f32[72,256]{1,0:T(8,128)S(1)}, f32[72,256]{1,0:T(8,128)S(1)}, u32[]{:S(2)}, u32[]{:S(2)}) collective-permute-start(f32[72,256]{1,0:T(8,128)S(1)} %add.132), channel_id=1, source_target_pairs={{0,96},{16,112},{32,64},{48,80},{64,32},{80,48},{96,0},{112,16},{1... | collective-permute-start | bytes 221192 | tf_op jit(solution)/shard_map/ppermute | solution.py:16
  95.6 17.1 %collective-permute-start.28 = (f32[72,256]{1,0:T(8,128)S(1)}, f32[72,256]{1,0:T(8,128)S(1)}, u32[]{:S(2)}, u32[]{:S(2)}) collective-permute-start(f32[72,256]{1,0:T(8,128)S(1)} %add.132), channel_id=1, source_target_pairs={{0,64},{16,80},{32,96},{48,112},{64,0},{80,16},{96,32},{112,48},{1... | collective-permute-start | bytes 221192 | tf_op jit(solution)/shard_map/ppermute | solution.py:16
  96.9 15.8 %collective-permute-start.27 = (f32[72,256]{1,0:T(8,128)S(1)}, f32[72,256]{1,0:T(8,128)S(1)}, u32[]{:S(2)}, u32[]{:S(2)}) collective-permute-start(f32[72,256]{1,0:T(8,128)S(1)} %add.132), channel_id=1, source_target_pairs={{0,32},{16,48},{32,0},{48,16},{64,96},{80,112},{96,64},{112,80},{1... | collective-permute-start | bytes 221192 | tf_op jit(solution)/shard_map/ppermute | solution.py:16
  108.5 8.1 %collective-permute-start.17 = (bf16[8,128,128]{2,1,0:T(8,128)(2,1)S(1)}, bf16[8,128,128]{2,1,0:T(8,128)(2,1)S(1)}, u32[]{:S(2)}, u32[]{:S(2)}) collective-permute-start(bf16[8,128,128]{2,1,0:T(8,128)(2,1)S(1)} %get-tuple-element.14), channel_id=1, source_target_pairs={{0,32},{16,48},{32,0},{48,16},{64,96},{80,112},{96,64},{112,80},{1... | collective-permute-start | bytes 786440 | tf_op jit(solution)/shard_map/ppermute | solution.py:16
  108.6 12.6 %collective-permute-start.19 = (bf16[8,128,128]{2,1,0:T(8,128)(2,1)S(1)}, bf16[8,128,128]{2,1,0:T(8,128)(2,1)S(1)}, u32[]{:S(2)}, u32[]{:S(2)}) collective-permute-start(bf16[8,128,128]{2,1,0:T(8,128)(2,1)S(1)} %get-tuple-element.15), channel_id=1, source_target_pairs={{0,96},{16,112},{32,64},{48,80},{64,32},{80,48},{96,0},{112,16},{1... | collective-permute-start | bytes 786440 | tf_op jit(solution)/shard_map/ppermute | solution.py:16
  109.2 12.0 %collective-permute-start.18 = (bf16[8,128,128]{2,1,0:T(8,128)(2,1)S(1)}, bf16[8,128,128]{2,1,0:T(8,128)(2,1)S(1)}, u32[]{:S(2)}, u32[]{:S(2)}) collective-permute-start(bf16[8,128,128]{2,1,0:T(8,128)(2,1)S(1)} %get-tuple-element.16), channel_id=1, source_target_pairs={{0,64},{16,80},{32,96},{48,112},{64,0},{80,16},{96,32},{112,48},{1... | collective-permute-start | bytes 786440 | tf_op jit(solution)/shard_map/ppermute | solution.py:16
  112.7 11.2 %collective-permute-start.30 = (f32[72,256]{1,0:T(8,128)S(1)}, f32[72,256]{1,0:T(8,128)S(1)}, u32[]{:S(2)}, u32[]{:S(2)}) collective-permute-start(f32[72,256]{1,0:T(8,128)S(1)} %add_add_fusion), channel_id=1, source_target_pairs={{0,1},{1,0},{2,3},{3,2},{4,5},{5,4},{6,7},{7,6},{8,9},{9,8},{10,11... | collective-permute-start | bytes 221192 | tf_op jit(solution)/shard_map/ppermute | solution.py:16
  121.4 6.6 %collective-permute-start.20 = (bf16[4,128,128]{2,1,0:T(8,128)(2,1)S(1)}, bf16[4,128,128]{2,1,0:T(8,128)(2,1)S(1)}, u32[]{:S(2)}, u32[]{:S(2)}) collective-permute-start(bf16[4,128,128]{2,1,0:T(8,128)(2,1)S(1)} %slice.102), channel_id=1, source_target_pairs={{0,16},{16,0},{32,48},{48,32},{64,80},{80,64},{96,112},{112,96},{1... | collective-permute-start | bytes 393224 | tf_op jit(solution)/shard_map/ppermute | solution.py:16

commit v2 on v1

v2 whole, which is shorter than its diff:
```python
import functools

import jax
import jax.numpy as jnp
from jax import lax
from jax.experimental import pallas as pl
from jax.experimental.pallas import tpu as pltpu
from jax.sharding import PartitionSpec as P

HALF = jnp.bfloat16
FULL = jnp.float32


def swap(array, axis, distance):
    size = lax.axis_size(axis)
    return lax.ppermute(array, axis, [(j, j ^ distance) for j in range(size)])


def tile_kernel(chunk, num_pieces, flip, table_ref, *refs):
    values_hbm = refs[0]
    pieces = refs[1 : 1 + num_pieces]
    *outs, done = refs[1 + num_pieces : -4]
    source, values, total, sems = refs[-4:]
    num_chunks = values.shape[0] // chunk

    def copy(i):
        span = pl.ds(i * chunk, chunk)
        return pltpu.make_async_copy(values_hbm.at[span], values.at[span], sems.at[i])

    live_chunks = table_ref[values.shape[0]]
    for i in range(num_chunks):

        @pl.when(i < live_chunks)
        def _():
            copy(i).start()

    first = 0
    for piece in pieces:
        tiles = piece.shape[0] // source.shape[1]
        source[pl.ds(first, tiles)] = piece[...].reshape((tiles,) + source.shape[1:])
        first += tiles
    total[...] = jnp.zeros_like(total)

    def step(i, carry):
        copy(i).wait()
        products, targets = [], []
        for u in range(chunk):
            slot = i * chunk + u
            entry = table_ref[slot]
            picked = source[entry & 255]
            pair = (picked, values[slot]) if flip else (values[slot], picked)
            products.append(jnp.dot(*pair, preferred_element_type=FULL))
            targets.append(entry >> 8)
        for target, product in zip(targets, products):
            total[target] += product
        return carry

    lax.fori_loop(0, live_chunks, step, 0)
    first = 0
    for out in outs:
        tiles = out.shape[0] // total.shape[1]
        out[...] = total[pl.ds(first, tiles)].astype(out.dtype).reshape(out.shape)
        first += tiles
    done[...] = jnp.zeros_like(done)


def tile_sums(values, pieces, source_index, target_index, count, out_types, flip, zero_shape=(8, 128)):
    slots, side, _ = values.shape
    chunk = max(d for d in range(1, 65) if slots % d == 0)
    num_source = sum(piece.shape[0] for piece in pieces) // side
    num_out = sum(n for n, _ in out_types)
    width = pieces[0].shape[1]
    target_index = jnp.where(jnp.arange(slots, dtype=jnp.int32) < count, target_index, num_out)
    table = jnp.concatenate([source_index | (target_index << 8), (count + chunk - 1) // chunk])
    smem = pl.BlockSpec(memory_space=pltpu.SMEM)
    vmem = pl.BlockSpec(memory_space=pltpu.VMEM)
    return pl.pallas_call(
        functools.partial(tile_kernel, chunk, len(pieces), flip),
        out_shape=[jax.ShapeDtypeStruct((n * side, width), kind) for n, kind in out_types]
        + [jax.ShapeDtypeStruct(zero_shape, FULL)],
        in_specs=[smem, pl.BlockSpec(memory_space=pltpu.HBM)] + [vmem] * len(pieces),
        out_specs=[vmem] * (len(out_types) + 1),
        scratch_shapes=[
            pltpu.VMEM((num_source, side, width), HALF),
            pltpu.VMEM((slots, side, side), HALF),
            pltpu.VMEM((num_out + 1, side, width), FULL),
            pltpu.SemaphoreType.DMA((slots // chunk,)),
        ],
        cost_estimate=pl.CostEstimate(
            flops=8 * slots * side * side * width, bytes_accessed=2 * slots * side * side, transcendentals=0
        ),
        compiler_params=pltpu.CompilerParams(vmem_limit_bytes=42 * 2**20),
    )(table, pltpu.with_memory_space_constraint(values, pltpu.HBM), *pieces)


def after(array, event):
    return lax.optimization_barrier((array, event))[0]


def shards(features, weight, bias, tile_values, tile_rows, tile_cols, tile_count, upstream):
    side = tile_values.shape[3]
    width = features.shape[1]
    hidden = weight.shape[1]
    nodes = features.shape[0]
    per = nodes // side
    values = tile_values.reshape(tile_values.shape[2:])
    rows = tile_rows.reshape(-1)
    cols = tile_cols.reshape(-1)
    count = tile_count.reshape(1)
    my_row = lax.axis_index("row")
    my_col = lax.axis_index("col")
    row_owner = (rows // per) ^ my_col
    row_place = (row_owner % 2) * (lax.axis_size("col") // 2 * per) + (row_owner // 2) * per + rows % per
    col_place = ((cols // per) ^ my_row) * per + cols % per

    pair = jnp.concatenate([features, swap(features, "row", 1)], axis=0)
    pieces = [pair] + [swap(pair, "row", d) for d in (2, 4, 6)]
    half_tiles = lax.axis_size("col") // 2 * per
    keep, send, _ = tile_sums(
        values, pieces, col_place, row_place, count, [(half_tiles, FULL), (half_tiles, HALF)], False
    )

    block = (keep + swap(send, "col", 1).astype(FULL)).astype(HALF).reshape(4, 2 * nodes, width)
    total = block[0].astype(FULL)
    for other in [swap(block[d], "col", 4 * d) for d in (2, 1, 3)]:
        total = total + other.astype(FULL)
    away = swap(total[nodes:].astype(HALF), "col", 2)
    s_half = (total[:nodes] + away.astype(FULL)).astype(HALF)

    pre = jnp.dot(s_half, weight, preferred_element_type=FULL) + bias
    activated = jax.nn.gelu(pre, approximate=True).astype(HALF)
    _, pullback = jax.vjp(lambda v: jax.nn.gelu(v, approximate=True), pre)
    grad_pre = pullback(upstream.astype(FULL))[0].astype(HALF)
    grad_tiles = grad_pre.reshape(per, side, hidden)
    grad_agg = jnp.einsum("fh,tbh->tfb", weight, grad_tiles, preferred_element_type=FULL).astype(HALF)
    grad_agg = grad_agg.reshape(per * width, side)

    pair = jnp.concatenate([grad_agg, swap(grad_agg, "col", 2)], axis=0)
    s_half, grad_pre = after((s_half, grad_pre), grad_agg)
    weight_term = jnp.dot(s_half.T, grad_pre, preferred_element_type=FULL)
    bias_term = jnp.sum(grad_pre.astype(FULL), axis=0)
    terms = jnp.concatenate([weight_term, jnp.broadcast_to(bias_term[None], (8, hidden))], axis=0)
    terms = terms + swap(terms, "col", 1)
    near = [pair] + [swap(pair, "col", d) for d in (4, 8, 12)]
    terms = after(terms, pair)
    terms = (terms + swap(terms, "row", 2)) + (swap(terms, "row", 4) + swap(terms, "row", 6))
    far = [swap(piece, "col", 1) for piece in near]
    terms = after(terms, near)
    other_terms = swap(terms, "row", 1)
    back, zero = tile_sums(
        values, near + far, row_place, col_place, count, [(lax.axis_size("row") * per, HALF)], True, terms.shape
    )
    back = back.reshape(4, 2 * nodes, side)
    total = back[0].astype(FULL)
    for other in [swap(back[d], "row", 2 * d) for d in (2, 1, 3)]:
        total = total + other.astype(FULL)
    terms = (terms + zero) + other_terms
    terms = terms + swap(terms, "col", 2)
    terms = (terms + swap(terms, "col", 4)) + (swap(terms, "col", 8) + swap(terms, "col", 12))
    away = swap(total[nodes:].astype(HALF), "row", 1)
    total = total[:nodes] + away.astype(FULL)
    feature_grad = jnp.swapaxes(total.reshape(per, width, side), 1, 2).astype(HALF).reshape(nodes, width)
    return (activated, feature_grad, terms[:width], terms[width])


def solution(mesh):
    in_specs = (
        P(("col", "row"), None),
        P(),
        P(),
        P("row", "col", None, None, None),
        P("row", "col", None),
        P("row", "col", None),
        P("row", "col"),
        P(("row", "col"), None),
    )
    out_specs = (P(("row", "col"), None), P(("col", "row"), None), P(), P())
    return jax.shard_map(shards, mesh=mesh, in_specs=in_specs, out_specs=out_specs, check_vma=False)
```

time: 129 us -> 119 us (0.922)
  starting transfers between devices: 40.4 us -> 33.5 us
  waiting for transfers between devices: 56.4 us -> 52.9 us
  local copies, waits for them, and re-layouts: 1.52 us -> 3.1 us
  other arithmetic: 3.8 us -> 2.35 us
    ppermute x31 -> x30, starting transfers between devices: 40.4 us -> 33.5 us  [swap(): return lax.ppermute(array, axis, [(j, j ^ distance) for j in range(size)])]
    ppermute x31 -> x30, waiting for transfers between devices: 56.4 us -> 52.9 us  [swap(): return lax.ppermute(array, axis, [(j, j ^ distance) for j in range(size)])]
    concatenate x2 -> x3, other arithmetic: 1.59 us -> 0.16 us  [the longest x2 0.15 us: tile_sums(): jnp.concatenate([source_index | target_index << 8, (count + chunk - 1) //...]
  transfers between devices with their start and end apart: 31 -> 30, of which waited for: 16 -> 15; matrix products, arithmetic and copies ran while one was open for 2% -> 4% of each run, Pallas kernels for 9% -> 10%
where the time goes in v2:
time: 119 us
  waiting for transfers between devices  52.9 us (44%)
  starting transfers between devices  33.5 us (28%)
  Pallas kernels  23.7 us (20%)
  local copies, waits for them, and re-layouts  3.1 us (3%)
  other arithmetic  2.35 us (2%)
  matrix products  1.72 us (1%)
  between operations  1.57 us (1%)
    ppermute x30, waiting for transfers between devices, swap(): return lax.ppermute(array, axis, [(j, j ^ distance) for j in range(size)])  52.9 us
    ppermute x30, starting transfers between devices, swap(): return lax.ppermute(array, axis, [(j, j ^ distance) for j in range(size)])  33.5 us
    pallas_call x2, Pallas kernels, tile_sums(): pl.pallas_call(functools.partial(tile_kernel, chunk, len(pieces), flip),...  23.7 us
  transfers between devices with their start and end apart: 30, of which 15 were waited for; matrix products, arithmetic and copies ran while one was open for 4% of the time, Pallas kernels for 10%

profile of v2, /device:TPU:0, one launch (start us, length us, event | category | flops | bytes accessed | tf_op | source)
XLA Modules:
  0.0 118.8 jit_solution(7747563496628129470)
XLA Ops:
  0.6 0.0 copy-start
  0.6 4.0 %collective-permute-start = (bf16[512,128]{1,0:T(8,128)(2,1)}, bf16[512,128]{1,0:T(8,128)(2,1)S(1)}, u32[]{:S(2)}, u32[]{:S(2)}) collective-permute-start(bf16[512,128]{1,0:T(8,128)(2,1)} %param.8), channel_id=1, source_target_pairs={{0,16},{16,0},{32,48},{48,32},{64,80},{80,64},{96,112},{112,96},{1... | collective-permute-start | bytes 393224 | tf_op jit(solution)/shard_map/ppermute | solution.py:16
  5.3 0.7 reduce
  6.0 0.7 reduce.1
  6.8 0.9 constant_dynamic-update-slice_fusion.1
  7.7 0.7 collective-permute-done
  8.4 2.8 %collective-permute-start.3 = (bf16[1024,128]{1,0:T(8,128)(2,1)S(1)}, bf16[1024,128]{1,0:T(8,128)(2,1)S(1)}, u32[]{:S(2)}, u32[]{:S(2)}) collective-permute-start(bf16[1024,128]{1,0:T(8,128)(2,1)S(1)} %constant_dynamic-update-slice_fusion.refs_1_), channel_id=1, source_target_pairs={{0,96},{16,112},{32,64},{48,80},{64,32},{80,48},{96,0},{112,16},{1... | collective-permute-start | bytes 786440 | tf_op jit(solution)/shard_map/ppermute | solution.py:16
  11.3 0.8 collective-permute-start.2
  12.1 0.5 collective-permute-start.1
  12.6 0.1 pad_add_fusion.1.table_ref
  12.7 10.1 %collective-permute-done.3.refs_4_ = bf16[1024,128]{1,0:T(8,128)(2,1)S(1)} collective-permute-done((bf16[1024,128]{1,0:T(8,128)(2,1)S(1)}, bf16[1024,128]{1,0:T(8,128)(2,1)S(1)}, u32[]{:S(2)}, u32[]{:S(2)}) %collective-permute-start.3) | collective-permute-done | bytes 262176 | tf_op jit(solution)/shard_map/ppermute | solution.py:16
  22.8 0.6 collective-permute-done.1.refs_2_
  23.4 12.2 %shard_map.111 = (f32[4096,128]{1,0:T(8,128)S(1)}, bf16[4096,128]{1,0:T(8,128)(2,1)S(1)}, f32[8,128]{1,0:T(8,128)}) custom-call(s32[705]{0:T(1024)S(1)} %pad_add_fusion.1.table_ref, bf16[704,128,128]{2,1,0:T(8,128)(2,1)} %bitcast.28, bf16[1024,128]{1,0:T(8,128)(2,1)S(1)} %constant_dynamic-update-slice_fusion.refs_1_, ...), custom_call_target="tpu_custom_call" | custom-call | flops 11811160064 | bytes 23068672 | tf_op jit(solution)/shard_map/pallas_call | solution.py:77
  35.6 0.1 collective-permute-start.4
  35.7 2.6 %collective-permute-done.4 = bf16[4096,128]{1,0:T(8,128)(2,1)S(1)} collective-permute-done((bf16[4096,128]{1,0:T(8,128)(2,1)S(1)}, bf16[4096,128]{1,0:T(8,128)(2,1)S(1)}, u32[]{:S(2)}, u32[]{:S(2)}) %collective-permute-start.4) | collective-permute-done | bytes 1048608 | tf_op jit(solution)/shard_map/ppermute | solution.py:16
  38.4 0.2 add_convert_fusion
  38.6 0.0 copy-start.1
  38.6 0.1 fusion.34
  38.7 2.4 %collective-permute-start.5 = (bf16[1024,128]{1,0:T(8,128)(2,1)S(1)}, bf16[1024,128]{1,0:T(8,128)(2,1)S(1)}, u32[]{:S(2)}, u32[]{:S(2)}) collective-permute-start(bf16[1024,128]{1,0:T(8,128)(2,1)S(1)} %get-tuple-element.25), channel_id=1, source_target_pairs={{0,8},{1,9},{2,10},{3,11},{4,12},{5,13},{6,14},{7,15},{8,0},{9,1},... | collective-permute-start | bytes 786440 | tf_op jit(solution)/shard_map/ppermute | solution.py:16
  41.1 1.1 collective-permute-start.6
  42.2 7.2 %collective-permute-done.5 = bf16[1024,128]{1,0:T(8,128)(2,1)S(1)} collective-permute-done((bf16[1024,128]{1,0:T(8,128)(2,1)S(1)}, bf16[1024,128]{1,0:T(8,128)(2,1)S(1)}, u32[]{:S(2)}, u32[]{:S(2)}) %collective-permute-start.5) | collective-permute-done | bytes 262176 | tf_op jit(solution)/shard_map/ppermute | solution.py:16
  49.4 4.8 %collective-permute-done.7 = bf16[1024,128]{1,0:T(8,128)(2,1)S(1)} collective-permute-done((bf16[1024,128]{1,0:T(8,128)(2,1)S(1)}, bf16[1024,128]{1,0:T(8,128)(2,1)S(1)}, u32[]{:S(2)}, u32[]{:S(2)}) %collective-permute-start.7) | collective-permute-done | bytes 262176 | tf_op jit(solution)/shard_map/ppermute | solution.py:16
  54.2 0.1 convert_add_fusion.1
  54.4 0.1 collective-permute-start.8
  54.5 5.4 %collective-permute-done.8 = bf16[512,128]{1,0:T(8,128)(2,1)S(1)} collective-permute-done((bf16[512,128]{1,0:T(8,128)(2,1)S(1)}, bf16[512,128]{1,0:T(8,128)(2,1)S(1)}, u32[]{:S(2)}, u32[]{:S(2)}) %collective-permute-start.8) | collective-permute-done | bytes 131104 | tf_op jit(solution)/shard_map/ppermute | solution.py:16
  59.9 1.3 %fusion.2 = (bf16[512,256]{1,0:T(8,128)(2,1)S(1)}, bf16[512,256]{1,0:T(8,128)(2,1)}) fusion(bf16[512,256]{1,0:T(8,128)(2,1)S(1)} %copy-done.1, f32[256]{0:T(256)S(1)} %copy-done.2, bf16[512,128]{1,0:T(8,128)(2,1)S(1)} %fusion.11, bf16[128,256]{1,0:T(8,128)(2,1)S(1)} %copy-done), kind=kOutput, calls=%fused_computation.9 | convolution fusion | flops 36700160 | bytes 984064 | tf_op jit(solution)/shard_map/dot_general | solution.py:130
  61.2 0.2 convolution_convert_fusion
  61.4 0.4 collective-permute-start.9
  61.8 0.1 convert_reduce_fusion
  61.9 0.2 fusion.35
  62.1 0.1 collective-permute-start.21
  62.2 4.2 %collective-permute-done.9 = bf16[512,128]{1,0:T(8,128)(2,1)S(1)} collective-permute-done((bf16[512,128]{1,0:T(8,128)(2,1)S(1)}, bf16[512,128]{1,0:T(8,128)(2,1)S(1)}, u32[]{:S(2)}, u32[]{:S(2)}) %collective-permute-start.9) | collective-permute-done | bytes 131104 | tf_op jit(solution)/shard_map/ppermute | solution.py:16
  66.5 2.0 %collective-permute-start.12 = (bf16[1024,128]{1,0:T(8,128)(2,1)S(1)}, bf16[1024,128]{1,0:T(8,128)(2,1)S(1)}, u32[]{:S(2)}, u32[]{:S(2)}) collective-permute-start(bf16[1024,128]{1,0:T(8,128)(2,1)S(1)} %pad_maximum_fusion.refs_1_), channel_id=1, source_target_pairs={{0,12},{1,13},{2,14},{3,15},{4,8},{5,9},{6,10},{7,11},{8,4},{9,5},... | collective-permute-start | bytes 786440 | tf_op jit(solution)/shard_map/ppermute | solution.py:16
  68.5 0.6 collective-permute-start.11
  69.1 1.6 %collective-permute-start.10 = (bf16[1024,128]{1,0:T(8,128)(2,1)S(1)}, bf16[1024,128]{1,0:T(8,128)(2,1)S(1)}, u32[]{:S(2)}, u32[]{:S(2)}) collective-permute-start(bf16[1024,128]{1,0:T(8,128)(2,1)S(1)} %pad_maximum_fusion.refs_1_), channel_id=1, source_target_pairs={{0,4},{1,5},{2,6},{3,7},{4,0},{5,1},{6,2},{7,3},{8,12},{9,13},{10,... | collective-permute-start | bytes 786440 | tf_op jit(solution)/shard_map/ppermute | solution.py:16
  70.7 2.8 %collective-permute-start.24 = (f32[136,256]{1,0:T(8,128)S(1)}, f32[136,256]{1,0:T(8,128)S(1)}, u32[]{:S(2)}, u32[]{:S(2)}) collective-permute-start(f32[136,256]{1,0:T(8,128)S(1)} %fusion.31), channel_id=1, source_target_pairs={{0,96},{16,112},{32,64},{48,80},{64,32},{80,48},{96,0},{112,16},{1... | collective-permute-start | bytes 417800 | tf_op jit(solution)/shard_map/ppermute | solution.py:16
  73.5 0.8 collective-permute-start.23
  74.3 2.8 %collective-permute-done.24 = f32[136,256]{1,0:T(8,128)S(1)} collective-permute-done((f32[136,256]{1,0:T(8,128)S(1)}, f32[136,256]{1,0:T(8,128)S(1)}, u32[]{:S(2)}, u32[]{:S(2)}) %collective-permute-start.24) | collective-permute-done | bytes 139296 | tf_op jit(solution)/shard_map/ppermute | solution.py:16
  77.0 0.6 collective-permute-start.22
  77.6 3.3 %collective-permute-done.23 = f32[136,256]{1,0:T(8,128)S(1)} collective-permute-done((f32[136,256]{1,0:T(8,128)S(1)}, f32[136,256]{1,0:T(8,128)S(1)}, u32[]{:S(2)}, u32[]{:S(2)}) %collective-permute-start.23) | collective-permute-done | bytes 139296 | tf_op jit(solution)/shard_map/ppermute | solution.py:16
  81.0 0.5 collective-permute-start.16
  81.5 0.1 collective-permute-start.15
  81.6 0.4 collective-permute-start.14
  82.0 0.1 pad_add_fusion.table_ref
  82.1 0.0 collective-permute-done.22
  82.1 3.2 %collective-permute-start.25 = (f32[136,256]{1,0:T(8,128)S(1)}, f32[136,256]{1,0:T(8,128)S(1)}, u32[]{:S(2)}, u32[]{:S(2)}) collective-permute-start(f32[136,256]{1,0:T(8,128)S(1)} %add_add_fusion.2), channel_id=1, source_target_pairs={{0,16},{16,0},{32,48},{48,32},{64,80},{80,64},{96,112},{112,96},{1... | collective-permute-start | bytes 417800 | tf_op jit(solution)/shard_map/ppermute | solution.py:16
  85.4 11.5 %shard_map.112 = (bf16[4096,128]{1,0:T(8,128)(2,1)S(1)}, f32[136,256]{1,0:T(8,128)S(1)}) custom-call(s32[705]{0:T(1024)S(1)} %pad_add_fusion.table_ref, bf16[704,128,128]{2,1,0:T(8,128)(2,1)} %bitcast.29, bf16[1024,128]{1,0:T(8,128)(2,1)S(1)} %pad_maximum_fusion.refs_1_, bf16[1024,128]{1,0:T(8,128)(2,1)S(1)} %collective-permute-done.10.refs_2_, ...), custom_call_target="tpu_custom_call" | custom-call | flops 11811160064 | bytes 23068672 | tf_op jit(solution)/shard_map/pallas_call | solution.py:77
  96.9 0.1 fusion.33
  96.9 0.1 collective-permute-start.17
  97.0 0.8 collective-permute-start.19
  97.9 2.6 %collective-permute-start.18 = (bf16[1024,128]{1,0:T(8,128)(2,1)S(1)}, bf16[1024,128]{1,0:T(8,128)(2,1)S(1)}, u32[]{:S(2)}, u32[]{:S(2)}) collective-permute-start(bf16[1024,128]{1,0:T(8,128)(2,1)S(1)} %get-tuple-element.24), channel_id=1, source_target_pairs={{0,32},{16,48},{32,0},{48,16},{64,96},{80,112},{96,64},{112,80},{1... | collective-permute-start | bytes 786440 | tf_op jit(solution)/shard_map/ppermute | solution.py:16
  100.5 0.1 collective-permute-start.26
  100.6 5.0 %collective-permute-done.26 = f32[136,256]{1,0:T(8,128)S(1)} collective-permute-done((f32[136,256]{1,0:T(8,128)S(1)}, f32[136,256]{1,0:T(8,128)S(1)}, u32[]{:S(2)}, u32[]{:S(2)}) %collective-permute-start.26) | collective-permute-done | bytes 139296 | tf_op jit(solution)/shard_map/ppermute | solution.py:16
  105.7 3.9 %collective-permute-start.29 = (f32[136,256]{1,0:T(8,128)S(1)}, f32[136,256]{1,0:T(8,128)S(1)}, u32[]{:S(2)}, u32[]{:S(2)}) collective-permute-start(f32[136,256]{1,0:T(8,128)S(1)} %add.132), channel_id=1, source_target_pairs={{0,12},{1,13},{2,14},{3,15},{4,8},{5,9},{6,10},{7,11},{8,4},{9,5},... | collective-permute-start | bytes 417800 | tf_op jit(solution)/shard_map/ppermute | solution.py:16
  109.6 0.9 collective-permute-start.27
  110.6 0.3 collective-permute-done.19
  110.9 0.1 convert_add_fusion
  111.0 0.1 collective-permute-start.20
  111.1 2.6 %collective-permute-done.29 = f32[136,256]{1,0:T(8,128)S(1)} collective-permute-done((f32[136,256]{1,0:T(8,128)S(1)}, f32[136,256]{1,0:T(8,128)S(1)}, u32[]{:S(2)}, u32[]{:S(2)}) %collective-permute-start.29) | collective-permute-done | bytes 139296 | tf_op jit(solution)/shard_map/ppermute | solution.py:16
  113.7 2.5 %collective-permute-done.28 = f32[136,256]{1,0:T(8,128)S(1)} collective-permute-done((f32[136,256]{1,0:T(8,128)S(1)}, f32[136,256]{1,0:T(8,128)S(1)}, u32[]{:S(2)}, u32[]{:S(2)}) %collective-permute-start.28) | collective-permute-done | bytes 139296 | tf_op jit(solution)/shard_map/ppermute | solution.py:16
  116.2 0.6 slice.75
  116.8 0.7 slice.74
  117.4 0.6 collective-permute-done.20
  118.1 0.8 copy.12
  (36 shorter events, 0.4 us)
Async XLA Ops:
  0.6 59.3 %copy-start = (bf16[128,256]{1,0:T(8,128)(2,1)S(1)}, bf16[128,256]{1,0:T(8,128)(2,1)}, u32[]{:S(2)}) copy-start(bf16[128,256]{1,0:T(8,128)(2,1)} %param.9) | copy-start | bytes 196612
  0.6 7.7 %collective-permute-start = (bf16[512,128]{1,0:T(8,128)(2,1)}, bf16[512,128]{1,0:T(8,128)(2,1)S(1)}, u32[]{:S(2)}, u32[]{:S(2)}) collective-permute-start(bf16[512,128]{1,0:T(8,128)(2,1)} %param.8), channel_id=1, source_target_pairs={{0,16},{16,0},{32,48},{48,32},{64,80},{80,64},{96,112},{112,96},{1... | collective-permute-start | bytes 393224 | tf_op jit(solution)/shard_map/ppermute | solution.py:16
  8.4 14.4 %collective-permute-start.3 = (bf16[1024,128]{1,0:T(8,128)(2,1)S(1)}, bf16[1024,128]{1,0:T(8,128)(2,1)S(1)}, u32[]{:S(2)}, u32[]{:S(2)}) collective-permute-start(bf16[1024,128]{1,0:T(8,128)(2,1)S(1)} %constant_dynamic-update-slice_fusion.refs_1_), channel_id=1, source_target_pairs={{0,96},{16,112},{32,64},{48,80},{64,32},{80,48},{96,0},{112,16},{1... | collective-permute-start | bytes 786440 | tf_op jit(solution)/shard_map/ppermute | solution.py:16
  11.3 11.6 %collective-permute-start.2 = (bf16[1024,128]{1,0:T(8,128)(2,1)S(1)}, bf16[1024,128]{1,0:T(8,128)(2,1)S(1)}, u32[]{:S(2)}, u32[]{:S(2)}) collective-permute-start(bf16[1024,128]{1,0:T(8,128)(2,1)S(1)} %constant_dynamic-update-slice_fusion.refs_1_), channel_id=1, source_target_pairs={{0,64},{16,80},{32,96},{48,112},{64,0},{80,16},{96,32},{112,48},{1... | collective-permute-start | bytes 786440 | tf_op jit(solution)/shard_map/ppermute | solution.py:16
  12.1 11.4 %collective-permute-start.1 = (bf16[1024,128]{1,0:T(8,128)(2,1)S(1)}, bf16[1024,128]{1,0:T(8,128)(2,1)S(1)}, u32[]{:S(2)}, u32[]{:S(2)}) collective-permute-start(bf16[1024,128]{1,0:T(8,128)(2,1)S(1)} %constant_dynamic-update-slice_fusion.refs_1_), channel_id=1, source_target_pairs={{0,32},{16,48},{32,0},{48,16},{64,96},{80,112},{96,64},{112,80},{1... | collective-permute-start | bytes 786440 | tf_op jit(solution)/shard_map/ppermute | solution.py:16
  35.6 2.7 %collective-permute-start.4 = (bf16[4096,128]{1,0:T(8,128)(2,1)S(1)}, bf16[4096,128]{1,0:T(8,128)(2,1)S(1)}, u32[]{:S(2)}, u32[]{:S(2)}) collective-permute-start(bf16[4096,128]{1,0:T(8,128)(2,1)S(1)} %get-tuple-element.13), channel_id=1, source_target_pairs={{0,1},{1,0},{2,3},{3,2},{4,5},{5,4},{6,7},{7,6},{8,9},{9,8},{10,11... | collective-permute-start | bytes 3145736 | tf_op jit(solution)/shard_map/ppermute | solution.py:16
  38.6 21.3 %copy-start.1 = (bf16[512,256]{1,0:T(8,128)(2,1)S(1)}, bf16[512,256]{1,0:T(8,128)(2,1)}, u32[]{:S(2)}) copy-start(bf16[512,256]{1,0:T(8,128)(2,1)} %param.15) | copy-start | bytes 786436
  38.6 21.3 %copy-start.2 = (f32[256]{0:T(256)S(1)}, f32[256]{0:T(256)}, u32[]{:S(2)}) copy-start(f32[256]{0:T(256)} %param.10) | copy-start | bytes 3076
  38.7 10.8 %collective-permute-start.5 = (bf16[1024,128]{1,0:T(8,128)(2,1)S(1)}, bf16[1024,128]{1,0:T(8,128)(2,1)S(1)}, u32[]{:S(2)}, u32[]{:S(2)}) collective-permute-start(bf16[1024,128]{1,0:T(8,128)(2,1)S(1)} %get-tuple-element.25), channel_id=1, source_target_pairs={{0,8},{1,9},{2,10},{3,11},{4,12},{5,13},{6,14},{7,15},{8,0},{9,1},... | collective-permute-start | bytes 786440 | tf_op jit(solution)/shard_map/ppermute | solution.py:16
  41.1 13.1 %collective-permute-start.7 = (bf16[1024,128]{1,0:T(8,128)(2,1)S(1)}, bf16[1024,128]{1,0:T(8,128)(2,1)S(1)}, u32[]{:S(2)}, u32[]{:S(2)}) collective-permute-start(bf16[1024,128]{1,0:T(8,128)(2,1)S(1)} %get-tuple-element.26), channel_id=1, source_target_pairs={{0,12},{1,13},{2,14},{3,15},{4,8},{5,9},{6,10},{7,11},{8,4},{9,5},... | collective-permute-start | bytes 786440 | tf_op jit(solution)/shard_map/ppermute | solution.py:16
  41.1 13.1 %collective-permute-start.6 = (bf16[1024,128]{1,0:T(8,128)(2,1)S(1)}, bf16[1024,128]{1,0:T(8,128)(2,1)S(1)}, u32[]{:S(2)}, u32[]{:S(2)}) collective-permute-start(bf16[1024,128]{1,0:T(8,128)(2,1)S(1)} %get-tuple-element.27), channel_id=1, source_target_pairs={{0,4},{1,5},{2,6},{3,7},{4,0},{5,1},{6,2},{7,3},{8,12},{9,13},{10,... | collective-permute-start | bytes 786440 | tf_op jit(solution)/shard_map/ppermute | solution.py:16
  54.4 5.5 %collective-permute-start.8 = (bf16[512,128]{1,0:T(8,128)(2,1)S(1)}, bf16[512,128]{1,0:T(8,128)(2,1)S(1)}, u32[]{:S(2)}, u32[]{:S(2)}) collective-permute-start(bf16[512,128]{1,0:T(8,128)(2,1)S(1)} %slice.87), channel_id=1, source_target_pairs={{0,2},{1,3},{2,0},{3,1},{4,6},{5,7},{6,4},{7,5},{8,10},{9,11},{10,... | collective-permute-start | bytes 393224 | tf_op jit(solution)/shard_map/ppermute | solution.py:16
  61.4 5.0 %collective-permute-start.9 = (bf16[512,128]{1,0:T(8,128)(2,1)S(1)}, bf16[512,128]{1,0:T(8,128)(2,1)S(1)}, u32[]{:S(2)}, u32[]{:S(2)}) collective-permute-start(bf16[512,128]{1,0:T(8,128)(2,1)S(1)} %bitcast.23), channel_id=1, source_target_pairs={{0,2},{1,3},{2,0},{3,1},{4,6},{5,7},{6,4},{7,5},{8,10},{9,11},{10,... | collective-permute-start | bytes 393224 | tf_op jit(solution)/shard_map/ppermute | solution.py:16
  62.1 8.5 %collective-permute-start.21 = (f32[136,256]{1,0:T(8,128)S(1)}, f32[136,256]{1,0:T(8,128)S(1)}, u32[]{:S(2)}, u32[]{:S(2)}) collective-permute-start(f32[136,256]{1,0:T(8,128)S(1)} %pad_maximum_fusion.1), channel_id=1, source_target_pairs={{0,1},{1,0},{2,3},{3,2},{4,5},{5,4},{6,7},{7,6},{8,9},{9,8},{10,11... | collective-permute-start | bytes 417800 | tf_op jit(solution)/shard_map/ppermute | solution.py:16
  66.5 14.5 %collective-permute-start.12 = (bf16[1024,128]{1,0:T(8,128)(2,1)S(1)}, bf16[1024,128]{1,0:T(8,128)(2,1)S(1)}, u32[]{:S(2)}, u32[]{:S(2)}) collective-permute-start(bf16[1024,128]{1,0:T(8,128)(2,1)S(1)} %pad_maximum_fusion.refs_1_), channel_id=1, source_target_pairs={{0,12},{1,13},{2,14},{3,15},{4,8},{5,9},{6,10},{7,11},{8,4},{9,5},... | collective-permute-start | bytes 786440 | tf_op jit(solution)/shard_map/ppermute | solution.py:16
  68.5 12.9 %collective-permute-start.11 = (bf16[1024,128]{1,0:T(8,128)(2,1)S(1)}, bf16[1024,128]{1,0:T(8,128)(2,1)S(1)}, u32[]{:S(2)}, u32[]{:S(2)}) collective-permute-start(bf16[1024,128]{1,0:T(8,128)(2,1)S(1)} %pad_maximum_fusion.refs_1_), channel_id=1, source_target_pairs={{0,8},{1,9},{2,10},{3,11},{4,12},{5,13},{6,14},{7,15},{8,0},{9,1},... | collective-permute-start | bytes 786440 | tf_op jit(solution)/shard_map/ppermute | solution.py:16
  69.1 12.5 %collective-permute-start.10 = (bf16[1024,128]{1,0:T(8,128)(2,1)S(1)}, bf16[1024,128]{1,0:T(8,128)(2,1)S(1)}, u32[]{:S(2)}, u32[]{:S(2)}) collective-permute-start(bf16[1024,128]{1,0:T(8,128)(2,1)S(1)} %pad_maximum_fusion.refs_1_), channel_id=1, source_target_pairs={{0,4},{1,5},{2,6},{3,7},{4,0},{5,1},{6,2},{7,3},{8,12},{9,13},{10,... | collective-permute-start | bytes 786440 | tf_op jit(solution)/shard_map/ppermute | solution.py:16
  70.7 6.3 %collective-permute-start.24 = (f32[136,256]{1,0:T(8,128)S(1)}, f32[136,256]{1,0:T(8,128)S(1)}, u32[]{:S(2)}, u32[]{:S(2)}) collective-permute-start(f32[136,256]{1,0:T(8,128)S(1)} %fusion.31), channel_id=1, source_target_pairs={{0,96},{16,112},{32,64},{48,80},{64,32},{80,48},{96,0},{112,16},{1... | collective-permute-start | bytes 417800 | tf_op jit(solution)/shard_map/ppermute | solution.py:16
  73.5 7.5 %collective-permute-start.23 = (f32[136,256]{1,0:T(8,128)S(1)}, f32[136,256]{1,0:T(8,128)S(1)}, u32[]{:S(2)}, u32[]{:S(2)}) collective-permute-start(f32[136,256]{1,0:T(8,128)S(1)} %fusion.31), channel_id=1, source_target_pairs={{0,64},{16,80},{32,96},{48,112},{64,0},{80,16},{96,32},{112,48},{1... | collective-permute-start | bytes 417800 | tf_op jit(solution)/shard_map/ppermute | solution.py:16
  77.0 5.1 %collective-permute-start.22 = (f32[136,256]{1,0:T(8,128)S(1)}, f32[136,256]{1,0:T(8,128)S(1)}, u32[]{:S(2)}, u32[]{:S(2)}) collective-permute-start(f32[136,256]{1,0:T(8,128)S(1)} %fusion.31), channel_id=1, source_target_pairs={{0,32},{16,48},{32,0},{48,16},{64,96},{80,112},{96,64},{112,80},{1... | collective-permute-start | bytes 417800 | tf_op jit(solution)/shard_map/ppermute | solution.py:16
  80.9 4.4 %collective-permute-start.13 = (bf16[1024,128]{1,0:T(8,128)(2,1)S(1)}, bf16[1024,128]{1,0:T(8,128)(2,1)S(1)}, u32[]{:S(2)}, u32[]{:S(2)}) collective-permute-start(bf16[1024,128]{1,0:T(8,128)(2,1)S(1)} %pad_maximum_fusion.refs_1_), channel_id=1, source_target_pairs={{0,1},{1,0},{2,3},{3,2},{4,5},{5,4},{6,7},{7,6},{8,9},{9,8},{10,11... | collective-permute-start | bytes 786440 | tf_op jit(solution)/shard_map/ppermute | solution.py:16
  81.0 4.4 %collective-permute-start.16 = (bf16[1024,128]{1,0:T(8,128)(2,1)S(1)}, bf16[1024,128]{1,0:T(8,128)(2,1)S(1)}, u32[]{:S(2)}, u32[]{:S(2)}) collective-permute-start(bf16[1024,128]{1,0:T(8,128)(2,1)S(1)} %collective-permute-done.12.refs_4_), channel_id=1, source_target_pairs={{0,1},{1,0},{2,3},{3,2},{4,5},{5,4},{6,7},{7,6},{8,9},{9,8},{10,11... | collective-permute-start | bytes 786440 | tf_op jit(solution)/shard_map/ppermute | solution.py:16
  81.5 3.9 %collective-permute-start.15 = (bf16[1024,128]{1,0:T(8,128)(2,1)S(1)}, bf16[1024,128]{1,0:T(8,128)(2,1)S(1)}, u32[]{:S(2)}, u32[]{:S(2)}) collective-permute-start(bf16[1024,128]{1,0:T(8,128)(2,1)S(1)} %collective-permute-done.11.refs_3_), channel_id=1, source_target_pairs={{0,1},{1,0},{2,3},{3,2},{4,5},{5,4},{6,7},{7,6},{8,9},{9,8},{10,11... | collective-permute-start | bytes 786440 | tf_op jit(solution)/shard_map/ppermute | solution.py:16
  81.6 3.8 %collective-permute-start.14 = (bf16[1024,128]{1,0:T(8,128)(2,1)S(1)}, bf16[1024,128]{1,0:T(8,128)(2,1)S(1)}, u32[]{:S(2)}, u32[]{:S(2)}) collective-permute-start(bf16[1024,128]{1,0:T(8,128)(2,1)S(1)} %collective-permute-done.10.refs_2_), channel_id=1, source_target_pairs={{0,1},{1,0},{2,3},{3,2},{4,5},{5,4},{6,7},{7,6},{8,9},{9,8},{10,11... | collective-permute-start | bytes 786440 | tf_op jit(solution)/shard_map/ppermute | solution.py:16
  82.1 18.4 %collective-permute-start.25 = (f32[136,256]{1,0:T(8,128)S(1)}, f32[136,256]{1,0:T(8,128)S(1)}, u32[]{:S(2)}, u32[]{:S(2)}) collective-permute-start(f32[136,256]{1,0:T(8,128)S(1)} %add_add_fusion.2), channel_id=1, source_target_pairs={{0,16},{16,0},{32,48},{48,32},{64,80},{80,64},{96,112},{112,96},{1... | collective-permute-start | bytes 417800 | tf_op jit(solution)/shard_map/ppermute | solution.py:16
  96.9 12.7 %collective-permute-start.17 = (bf16[1024,128]{1,0:T(8,128)(2,1)S(1)}, bf16[1024,128]{1,0:T(8,128)(2,1)S(1)}, u32[]{:S(2)}, u32[]{:S(2)}) collective-permute-start(bf16[1024,128]{1,0:T(8,128)(2,1)S(1)} %get-tuple-element.22), channel_id=1, source_target_pairs={{0,64},{16,80},{32,96},{48,112},{64,0},{80,16},{96,32},{112,48},{1... | collective-permute-start | bytes 786440 | tf_op jit(solution)/shard_map/ppermute | solution.py:16
  97.0 13.8 %collective-permute-start.19 = (bf16[1024,128]{1,0:T(8,128)(2,1)S(1)}, bf16[1024,128]{1,0:T(8,128)(2,1)S(1)}, u32[]{:S(2)}, u32[]{:S(2)}) collective-permute-start(bf16[1024,128]{1,0:T(8,128)(2,1)S(1)} %get-tuple-element.23), channel_id=1, source_target_pairs={{0,96},{16,112},{32,64},{48,80},{64,32},{80,48},{96,0},{112,16},{1... | collective-permute-start | bytes 786440 | tf_op jit(solution)/shard_map/ppermute | solution.py:16
  97.9 13.0 %collective-permute-start.18 = (bf16[1024,128]{1,0:T(8,128)(2,1)S(1)}, bf16[1024,128]{1,0:T(8,128)(2,1)S(1)}, u32[]{:S(2)}, u32[]{:S(2)}) collective-permute-start(bf16[1024,128]{1,0:T(8,128)(2,1)S(1)} %get-tuple-element.24), channel_id=1, source_target_pairs={{0,32},{16,48},{32,0},{48,16},{64,96},{80,112},{96,64},{112,80},{1... | collective-permute-start | bytes 786440 | tf_op jit(solution)/shard_map/ppermute | solution.py:16
  100.5 5.1 %collective-permute-start.26 = (f32[136,256]{1,0:T(8,128)S(1)}, f32[136,256]{1,0:T(8,128)S(1)}, u32[]{:S(2)}, u32[]{:S(2)}) collective-permute-start(f32[136,256]{1,0:T(8,128)S(1)} %add_add_fusion.1), channel_id=1, source_target_pairs={{0,2},{1,3},{2,0},{3,1},{4,6},{5,7},{6,4},{7,5},{8,10},{9,11},{10,... | collective-permute-start | bytes 417800 | tf_op jit(solution)/shard_map/ppermute | solution.py:16
  105.7 8.0 %collective-permute-start.29 = (f32[136,256]{1,0:T(8,128)S(1)}, f32[136,256]{1,0:T(8,128)S(1)}, u32[]{:S(2)}, u32[]{:S(2)}) collective-permute-start(f32[136,256]{1,0:T(8,128)S(1)} %add.132), channel_id=1, source_target_pairs={{0,12},{1,13},{2,14},{3,15},{4,8},{5,9},{6,10},{7,11},{8,4},{9,5},... | collective-permute-start | bytes 417800 | tf_op jit(solution)/shard_map/ppermute | solution.py:16
  109.6 6.6 %collective-permute-start.28 = (f32[136,256]{1,0:T(8,128)S(1)}, f32[136,256]{1,0:T(8,128)S(1)}, u32[]{:S(2)}, u32[]{:S(2)}) collective-permute-start(f32[136,256]{1,0:T(8,128)S(1)} %add.132), channel_id=1, source_target_pairs={{0,8},{1,9},{2,10},{3,11},{4,12},{5,13},{6,14},{7,15},{8,0},{9,1},... | collective-permute-start | bytes 417800 | tf_op jit(solution)/shard_map/ppermute | solution.py:16
  109.6 6.6 %collective-permute-start.27 = (f32[136,256]{1,0:T(8,128)S(1)}, f32[136,256]{1,0:T(8,128)S(1)}, u32[]{:S(2)}, u32[]{:S(2)}) collective-permute-start(f32[136,256]{1,0:T(8,128)S(1)} %add.132), channel_id=1, source_target_pairs={{0,4},{1,5},{2,6},{3,7},{4,0},{5,1},{6,2},{7,3},{8,12},{9,13},{10,... | collective-permute-start | bytes 417800 | tf_op jit(solution)/shard_map/ppermute | solution.py:16
  111.0 7.0 %collective-permute-start.20 = (bf16[512,128]{1,0:T(8,128)(2,1)S(1)}, bf16[512,128]{1,0:T(8,128)(2,1)S(1)}, u32[]{:S(2)}, u32[]{:S(2)}) collective-permute-start(bf16[512,128]{1,0:T(8,128)(2,1)S(1)} %slice.86), channel_id=1, source_target_pairs={{0,16},{16,0},{32,48},{48,32},{64,80},{80,64},{96,112},{112,96},{1... | collective-permute-start | bytes 393224 | tf_op jit(solution)/shard_map/ppermute | solution.py:16

commit v3 on v2

v3 whole, which is shorter than its diff:
```python
import functools

import jax
import jax.numpy as jnp
from jax import lax
from jax.experimental import pallas as pl
from jax.experimental.pallas import tpu as pltpu
from jax.sharding import PartitionSpec as P

HALF = jnp.bfloat16
FULL = jnp.float32


def swap(array, axis, distance):
    size = lax.axis_size(axis)
    return lax.ppermute(array, axis, [(j, j ^ distance) for j in range(size)])


def tile_kernel(chunk, num_pieces, num_totals, num_ready, flip, table_any, *refs):
    values_hbm = refs[0]
    pieces = refs[1 : 1 + num_pieces]
    outs = refs[1 + num_pieces + num_ready : -6]
    source, values, total, sems = refs[-6:-2]
    table_ref, table_sem = refs[-2:]
    num_chunks = values.shape[0] // chunk

    def copy(i):
        span = pl.ds(i * chunk, chunk)
        return pltpu.make_async_copy(values_hbm.at[span], values.at[span], sems.at[i])

    fetch = pltpu.make_async_copy(table_any, table_ref, table_sem)
    fetch.start()
    copy(0).start()
    first = 0
    for piece in pieces:
        tiles = piece.shape[0] // source.shape[1]
        source[pl.ds(first, tiles)] = piece[...].reshape((tiles,) + source.shape[1:])
        first += tiles
    fetch.wait()
    live_chunks = table_ref[values.shape[0]]
    for i in range(1, num_chunks):

        @pl.when(i < live_chunks)
        def _():
            copy(i).start()

    total[...] = jnp.zeros_like(total)

    def step(i, carry):
        copy(i).wait()
        products, targets = [], []
        for u in range(chunk):
            slot = i * chunk + u
            entry = table_ref[slot]
            picked = source[entry & 255]
            pair = (picked, values[slot]) if flip else (values[slot], picked)
            products.append(jnp.dot(*pair, preferred_element_type=FULL))
            targets.append(entry >> 8)
        for target, product in zip(targets, products):
            total[target] += product
        return carry

    lax.fori_loop(0, live_chunks, step, 0)
    first = 0
    for out in outs[:num_totals]:
        tiles = out.shape[0] // total.shape[1]
        out[...] = total[pl.ds(first, tiles)].astype(out.dtype).reshape(out.shape)
        first += tiles
    for out in outs[num_totals:]:
        out[...] = jnp.zeros_like(out)


def tile_sums(values, pieces, source_index, target_index, count, out_types, flip, zero_shape=None, ready=None):
    slots, side, _ = values.shape
    chunk = max(d for d in range(1, 65) if slots % d == 0)
    num_source = sum(piece.shape[0] for piece in pieces) // side
    num_out = sum(n for n, _ in out_types)
    width = pieces[0].shape[1]
    target_index = jnp.where(jnp.arange(slots, dtype=jnp.int32) < count, target_index, num_out)
    table = jnp.concatenate([source_index | (target_index << 8), jnp.maximum((count + chunk - 1) // chunk, 1)])
    vmem = pl.BlockSpec(memory_space=pltpu.VMEM)
    return pl.pallas_call(
        functools.partial(tile_kernel, chunk, len(pieces), len(out_types), int(ready is not None), flip),
        out_shape=[jax.ShapeDtypeStruct((n * side, width), kind) for n, kind in out_types]
        + ([jax.ShapeDtypeStruct(zero_shape, FULL)] if zero_shape else []),
        in_specs=[pl.BlockSpec(memory_space=pl.ANY), pl.BlockSpec(memory_space=pltpu.HBM)] + [vmem] * len(pieces)
        + [pl.BlockSpec(memory_space=pl.ANY)] * (ready is not None),
        out_specs=[vmem] * (len(out_types) + bool(zero_shape)),
        scratch_shapes=[
            pltpu.VMEM((num_source, side, width), HALF),
            pltpu.VMEM((slots, side, side), HALF),
            pltpu.VMEM((num_out + 1, side, width), FULL),
            pltpu.SemaphoreType.DMA((slots // chunk,)),
            pltpu.SMEM(table.shape, jnp.int32),
            pltpu.SemaphoreType.DMA,
        ],
        cost_estimate=pl.CostEstimate(
            flops=8 * slots * side * side * width, bytes_accessed=2 * slots * side * side, transcendentals=0
        ),
        compiler_params=pltpu.CompilerParams(vmem_limit_bytes=42 * 2**20),
    )(table, pltpu.with_memory_space_constraint(values, pltpu.HBM), *pieces, *([] if ready is None else [ready]))


def after(array, event):
    return lax.optimization_barrier((array, event))[0]


def shards(features, weight, bias, tile_values, tile_rows, tile_cols, tile_count, upstream):
    side = tile_values.shape[3]
    width = features.shape[1]
    hidden = weight.shape[1]
    nodes = features.shape[0]
    per = nodes // side
    values = tile_values.reshape(tile_values.shape[2:])
    rows = tile_rows.reshape(-1)
    cols = tile_cols.reshape(-1)
    count = tile_count.reshape(1)
    my_row = lax.axis_index("row")
    my_col = lax.axis_index("col")
    row_owner = (rows // per) ^ my_col
    row_place = (row_owner % 2) * (lax.axis_size("col") // 2 * per) + (row_owner // 2) * per + rows % per
    col_place = ((cols // per) ^ my_row) * per + cols % per

    pair = jnp.concatenate([features, swap(features, "row", 1)], axis=0)
    pieces = [pair] + [swap(pair, "row", d) for d in (2, 4, 6)]
    up_away = swap(upstream, "col", 2)
    half_tiles = lax.axis_size("col") // 2 * per
    keep, send = tile_sums(
        values, pieces, col_place, row_place, count, [(half_tiles, FULL), (half_tiles, HALF)], False, ready=up_away
    )

    block = (keep + swap(send, "col", 1).astype(FULL)).astype(HALF).reshape(4, 2 * nodes, width)
    total = block[0].astype(FULL)
    for other in [swap(block[d], "col", 4 * d) for d in (2, 1, 3)]:
        total = total + other.astype(FULL)
    both = total.astype(HALF)
    both = (both.astype(FULL) + swap(jnp.concatenate([both[nodes:], both[:nodes]], axis=0), "col", 2).astype(FULL)).astype(HALF)
    up = jnp.concatenate([upstream, up_away], axis=0)
    pre = jnp.dot(both, weight, preferred_element_type=FULL) + bias
    activated = jax.nn.gelu(pre[:nodes], approximate=True).astype(HALF)
    _, pullback = jax.vjp(lambda v: jax.nn.gelu(v, approximate=True), pre)
    grad_both = pullback(up.astype(FULL))[0].astype(HALF)
    grad_tiles = grad_both.reshape(2 * per, side, hidden)
    pair = jnp.einsum("fh,tbh->tfb", weight, grad_tiles, preferred_element_type=FULL).astype(HALF)
    pair = pair.reshape(2 * per * width, side)
    grad_agg = pair
    s_half, grad_pre = both[:nodes], grad_both[:nodes]

    s_half, grad_pre = after((s_half, grad_pre), grad_agg)
    weight_term = jnp.dot(s_half.T, grad_pre, preferred_element_type=FULL)
    bias_term = jnp.sum(grad_pre.astype(FULL), axis=0)
    terms = jnp.concatenate([weight_term, jnp.broadcast_to(bias_term[None], (8, hidden))], axis=0)
    terms = (terms + swap(terms, "row", 2)) + (swap(terms, "row", 4) + swap(terms, "row", 6))
    near = [pair] + [swap(pair, "col", d) for d in (4, 8, 12)]
    far = [swap(piece, "col", 1) for piece in near]
    other_terms = [swap(terms, "row", 1)]
    back, zero = tile_sums(
        values, near + far, row_place, col_place, count, [(lax.axis_size("row") * per, HALF)], True, terms.shape
    )
    back = back.reshape(4, 2 * nodes, side)
    total = back[0].astype(FULL)
    for other in [swap(back[d], "row", 2 * d) for d in (2, 1, 3)]:
        total = total + other.astype(FULL)
    terms = (terms + zero) + other_terms[0]
    terms = terms + swap(terms, "col", 2)
    terms = (terms + swap(terms, "col", 4)) + (swap(terms, "col", 8) + swap(terms, "col", 12))
    terms = terms + swap(terms, "col", 1)
    away = swap(total[nodes:].astype(HALF), "row", 1)
    total = total[:nodes] + away.astype(FULL)
    feature_grad = jnp.swapaxes(total.reshape(per, width, side), 1, 2).astype(HALF).reshape(nodes, width)
    return (activated, feature_grad, terms[:width], terms[width])


def solution(mesh):
    in_specs = (
        P(("col", "row"), None),
        P(),
        P(),
        P("row", "col", None, None, None),
        P("row", "col", None),
        P("row", "col", None),
        P("row", "col"),
        P(("row", "col"), None),
    )
    out_specs = (P(("row", "col"), None), P(("col", "row"), None), P(), P())
    return jax.shard_map(shards, mesh=mesh, in_specs=in_specs, out_specs=out_specs, check_vma=False)
```

time: 119 us -> 117 us (0.983)
  Pallas kernels: 23.7 us -> 22 us
  waiting for transfers between devices: 52.9 us -> 51.5 us
    pallas_call x2, Pallas kernels: 23.7 us -> 22 us  [tile_sums(): pl.pallas_call(functools.partial(tile_kernel, chunk, len(pieces), len(out...]
    ppermute x30, waiting for transfers between devices: 52.9 us -> 51.5 us  [swap(): return lax.ppermute(array, axis, [(j, j ^ distance) for j in range(size)])]
  transfers between devices with their start and end apart: 30 -> 30, of which waited for: 15 -> 18; matrix products, arithmetic and copies ran while one was open for 4% -> 4% of each run, Pallas kernels for 10% -> 9%
where the time goes in v3:
time: 117 us; the launch traced here: 116 us
  waiting for transfers between devices  51.5 us (44%)
  starting transfers between devices  33.2 us (28%)
  Pallas kernels  22 us (19%)
  other arithmetic  3.29 us (3%)
  local copies, waits for them, and re-layouts  3.13 us (3%)
  between operations  1.58 us (1%)
  matrix products  1.46 us (1%)
    ppermute x30, waiting for transfers between devices, swap(): return lax.ppermute(array, axis, [(j, j ^ distance) for j in range(size)])  51.5 us
    ppermute x30, starting transfers between devices, swap(): return lax.ppermute(array, axis, [(j, j ^ distance) for j in range(size)])  33.2 us
    pallas_call x2, Pallas kernels, tile_sums(): pl.pallas_call(functools.partial(tile_kernel, chunk, len(pieces), len(out...  22 us
  transfers between devices with their start and end apart: 30, of which 18 were waited for; matrix products, arithmetic and copies ran while one was open for 4% of the time, Pallas kernels for 9%

profile of v3, /device:TPU:0, one launch (start us, length us, event | category | flops | bytes accessed | tf_op | source)
XLA Modules:
  0.0 116.1 jit_solution(5801950596576274233)
XLA Ops:
  0.6 4.0 %collective-permute-start = (bf16[512,128]{1,0:T(8,128)(2,1)}, bf16[512,128]{1,0:T(8,128)(2,1)S(1)}, u32[]{:S(2)}, u32[]{:S(2)}) collective-permute-start(bf16[512,128]{1,0:T(8,128)(2,1)} %param.8), channel_id=1, source_target_pairs={{0,16},{16,0},{32,48},{48,32},{64,80},{80,64},{96,112},{112,96},{1... | collective-permute-start | bytes 393224 | tf_op jit(solution)/shard_map/ppermute | solution.py:16
  4.7 1.0 collective-permute-start.4
  6.4 0.7 reduce
  7.1 0.7 reduce.1
  7.8 0.9 constant_dynamic-update-slice_fusion.1
  8.7 0.5 collective-permute-done
  9.2 2.8 %collective-permute-start.3 = (bf16[1024,128]{1,0:T(8,128)(2,1)S(1)}, bf16[1024,128]{1,0:T(8,128)(2,1)S(1)}, u32[]{:S(2)}, u32[]{:S(2)}) collective-permute-start(bf16[1024,128]{1,0:T(8,128)(2,1)S(1)} %constant_dynamic-update-slice_fusion.refs_1_), channel_id=1, source_target_pairs={{0,96},{16,112},{32,64},{48,80},{64,32},{80,48},{96,0},{112,16},{1... | collective-permute-start | bytes 786440 | tf_op jit(solution)/shard_map/ppermute | solution.py:16
  12.1 0.8 collective-permute-start.2
  12.9 0.5 collective-permute-start.1
  13.4 0.1 pad_add_fusion.1.table_any
  13.5 1.2 %collective-permute-done.4.refs_5_ = bf16[512,256]{1,0:T(8,128)(2,1)S(1)} collective-permute-done((bf16[512,256]{1,0:T(8,128)(2,1)}, bf16[512,256]{1,0:T(8,128)(2,1)S(1)}, u32[]{:S(2)}, u32[]{:S(2)}) %collective-permute-start.4) | collective-permute-done | bytes 262176 | tf_op jit(solution)/shard_map/ppermute | solution.py:16
  14.7 8.4 %collective-permute-done.3.refs_4_ = bf16[1024,128]{1,0:T(8,128)(2,1)S(1)} collective-permute-done((bf16[1024,128]{1,0:T(8,128)(2,1)S(1)}, bf16[1024,128]{1,0:T(8,128)(2,1)S(1)}, u32[]{:S(2)}, u32[]{:S(2)}) %collective-permute-start.3) | collective-permute-done | bytes 262176 | tf_op jit(solution)/shard_map/ppermute | solution.py:16
  23.2 0.6 collective-permute-done.1.refs_2_
  23.8 11.1 %shard_map.111 = (f32[4096,128]{1,0:T(8,128)S(1)}, bf16[4096,128]{1,0:T(8,128)(2,1)S(1)}) custom-call(s32[705]{0:T(1024)S(1)} %pad_add_fusion.1.table_any, bf16[704,128,128]{2,1,0:T(8,128)(2,1)} %bitcast.31, bf16[1024,128]{1,0:T(8,128)(2,1)S(1)} %constant_dynamic-update-slice_fusion.refs_1_, bf16[1024,128]{1,0:T(8,128)(2,1)S(1)} %collective-permute-done.1.refs_2_, ...), custom_call_target="tpu_custom_call" | custom-call | flops 11811160064 | bytes 23068672 | tf_op jit(solution)/shard_map/pallas_call | solution.py:82
  34.9 0.1 collective-permute-start.5
  35.0 2.6 %collective-permute-done.5 = bf16[4096,128]{1,0:T(8,128)(2,1)S(1)} collective-permute-done((bf16[4096,128]{1,0:T(8,128)(2,1)S(1)}, bf16[4096,128]{1,0:T(8,128)(2,1)S(1)}, u32[]{:S(2)}, u32[]{:S(2)}) %collective-permute-start.5) | collective-permute-done | bytes 1048608 | tf_op jit(solution)/shard_map/ppermute | solution.py:16
  37.6 0.2 add_convert_fusion
  37.9 3.3 %collective-permute-start.6 = (bf16[1024,128]{1,0:T(8,128)(2,1)S(1)}, bf16[1024,128]{1,0:T(8,128)(2,1)S(1)}, u32[]{:S(2)}, u32[]{:S(2)}) collective-permute-start(bf16[1024,128]{1,0:T(8,128)(2,1)S(1)} %get-tuple-element.21), channel_id=1, source_target_pairs={{0,8},{1,9},{2,10},{3,11},{4,12},{5,13},{6,14},{7,15},{8,0},{9,1},... | collective-permute-start | bytes 786440 | tf_op jit(solution)/shard_map/ppermute | solution.py:16
  41.2 1.0 collective-permute-start.8
  42.3 6.4 %collective-permute-done.6 = bf16[1024,128]{1,0:T(8,128)(2,1)S(1)} collective-permute-done((bf16[1024,128]{1,0:T(8,128)(2,1)S(1)}, bf16[1024,128]{1,0:T(8,128)(2,1)S(1)}, u32[]{:S(2)}, u32[]{:S(2)}) %collective-permute-start.6) | collective-permute-done | bytes 262176 | tf_op jit(solution)/shard_map/ppermute | solution.py:16
  48.7 4.8 %collective-permute-done.8 = bf16[1024,128]{1,0:T(8,128)(2,1)S(1)} collective-permute-done((bf16[1024,128]{1,0:T(8,128)(2,1)S(1)}, bf16[1024,128]{1,0:T(8,128)(2,1)S(1)}, u32[]{:S(2)}, u32[]{:S(2)}) %collective-permute-start.8) | collective-permute-done | bytes 262176 | tf_op jit(solution)/shard_map/ppermute | solution.py:16
  53.5 0.1 add_convert_fusion.2
  53.7 0.2 collective-permute-start.9
  53.9 8.1 %collective-permute-done.9 = bf16[1024,128]{1,0:T(8,128)(2,1)S(1)} collective-permute-done((bf16[1024,128]{1,0:T(8,128)(2,1)S(1)}, bf16[1024,128]{1,0:T(8,128)(2,1)S(1)}, u32[]{:S(2)}, u32[]{:S(2)}) %collective-permute-start.9) | collective-permute-done | bytes 262176 | tf_op jit(solution)/shard_map/ppermute | solution.py:16
  62.0 0.1 add_convert_fusion.1
  62.1 0.9 fusion.2
  63.1 0.3 convolution_convert_fusion
  63.4 2.3 %collective-permute-start.12 = (bf16[1024,128]{1,0:T(8,128)(2,1)S(1)}, bf16[1024,128]{1,0:T(8,128)(2,1)S(1)}, u32[]{:S(2)}, u32[]{:S(2)}) collective-permute-start(bf16[1024,128]{1,0:T(8,128)(2,1)S(1)} %bitcast.22), channel_id=1, source_target_pairs={{0,12},{1,13},{2,14},{3,15},{4,8},{5,9},{6,10},{7,11},{8,4},{9,5},... | collective-permute-start | bytes 786440 | tf_op jit(solution)/shard_map/ppermute | solution.py:16
  65.7 0.9 collective-permute-start.11
  66.6 1.0 collective-permute-start.10
  67.6 0.1 convert_reduce_fusion
  67.7 0.2 fusion.42
  67.9 3.1 %collective-permute-start.22 = (f32[136,256]{1,0:T(8,128)S(1)}, f32[136,256]{1,0:T(8,128)S(1)}, u32[]{:S(2)}, u32[]{:S(2)}) collective-permute-start(f32[136,256]{1,0:T(8,128)S(1)} %pad_maximum_fusion.1), channel_id=1, source_target_pairs={{0,64},{16,80},{32,96},{48,112},{64,0},{80,16},{96,32},{112,48},{1... | collective-permute-start | bytes 417800 | tf_op jit(solution)/shard_map/ppermute | solution.py:16
  71.0 0.4 collective-permute-start.23
  71.3 3.3 %collective-permute-done.22 = f32[136,256]{1,0:T(8,128)S(1)} collective-permute-done((f32[136,256]{1,0:T(8,128)S(1)}, f32[136,256]{1,0:T(8,128)S(1)}, u32[]{:S(2)}, u32[]{:S(2)}) %collective-permute-start.22) | collective-permute-done | bytes 139296 | tf_op jit(solution)/shard_map/ppermute | solution.py:16
  74.7 0.7 collective-permute-start.21
  75.3 2.0 %collective-permute-done.23 = f32[136,256]{1,0:T(8,128)S(1)} collective-permute-done((f32[136,256]{1,0:T(8,128)S(1)}, f32[136,256]{1,0:T(8,128)S(1)}, u32[]{:S(2)}, u32[]{:S(2)}) %collective-permute-start.23) | collective-permute-done | bytes 139296 | tf_op jit(solution)/shard_map/ppermute | solution.py:16
  77.3 0.4 collective-permute-done.12.refs_4_
  77.7 0.1 collective-permute-start.16
  77.8 0.4 collective-permute-start.15
  78.2 0.1 collective-permute-done.10.refs_2_
  78.3 0.1 pad_add_fusion.table_any
  78.4 1.3 %collective-permute-done.21 = f32[136,256]{1,0:T(8,128)S(1)} collective-permute-done((f32[136,256]{1,0:T(8,128)S(1)}, f32[136,256]{1,0:T(8,128)S(1)}, u32[]{:S(2)}, u32[]{:S(2)}) %collective-permute-start.21) | collective-permute-done | bytes 139296 | tf_op jit(solution)/shard_map/ppermute | solution.py:16
  79.8 2.5 %collective-permute-start.24 = (f32[136,256]{1,0:T(8,128)S(1)}, f32[136,256]{1,0:T(8,128)S(1)}, u32[]{:S(2)}, u32[]{:S(2)}) collective-permute-start(f32[136,256]{1,0:T(8,128)S(1)} %add_add_fusion.2), channel_id=1, source_target_pairs={{0,16},{16,0},{32,48},{48,32},{64,80},{80,64},{96,112},{112,96},{1... | collective-permute-start | bytes 417800 | tf_op jit(solution)/shard_map/ppermute | solution.py:16
  82.3 10.9 %shard_map.112 = (bf16[4096,128]{1,0:T(8,128)(2,1)S(1)}, f32[136,256]{1,0:T(8,128)S(1)}) custom-call(s32[705]{0:T(1024)S(1)} %pad_add_fusion.table_any, bf16[704,128,128]{2,1,0:T(8,128)(2,1)} %bitcast.32, bf16[1024,128]{1,0:T(8,128)(2,1)S(1)} %bitcast.26, bf16[1024,128]{1,0:T(8,128)(2,1)S(1)} %collective-permute-done.10.refs_2_, ...), custom_call_target="tpu_custom_call" | custom-call | flops 11811160064 | bytes 23068672 | tf_op jit(solution)/shard_map/pallas_call | solution.py:82
  93.3 1.8 %collective-permute-start.17 = (bf16[1024,128]{1,0:T(8,128)(2,1)S(1)}, bf16[1024,128]{1,0:T(8,128)(2,1)S(1)}, u32[]{:S(2)}, u32[]{:S(2)}) collective-permute-start(bf16[1024,128]{1,0:T(8,128)(2,1)S(1)} %get-tuple-element.18), channel_id=1, source_target_pairs={{0,64},{16,80},{32,96},{48,112},{64,0},{80,16},{96,32},{112,48},{1... | collective-permute-start | bytes 786440 | tf_op jit(solution)/shard_map/ppermute | solution.py:16
  95.1 0.8 collective-permute-start.19
  95.9 1.0 collective-permute-start.18
  96.9 0.1 collective-permute-start.25
  97.0 0.9 fusion.17
  97.9 4.2 %collective-permute-done.25 = f32[136,256]{1,0:T(8,128)S(1)} collective-permute-done((f32[136,256]{1,0:T(8,128)S(1)}, f32[136,256]{1,0:T(8,128)S(1)}, u32[]{:S(2)}, u32[]{:S(2)}) %collective-permute-start.25) | collective-permute-done | bytes 139296 | tf_op jit(solution)/shard_map/ppermute | solution.py:16
  102.0 2.8 %collective-permute-start.28 = (f32[136,256]{1,0:T(8,128)S(1)}, f32[136,256]{1,0:T(8,128)S(1)}, u32[]{:S(2)}, u32[]{:S(2)}) collective-permute-start(f32[136,256]{1,0:T(8,128)S(1)} %add.141), channel_id=1, source_target_pairs={{0,12},{1,13},{2,14},{3,15},{4,8},{5,9},{6,10},{7,11},{8,4},{9,5},... | collective-permute-start | bytes 417800 | tf_op jit(solution)/shard_map/ppermute | solution.py:16
  104.9 1.0 collective-permute-start.27
  105.9 0.3 collective-permute-start.26
  106.2 1.0 collective-permute-done.19
  107.2 0.1 convert_add_fusion
  107.4 0.1 collective-permute-start.20
  107.5 1.7 %collective-permute-done.28 = f32[136,256]{1,0:T(8,128)S(1)} collective-permute-done((f32[136,256]{1,0:T(8,128)S(1)}, f32[136,256]{1,0:T(8,128)S(1)}, u32[]{:S(2)}, u32[]{:S(2)}) %collective-permute-start.28) | collective-permute-done | bytes 139296 | tf_op jit(solution)/shard_map/ppermute | solution.py:16
  109.2 2.2 %collective-permute-done.27 = f32[136,256]{1,0:T(8,128)S(1)} collective-permute-done((f32[136,256]{1,0:T(8,128)S(1)}, f32[136,256]{1,0:T(8,128)S(1)}, u32[]{:S(2)}, u32[]{:S(2)}) %collective-permute-start.27) | collective-permute-done | bytes 139296 | tf_op jit(solution)/shard_map/ppermute | solution.py:16
  111.5 0.1 collective-permute-start.29
  111.6 2.5 %collective-permute-done.20 = bf16[512,128]{1,0:T(8,128)(2,1)S(1)} collective-permute-done((bf16[512,128]{1,0:T(8,128)(2,1)S(1)}, bf16[512,128]{1,0:T(8,128)(2,1)S(1)}, u32[]{:S(2)}, u32[]{:S(2)}) %collective-permute-start.20) | collective-permute-done | bytes 131104 | tf_op jit(solution)/shard_map/ppermute | solution.py:16
  114.1 0.8 copy.12
  114.9 0.6 slice.89
  115.5 0.7 slice.88
  (39 shorter events, 0.5 us)
Async XLA Ops:
  0.6 61.5 %copy-start = (bf16[128,256]{1,0:T(8,128)(2,1)S(1)}, bf16[128,256]{1,0:T(8,128)(2,1)}, u32[]{:S(2)}) copy-start(bf16[128,256]{1,0:T(8,128)(2,1)} %param.9) | copy-start | bytes 196612
  0.6 8.6 %collective-permute-start = (bf16[512,128]{1,0:T(8,128)(2,1)}, bf16[512,128]{1,0:T(8,128)(2,1)S(1)}, u32[]{:S(2)}, u32[]{:S(2)}) collective-permute-start(bf16[512,128]{1,0:T(8,128)(2,1)} %param.8), channel_id=1, source_target_pairs={{0,16},{16,0},{32,48},{48,32},{64,80},{80,64},{96,112},{112,96},{1... | collective-permute-start | bytes 393224 | tf_op jit(solution)/shard_map/ppermute | solution.py:16
  4.7 10.1 %collective-permute-start.4 = (bf16[512,256]{1,0:T(8,128)(2,1)}, bf16[512,256]{1,0:T(8,128)(2,1)S(1)}, u32[]{:S(2)}, u32[]{:S(2)}) collective-permute-start(bf16[512,256]{1,0:T(8,128)(2,1)} %param.15), channel_id=1, source_target_pairs={{0,2},{1,3},{2,0},{3,1},{4,6},{5,7},{6,4},{7,5},{8,10},{9,11},{10,... | collective-permute-start | bytes 786440 | tf_op jit(solution)/shard_map/ppermute | solution.py:16
  9.2 13.9 %collective-permute-start.3 = (bf16[1024,128]{1,0:T(8,128)(2,1)S(1)}, bf16[1024,128]{1,0:T(8,128)(2,1)S(1)}, u32[]{:S(2)}, u32[]{:S(2)}) collective-permute-start(bf16[1024,128]{1,0:T(8,128)(2,1)S(1)} %constant_dynamic-update-slice_fusion.refs_1_), channel_id=1, source_target_pairs={{0,96},{16,112},{32,64},{48,80},{64,32},{80,48},{96,0},{112,16},{1... | collective-permute-start | bytes 786440 | tf_op jit(solution)/shard_map/ppermute | solution.py:16
  12.1 11.1 %collective-permute-start.2 = (bf16[1024,128]{1,0:T(8,128)(2,1)S(1)}, bf16[1024,128]{1,0:T(8,128)(2,1)S(1)}, u32[]{:S(2)}, u32[]{:S(2)}) collective-permute-start(bf16[1024,128]{1,0:T(8,128)(2,1)S(1)} %constant_dynamic-update-slice_fusion.refs_1_), channel_id=1, source_target_pairs={{0,64},{16,80},{32,96},{48,112},{64,0},{80,16},{96,32},{112,48},{1... | collective-permute-start | bytes 786440 | tf_op jit(solution)/shard_map/ppermute | solution.py:16
  12.9 10.9 %collective-permute-start.1 = (bf16[1024,128]{1,0:T(8,128)(2,1)S(1)}, bf16[1024,128]{1,0:T(8,128)(2,1)S(1)}, u32[]{:S(2)}, u32[]{:S(2)}) collective-permute-start(bf16[1024,128]{1,0:T(8,128)(2,1)S(1)} %constant_dynamic-update-slice_fusion.refs_1_), channel_id=1, source_target_pairs={{0,32},{16,48},{32,0},{48,16},{64,96},{80,112},{96,64},{112,80},{1... | collective-permute-start | bytes 786440 | tf_op jit(solution)/shard_map/ppermute | solution.py:16
  34.9 2.7 %collective-permute-start.5 = (bf16[4096,128]{1,0:T(8,128)(2,1)S(1)}, bf16[4096,128]{1,0:T(8,128)(2,1)S(1)}, u32[]{:S(2)}, u32[]{:S(2)}) collective-permute-start(bf16[4096,128]{1,0:T(8,128)(2,1)S(1)} %get-tuple-element.11), channel_id=1, source_target_pairs={{0,1},{1,0},{2,3},{3,2},{4,5},{5,4},{6,7},{7,6},{8,9},{9,8},{10,11... | collective-permute-start | bytes 3145736 | tf_op jit(solution)/shard_map/ppermute | solution.py:16
  37.9 24.2 %copy-start.1 = (bf16[512,256]{1,0:T(8,128)(2,1)S(1)}, bf16[512,256]{1,0:T(8,128)(2,1)}, u32[]{:S(2)}) copy-start(bf16[512,256]{1,0:T(8,128)(2,1)} %param.15) | copy-start | bytes 786436
  37.9 24.2 %copy-start.2 = (f32[256]{0:T(256)S(1)}, f32[256]{0:T(256)}, u32[]{:S(2)}) copy-start(f32[256]{0:T(256)} %param.10) | copy-start | bytes 3076
  37.9 10.8 %collective-permute-start.6 = (bf16[1024,128]{1,0:T(8,128)(2,1)S(1)}, bf16[1024,128]{1,0:T(8,128)(2,1)S(1)}, u32[]{:S(2)}, u32[]{:S(2)}) collective-permute-start(bf16[1024,128]{1,0:T(8,128)(2,1)S(1)} %get-tuple-element.21), channel_id=1, source_target_pairs={{0,8},{1,9},{2,10},{3,11},{4,12},{5,13},{6,14},{7,15},{8,0},{9,1},... | collective-permute-start | bytes 786440 | tf_op jit(solution)/shard_map/ppermute | solution.py:16
  41.2 12.3 %collective-permute-start.8 = (bf16[1024,128]{1,0:T(8,128)(2,1)S(1)}, bf16[1024,128]{1,0:T(8,128)(2,1)S(1)}, u32[]{:S(2)}, u32[]{:S(2)}) collective-permute-start(bf16[1024,128]{1,0:T(8,128)(2,1)S(1)} %get-tuple-element.22), channel_id=1, source_target_pairs={{0,12},{1,13},{2,14},{3,15},{4,8},{5,9},{6,10},{7,11},{8,4},{9,5},... | collective-permute-start | bytes 786440 | tf_op jit(solution)/shard_map/ppermute | solution.py:16
  42.3 11.2 %collective-permute-start.7 = (bf16[1024,128]{1,0:T(8,128)(2,1)S(1)}, bf16[1024,128]{1,0:T(8,128)(2,1)S(1)}, u32[]{:S(2)}, u32[]{:S(2)}) collective-permute-start(bf16[1024,128]{1,0:T(8,128)(2,1)S(1)} %get-tuple-element.23), channel_id=1, source_target_pairs={{0,4},{1,5},{2,6},{3,7},{4,0},{5,1},{6,2},{7,3},{8,12},{9,13},{10,... | collective-permute-start | bytes 786440 | tf_op jit(solution)/shard_map/ppermute | solution.py:16
  53.7 8.3 %collective-permute-start.9 = (bf16[1024,128]{1,0:T(8,128)(2,1)S(1)}, bf16[1024,128]{1,0:T(8,128)(2,1)S(1)}, u32[]{:S(2)}, u32[]{:S(2)}) collective-permute-start(bf16[1024,128]{1,0:T(8,128)(2,1)S(1)} %pad_maximum_fusion), channel_id=1, source_target_pairs={{0,2},{1,3},{2,0},{3,1},{4,6},{5,7},{6,4},{7,5},{8,10},{9,11},{10,... | collective-permute-start | bytes 786440 | tf_op jit(solution)/shard_map/ppermute | solution.py:16
  63.4 14.3 %collective-permute-start.12 = (bf16[1024,128]{1,0:T(8,128)(2,1)S(1)}, bf16[1024,128]{1,0:T(8,128)(2,1)S(1)}, u32[]{:S(2)}, u32[]{:S(2)}) collective-permute-start(bf16[1024,128]{1,0:T(8,128)(2,1)S(1)} %bitcast.22), channel_id=1, source_target_pairs={{0,12},{1,13},{2,14},{3,15},{4,8},{5,9},{6,10},{7,11},{8,4},{9,5},... | collective-permute-start | bytes 786440 | tf_op jit(solution)/shard_map/ppermute | solution.py:16
  65.7 12.1 %collective-permute-start.11 = (bf16[1024,128]{1,0:T(8,128)(2,1)S(1)}, bf16[1024,128]{1,0:T(8,128)(2,1)S(1)}, u32[]{:S(2)}, u32[]{:S(2)}) collective-permute-start(bf16[1024,128]{1,0:T(8,128)(2,1)S(1)} %bitcast.23), channel_id=1, source_target_pairs={{0,8},{1,9},{2,10},{3,11},{4,12},{5,13},{6,14},{7,15},{8,0},{9,1},... | collective-permute-start | bytes 786440 | tf_op jit(solution)/shard_map/ppermute | solution.py:16
  66.6 11.7 %collective-permute-start.10 = (bf16[1024,128]{1,0:T(8,128)(2,1)S(1)}, bf16[1024,128]{1,0:T(8,128)(2,1)S(1)}, u32[]{:S(2)}, u32[]{:S(2)}) collective-permute-start(bf16[1024,128]{1,0:T(8,128)(2,1)S(1)} %bitcast.24), channel_id=1, source_target_pairs={{0,4},{1,5},{2,6},{3,7},{4,0},{5,1},{6,2},{7,3},{8,12},{9,13},{10,... | collective-permute-start | bytes 786440 | tf_op jit(solution)/shard_map/ppermute | solution.py:16
  67.9 6.7 %collective-permute-start.22 = (f32[136,256]{1,0:T(8,128)S(1)}, f32[136,256]{1,0:T(8,128)S(1)}, u32[]{:S(2)}, u32[]{:S(2)}) collective-permute-start(f32[136,256]{1,0:T(8,128)S(1)} %pad_maximum_fusion.1), channel_id=1, source_target_pairs={{0,64},{16,80},{32,96},{48,112},{64,0},{80,16},{96,32},{112,48},{1... | collective-permute-start | bytes 417800 | tf_op jit(solution)/shard_map/ppermute | solution.py:16
  71.0 6.3 %collective-permute-start.23 = (f32[136,256]{1,0:T(8,128)S(1)}, f32[136,256]{1,0:T(8,128)S(1)}, u32[]{:S(2)}, u32[]{:S(2)}) collective-permute-start(f32[136,256]{1,0:T(8,128)S(1)} %pad_maximum_fusion.1), channel_id=1, source_target_pairs={{0,96},{16,112},{32,64},{48,80},{64,32},{80,48},{96,0},{112,16},{1... | collective-permute-start | bytes 417800 | tf_op jit(solution)/shard_map/ppermute | solution.py:16
  74.7 5.1 %collective-permute-start.21 = (f32[136,256]{1,0:T(8,128)S(1)}, f32[136,256]{1,0:T(8,128)S(1)}, u32[]{:S(2)}, u32[]{:S(2)}) collective-permute-start(f32[136,256]{1,0:T(8,128)S(1)} %pad_maximum_fusion.1), channel_id=1, source_target_pairs={{0,32},{16,48},{32,0},{48,16},{64,96},{80,112},{96,64},{112,80},{1... | collective-permute-start | bytes 417800 | tf_op jit(solution)/shard_map/ppermute | solution.py:16
  77.3 5.0 %collective-permute-start.13 = (bf16[1024,128]{1,0:T(8,128)(2,1)S(1)}, bf16[1024,128]{1,0:T(8,128)(2,1)S(1)}, u32[]{:S(2)}, u32[]{:S(2)}) collective-permute-start(bf16[1024,128]{1,0:T(8,128)(2,1)S(1)} %bitcast.25), channel_id=1, source_target_pairs={{0,1},{1,0},{2,3},{3,2},{4,5},{5,4},{6,7},{7,6},{8,9},{9,8},{10,11... | collective-permute-start | bytes 786440 | tf_op jit(solution)/shard_map/ppermute | solution.py:16
  77.7 4.6 %collective-permute-start.16 = (bf16[1024,128]{1,0:T(8,128)(2,1)S(1)}, bf16[1024,128]{1,0:T(8,128)(2,1)S(1)}, u32[]{:S(2)}, u32[]{:S(2)}) collective-permute-start(bf16[1024,128]{1,0:T(8,128)(2,1)S(1)} %collective-permute-done.12.refs_4_), channel_id=1, source_target_pairs={{0,1},{1,0},{2,3},{3,2},{4,5},{5,4},{6,7},{7,6},{8,9},{9,8},{10,11... | collective-permute-start | bytes 786440 | tf_op jit(solution)/shard_map/ppermute | solution.py:16
  77.8 4.5 %collective-permute-start.15 = (bf16[1024,128]{1,0:T(8,128)(2,1)S(1)}, bf16[1024,128]{1,0:T(8,128)(2,1)S(1)}, u32[]{:S(2)}, u32[]{:S(2)}) collective-permute-start(bf16[1024,128]{1,0:T(8,128)(2,1)S(1)} %collective-permute-done.11.refs_3_), channel_id=1, source_target_pairs={{0,1},{1,0},{2,3},{3,2},{4,5},{5,4},{6,7},{7,6},{8,9},{9,8},{10,11... | collective-permute-start | bytes 786440 | tf_op jit(solution)/shard_map/ppermute | solution.py:16
  78.3 4.0 %collective-permute-start.14 = (bf16[1024,128]{1,0:T(8,128)(2,1)S(1)}, bf16[1024,128]{1,0:T(8,128)(2,1)S(1)}, u32[]{:S(2)}, u32[]{:S(2)}) collective-permute-start(bf16[1024,128]{1,0:T(8,128)(2,1)S(1)} %collective-permute-done.10.refs_2_), channel_id=1, source_target_pairs={{0,1},{1,0},{2,3},{3,2},{4,5},{5,4},{6,7},{7,6},{8,9},{9,8},{10,11... | collective-permute-start | bytes 786440 | tf_op jit(solution)/shard_map/ppermute | solution.py:16
  79.8 17.1 %collective-permute-start.24 = (f32[136,256]{1,0:T(8,128)S(1)}, f32[136,256]{1,0:T(8,128)S(1)}, u32[]{:S(2)}, u32[]{:S(2)}) collective-permute-start(f32[136,256]{1,0:T(8,128)S(1)} %add_add_fusion.2), channel_id=1, source_target_pairs={{0,16},{16,0},{32,48},{48,32},{64,80},{80,64},{96,112},{112,96},{1... | collective-permute-start | bytes 417800 | tf_op jit(solution)/shard_map/ppermute | solution.py:16
  93.3 12.6 %collective-permute-start.17 = (bf16[1024,128]{1,0:T(8,128)(2,1)S(1)}, bf16[1024,128]{1,0:T(8,128)(2,1)S(1)}, u32[]{:S(2)}, u32[]{:S(2)}) collective-permute-start(bf16[1024,128]{1,0:T(8,128)(2,1)S(1)} %get-tuple-element.18), channel_id=1, source_target_pairs={{0,64},{16,80},{32,96},{48,112},{64,0},{80,16},{96,32},{112,48},{1... | collective-permute-start | bytes 786440 | tf_op jit(solution)/shard_map/ppermute | solution.py:16
  95.1 12.2 %collective-permute-start.19 = (bf16[1024,128]{1,0:T(8,128)(2,1)S(1)}, bf16[1024,128]{1,0:T(8,128)(2,1)S(1)}, u32[]{:S(2)}, u32[]{:S(2)}) collective-permute-start(bf16[1024,128]{1,0:T(8,128)(2,1)S(1)} %get-tuple-element.19), channel_id=1, source_target_pairs={{0,96},{16,112},{32,64},{48,80},{64,32},{80,48},{96,0},{112,16},{1... | collective-permute-start | bytes 786440 | tf_op jit(solution)/shard_map/ppermute | solution.py:16
  95.9 11.4 %collective-permute-start.18 = (bf16[1024,128]{1,0:T(8,128)(2,1)S(1)}, bf16[1024,128]{1,0:T(8,128)(2,1)S(1)}, u32[]{:S(2)}, u32[]{:S(2)}) collective-permute-start(bf16[1024,128]{1,0:T(8,128)(2,1)S(1)} %get-tuple-element.20), channel_id=1, source_target_pairs={{0,32},{16,48},{32,0},{48,16},{64,96},{80,112},{96,64},{112,80},{1... | collective-permute-start | bytes 786440 | tf_op jit(solution)/shard_map/ppermute | solution.py:16
  96.9 5.1 %collective-permute-start.25 = (f32[136,256]{1,0:T(8,128)S(1)}, f32[136,256]{1,0:T(8,128)S(1)}, u32[]{:S(2)}, u32[]{:S(2)}) collective-permute-start(f32[136,256]{1,0:T(8,128)S(1)} %add_add_fusion.1), channel_id=1, source_target_pairs={{0,2},{1,3},{2,0},{3,1},{4,6},{5,7},{6,4},{7,5},{8,10},{9,11},{10,... | collective-permute-start | bytes 417800 | tf_op jit(solution)/shard_map/ppermute | solution.py:16
  102.0 7.2 %collective-permute-start.28 = (f32[136,256]{1,0:T(8,128)S(1)}, f32[136,256]{1,0:T(8,128)S(1)}, u32[]{:S(2)}, u32[]{:S(2)}) collective-permute-start(f32[136,256]{1,0:T(8,128)S(1)} %add.141), channel_id=1, source_target_pairs={{0,12},{1,13},{2,14},{3,15},{4,8},{5,9},{6,10},{7,11},{8,4},{9,5},... | collective-permute-start | bytes 417800 | tf_op jit(solution)/shard_map/ppermute | solution.py:16
  104.9 6.6 %collective-permute-start.27 = (f32[136,256]{1,0:T(8,128)S(1)}, f32[136,256]{1,0:T(8,128)S(1)}, u32[]{:S(2)}, u32[]{:S(2)}) collective-permute-start(f32[136,256]{1,0:T(8,128)S(1)} %add.141), channel_id=1, source_target_pairs={{0,8},{1,9},{2,10},{3,11},{4,12},{5,13},{6,14},{7,15},{8,0},{9,1},... | collective-permute-start | bytes 417800 | tf_op jit(solution)/shard_map/ppermute | solution.py:16
  105.9 5.5 %collective-permute-start.26 = (f32[136,256]{1,0:T(8,128)S(1)}, f32[136,256]{1,0:T(8,128)S(1)}, u32[]{:S(2)}, u32[]{:S(2)}) collective-permute-start(f32[136,256]{1,0:T(8,128)S(1)} %add.141), channel_id=1, source_target_pairs={{0,4},{1,5},{2,6},{3,7},{4,0},{5,1},{6,2},{7,3},{8,12},{9,13},{10,... | collective-permute-start | bytes 417800 | tf_op jit(solution)/shard_map/ppermute | solution.py:16
  107.4 6.7 %collective-permute-start.20 = (bf16[512,128]{1,0:T(8,128)(2,1)S(1)}, bf16[512,128]{1,0:T(8,128)(2,1)S(1)}, u32[]{:S(2)}, u32[]{:S(2)}) collective-permute-start(bf16[512,128]{1,0:T(8,128)(2,1)S(1)} %slice.97), channel_id=1, source_target_pairs={{0,16},{16,0},{32,48},{48,32},{64,80},{80,64},{96,112},{112,96},{1... | collective-permute-start | bytes 393224 | tf_op jit(solution)/shard_map/ppermute | solution.py:16
  111.5 3.4 %collective-permute-start.29 = (f32[136,256]{1,0:T(8,128)S(1)}, f32[136,256]{1,0:T(8,128)S(1)}, u32[]{:S(2)}, u32[]{:S(2)}) collective-permute-start(f32[136,256]{1,0:T(8,128)S(1)} %add_add_fusion), channel_id=1, source_target_pairs={{0,1},{1,0},{2,3},{3,2},{4,5},{5,4},{6,7},{7,6},{8,9},{9,8},{10,11... | collective-permute-start | bytes 417800 | tf_op jit(solution)/shard_map/ppermute | solution.py:16

commit v4 on v3

--- a/solution.py
+++ b/solution.py
@@ -101,6 +101,31 @@
     )(table, pltpu.with_memory_space_constraint(values, pltpu.HBM), *pieces, *([] if ready is None else [ready]))
 
 
+def copy_kernel(array_ref, _, out_ref):
+    out_ref[...] = array_ref[...]
+
+
+def copy_after(array, event):
+    return pl.pallas_call(
+        copy_kernel,
+        out_shape=jax.ShapeDtypeStruct(array.shape, array.dtype),
+        in_specs=[pl.BlockSpec(memory_space=pltpu.VMEM), pl.BlockSpec(memory_space=pl.ANY)],
+        out_specs=pl.BlockSpec(memory_space=pltpu.VMEM),
+        compiler_params=pltpu.CompilerParams(vmem_limit_bytes=8 * 2**20),
+    )(array, event)
+
+
+def finish_kernel(total_ref, away_ref, terms_ref, other_ref, feature_ref, weight_ref, bias_ref):
+    side = total_ref.shape[1]
+    for first in range(0, feature_ref.shape[0], side):
+        span = slice(first, first + side)
+        tile = total_ref[span] + away_ref[span].astype(FULL)
+        feature_ref[span] = tile.T.astype(feature_ref.dtype)
+    rows = weight_ref.shape[0]
+    weight_ref[...] = terms_ref[:rows] + other_ref[:rows]
+    bias_ref[...] = terms_ref[rows : rows + 1] + other_ref[rows : rows + 1]
+
+
 def after(array, event):
     return lax.optimization_barrier((array, event))[0]
 
@@ -123,7 +148,7 @@
 
     pair = jnp.concatenate([features, swap(features, "row", 1)], axis=0)
     pieces = [pair] + [swap(pair, "row", d) for d in (2, 4, 6)]
-    up_away = swap(upstream, "col", 2)
+    up_away = swap(copy_after(upstream, pair), "col", 2)
     half_tiles = lax.axis_size("col") // 2 * per
     keep, send = tile_sums(
         values, pieces, col_place, row_place, count, [(half_tiles, FULL), (half_tiles, HALF)], False, ready=up_away
@@ -163,12 +188,21 @@
         total = total + other.astype(FULL)
     terms = (terms + zero) + other_terms[0]
     terms = terms + swap(terms, "col", 2)
-    terms = (terms + swap(terms, "col", 4)) + (swap(terms, "col", 8) + swap(terms, "col", 12))
-    terms = terms + swap(terms, "col", 1)
+    terms = terms + swap(terms, "col", 4)
+    terms = terms + swap(terms, "col", 8)
     away = swap(total[nodes:].astype(HALF), "row", 1)
-    total = total[:nodes] + away.astype(FULL)
-    feature_grad = jnp.swapaxes(total.reshape(per, width, side), 1, 2).astype(HALF).reshape(nodes, width)
-    return (activated, feature_grad, terms[:width], terms[width])
+    feature_grad, weight_grad, bias_grad = pl.pallas_call(
+        finish_kernel,
+        out_shape=[
+            jax.ShapeDtypeStruct((nodes, width), HALF),
+            jax.ShapeDtypeStruct((width, hidden), FULL),
+            jax.ShapeDtypeStruct((1, hidden), FULL),
+        ],
+        in_specs=[pl.BlockSpec(memory_space=pltpu.VMEM)] * 4,
+        out_specs=[pl.BlockSpec(memory_space=pltpu.VMEM)] * 3,
+        compiler_params=pltpu.CompilerParams(vmem_limit_bytes=8 * 2**20),
+    )(total, away, terms, swap(terms, "col", 1))
+    return (activated, feature_grad, weight_grad, bias_grad.reshape(hidden))
 
 
 def solution(mesh):

time: 117 us -> 116 us (level)
    slice x2 -> x0, local copies, waits for them, and re-layouts: 1.23 us -> none  [shards(): return (activated, feature_grad, terms[:width], terms[width])]
    ppermute x30 -> x29, waiting for transfers between devices: 51.5 us -> 52.5 us  [swap(): return lax.ppermute(array, axis, [(j, j ^ distance) for j in range(size)])]
    ppermute x30 -> x29, starting transfers between devices: 33.2 us -> 32.6 us  [swap(): return lax.ppermute(array, axis, [(j, j ^ distance) for j in range(size)])]
  transfers between devices with their start and end apart: 30 -> 29, of which waited for: 18 -> 17; matrix products, arithmetic and copies ran while one was open for 4% -> 3% of each run, Pallas kernels for 9% -> 9%
where the time goes in v4:
time: 116 us
  waiting for transfers between devices  52.5 us (45%)
  starting transfers between devices  32.6 us (28%)
  Pallas kernels  22.8 us (20%)
  other arithmetic  3.25 us (3%)
  local copies, waits for them, and re-layouts  2.08 us (2%)
  between operations  1.59 us (1%)
  matrix products  1.46 us (1%)
    ppermute x29, waiting for transfers between devices, swap(): return lax.ppermute(array, axis, [(j, j ^ distance) for j in range(size)])  52.5 us
    ppermute x29, starting transfers between devices, swap(): return lax.ppermute(array, axis, [(j, j ^ distance) for j in range(size)])  32.6 us
    pallas_call x2, Pallas kernels, tile_sums(): pl.pallas_call(functools.partial(tile_kernel, chunk, len(pieces), len(out...  22 us
  transfers between devices with their start and end apart: 29, of which 17 were waited for; matrix products, arithmetic and copies ran while one was open for 3% of the time, Pallas kernels for 9%

profile of v4, /device:TPU:0, one launch (start us, length us, event | category | flops | bytes accessed | tf_op | source)
XLA Modules:
  0.0 116.3 jit_solution(17828106210643784286)
XLA Ops:
  0.6 0.0 copy-start
  0.6 4.0 %collective-permute-start = (bf16[512,128]{1,0:T(8,128)(2,1)}, bf16[512,128]{1,0:T(8,128)(2,1)S(1)}, u32[]{:S(2)}, u32[]{:S(2)}) collective-permute-start(bf16[512,128]{1,0:T(8,128)(2,1)} %param.8), channel_id=1, source_target_pairs={{0,16},{16,0},{32,48},{48,32},{64,80},{80,64},{96,112},{112,96},{1... | collective-permute-start | bytes 393224 | tf_op jit(solution)/shard_map/ppermute | solution.py:16
  5.3 0.7 reduce
  6.0 0.7 reduce.1
  6.8 0.9 constant_dynamic-update-slice_fusion.1
  7.7 0.7 collective-permute-done
  8.4 2.8 %collective-permute-start.3 = (bf16[1024,128]{1,0:T(8,128)(2,1)S(1)}, bf16[1024,128]{1,0:T(8,128)(2,1)S(1)}, u32[]{:S(2)}, u32[]{:S(2)}) collective-permute-start(bf16[1024,128]{1,0:T(8,128)(2,1)S(1)} %constant_dynamic-update-slice_fusion._.refs_1_), channel_id=1, source_target_pairs={{0,96},{16,112},{32,64},{48,80},{64,32},{80,48},{96,0},{112,16},{1... | collective-permute-start | bytes 786440 | tf_op jit(solution)/shard_map/ppermute | solution.py:16
  11.3 0.8 collective-permute-start.2
  12.1 0.5 collective-permute-start.1
  12.6 0.9 copy-done.1
  13.6 1.4 %collective-permute-start.4 = (bf16[512,256]{1,0:T(8,128)(2,1)S(1)}, bf16[512,256]{1,0:T(8,128)(2,1)S(1)}, u32[]{:S(2)}, u32[]{:S(2)}) collective-permute-start(bf16[512,256]{1,0:T(8,128)(2,1)S(1)} %shard_map.111), channel_id=1, source_target_pairs={{0,2},{1,3},{2,0},{3,1},{4,6},{5,7},{6,4},{7,5},{8,10},{9,11},{10,... | collective-permute-start | bytes 786440 | tf_op jit(solution)/shard_map/ppermute | solution.py:16
  14.9 0.1 pad_add_fusion.1.table_any
  15.0 5.3 %collective-permute-done.4.refs_5_ = bf16[512,256]{1,0:T(8,128)(2,1)S(1)} collective-permute-done((bf16[512,256]{1,0:T(8,128)(2,1)S(1)}, bf16[512,256]{1,0:T(8,128)(2,1)S(1)}, u32[]{:S(2)}, u32[]{:S(2)}) %collective-permute-start.4) | collective-permute-done | bytes 262176 | tf_op jit(solution)/shard_map/ppermute | solution.py:16
  20.3 2.5 %collective-permute-done.3.refs_4_ = bf16[1024,128]{1,0:T(8,128)(2,1)S(1)} collective-permute-done((bf16[1024,128]{1,0:T(8,128)(2,1)S(1)}, bf16[1024,128]{1,0:T(8,128)(2,1)S(1)}, u32[]{:S(2)}, u32[]{:S(2)}) %collective-permute-start.3) | collective-permute-done | bytes 262176 | tf_op jit(solution)/shard_map/ppermute | solution.py:16
  22.8 0.6 collective-permute-done.1.refs_2_
  23.4 11.1 %shard_map.112 = (f32[4096,128]{1,0:T(8,128)S(1)}, bf16[4096,128]{1,0:T(8,128)(2,1)S(1)}) custom-call(s32[705]{0:T(1024)S(1)} %pad_add_fusion.1.table_any, bf16[704,128,128]{2,1,0:T(8,128)(2,1)} %bitcast.24, bf16[1024,128]{1,0:T(8,128)(2,1)S(1)} %constant_dynamic-update-slice_fusion._.refs_1_, bf16[1024,128]{1,0:T(8,128)(2,1)S(1)} %collective-permute-done.1.refs_2_, ...), custom_call_target="tpu_custom_call" | custom-call | flops 11811160064 | bytes 23068672 | tf_op jit(solution)/shard_map/pallas_call | solution.py:82
  34.5 0.1 collective-permute-start.5
  34.6 2.6 %collective-permute-done.5 = bf16[4096,128]{1,0:T(8,128)(2,1)S(1)} collective-permute-done((bf16[4096,128]{1,0:T(8,128)(2,1)S(1)}, bf16[4096,128]{1,0:T(8,128)(2,1)S(1)}, u32[]{:S(2)}, u32[]{:S(2)}) %collective-permute-start.5) | collective-permute-done | bytes 1048608 | tf_op jit(solution)/shard_map/ppermute | solution.py:16
  37.3 0.2 add_convert_fusion
  37.5 0.1 fusion.39
  37.5 0.0 copy-start.2
  37.6 0.0 copy-start.3
  37.6 0.8 collective-permute-start.6
  38.4 2.8 %collective-permute-start.7 = (bf16[1024,128]{1,0:T(8,128)(2,1)S(1)}, bf16[1024,128]{1,0:T(8,128)(2,1)S(1)}, u32[]{:S(2)}, u32[]{:S(2)}) collective-permute-start(bf16[1024,128]{1,0:T(8,128)(2,1)S(1)} %get-tuple-element.29), channel_id=1, source_target_pairs={{0,4},{1,5},{2,6},{3,7},{4,0},{5,1},{6,2},{7,3},{8,12},{9,13},{10,... | collective-permute-start | bytes 786440 | tf_op jit(solution)/shard_map/ppermute | solution.py:16
  41.1 7.2 %collective-permute-done.6 = bf16[1024,128]{1,0:T(8,128)(2,1)S(1)} collective-permute-done((bf16[1024,128]{1,0:T(8,128)(2,1)S(1)}, bf16[1024,128]{1,0:T(8,128)(2,1)S(1)}, u32[]{:S(2)}, u32[]{:S(2)}) %collective-permute-start.6) | collective-permute-done | bytes 262176 | tf_op jit(solution)/shard_map/ppermute | solution.py:16
  48.3 4.8 %collective-permute-done.8 = bf16[1024,128]{1,0:T(8,128)(2,1)S(1)} collective-permute-done((bf16[1024,128]{1,0:T(8,128)(2,1)S(1)}, bf16[1024,128]{1,0:T(8,128)(2,1)S(1)}, u32[]{:S(2)}, u32[]{:S(2)}) %collective-permute-start.8) | collective-permute-done | bytes 262176 | tf_op jit(solution)/shard_map/ppermute | solution.py:16
  53.1 0.1 add_convert_fusion.2
  53.3 0.6 collective-permute-start.9
  53.9 7.7 %collective-permute-done.9 = bf16[1024,128]{1,0:T(8,128)(2,1)S(1)} collective-permute-done((bf16[1024,128]{1,0:T(8,128)(2,1)S(1)}, bf16[1024,128]{1,0:T(8,128)(2,1)S(1)}, u32[]{:S(2)}, u32[]{:S(2)}) %collective-permute-start.9) | collective-permute-done | bytes 262176 | tf_op jit(solution)/shard_map/ppermute | solution.py:16
  61.6 0.1 add_convert_fusion.1
  61.8 0.9 fusion.2
  62.7 0.3 convolution_convert_fusion
  63.0 1.1 collective-permute-start.12
  64.1 0.1 collective-permute-start.11
  64.2 3.0 %collective-permute-start.10 = (bf16[1024,128]{1,0:T(8,128)(2,1)S(1)}, bf16[1024,128]{1,0:T(8,128)(2,1)S(1)}, u32[]{:S(2)}, u32[]{:S(2)}) collective-permute-start(bf16[1024,128]{1,0:T(8,128)(2,1)S(1)} %bitcast.20), channel_id=1, source_target_pairs={{0,4},{1,5},{2,6},{3,7},{4,0},{5,1},{6,2},{7,3},{8,12},{9,13},{10,... | collective-permute-start | bytes 786440 | tf_op jit(solution)/shard_map/ppermute | solution.py:16
  67.2 0.1 convert_reduce_fusion
  67.3 0.2 fusion.41
  67.5 3.1 %collective-permute-start.22 = (f32[136,256]{1,0:T(8,128)S(1)}, f32[136,256]{1,0:T(8,128)S(1)}, u32[]{:S(2)}, u32[]{:S(2)}) collective-permute-start(f32[136,256]{1,0:T(8,128)S(1)} %pad_maximum_fusion.1), channel_id=1, source_target_pairs={{0,64},{16,80},{32,96},{48,112},{64,0},{80,16},{96,32},{112,48},{1... | collective-permute-start | bytes 417800 | tf_op jit(solution)/shard_map/ppermute | solution.py:16
  70.6 3.8 %collective-permute-done.22 = f32[136,256]{1,0:T(8,128)S(1)} collective-permute-done((f32[136,256]{1,0:T(8,128)S(1)}, f32[136,256]{1,0:T(8,128)S(1)}, u32[]{:S(2)}, u32[]{:S(2)}) %collective-permute-start.22) | collective-permute-done | bytes 139296 | tf_op jit(solution)/shard_map/ppermute | solution.py:16
  74.4 2.5 %collective-permute-done.23 = f32[136,256]{1,0:T(8,128)S(1)} collective-permute-done((f32[136,256]{1,0:T(8,128)S(1)}, f32[136,256]{1,0:T(8,128)S(1)}, u32[]{:S(2)}, u32[]{:S(2)}) %collective-permute-start.23) | collective-permute-done | bytes 139296 | tf_op jit(solution)/shard_map/ppermute | solution.py:16
  76.9 0.4 collective-permute-done.12.refs_4_
  77.3 0.1 collective-permute-start.16
  77.4 0.4 collective-permute-start.15
  77.8 0.1 collective-permute-done.10.refs_2_
  77.9 0.1 pad_add_fusion.table_any
  78.0 1.4 %collective-permute-done.21 = f32[136,256]{1,0:T(8,128)S(1)} collective-permute-done((f32[136,256]{1,0:T(8,128)S(1)}, f32[136,256]{1,0:T(8,128)S(1)}, u32[]{:S(2)}, u32[]{:S(2)}) %collective-permute-start.21) | collective-permute-done | bytes 139296 | tf_op jit(solution)/shard_map/ppermute | solution.py:16
  79.5 2.8 %collective-permute-start.24 = (f32[136,256]{1,0:T(8,128)S(1)}, f32[136,256]{1,0:T(8,128)S(1)}, u32[]{:S(2)}, u32[]{:S(2)}) collective-permute-start(f32[136,256]{1,0:T(8,128)S(1)} %add_add_fusion.1), channel_id=1, source_target_pairs={{0,16},{16,0},{32,48},{48,32},{64,80},{80,64},{96,112},{112,96},{1... | collective-permute-start | bytes 417800 | tf_op jit(solution)/shard_map/ppermute | solution.py:16
  82.3 10.9 %shard_map.113 = (bf16[4096,128]{1,0:T(8,128)(2,1)S(1)}, f32[136,256]{1,0:T(8,128)S(1)}) custom-call(s32[705]{0:T(1024)S(1)} %pad_add_fusion.table_any, bf16[704,128,128]{2,1,0:T(8,128)(2,1)} %bitcast.25, bf16[1024,128]{1,0:T(8,128)(2,1)S(1)} %bitcast.22, bf16[1024,128]{1,0:T(8,128)(2,1)S(1)} %collective-permute-done.10.refs_2_, ...), custom_call_target="tpu_custom_call" | custom-call | flops 11811160064 | bytes 23068672 | tf_op jit(solution)/shard_map/pallas_call | solution.py:82
  93.3 0.1 collective-permute-start.25
  93.4 0.1 fusion.38
  93.4 0.1 collective-permute-start.17
  93.5 1.9 %collective-permute-start.19 = (bf16[1024,128]{1,0:T(8,128)(2,1)S(1)}, bf16[1024,128]{1,0:T(8,128)(2,1)S(1)}, u32[]{:S(2)}, u32[]{:S(2)}) collective-permute-start(bf16[1024,128]{1,0:T(8,128)(2,1)S(1)} %get-tuple-element.25), channel_id=1, source_target_pairs={{0,96},{16,112},{32,64},{48,80},{64,32},{80,48},{96,0},{112,16},{1... | collective-permute-start | bytes 786440 | tf_op jit(solution)/shard_map/ppermute | solution.py:16
  95.5 1.5 %collective-permute-start.18 = (bf16[1024,128]{1,0:T(8,128)(2,1)S(1)}, bf16[1024,128]{1,0:T(8,128)(2,1)S(1)}, u32[]{:S(2)}, u32[]{:S(2)}) collective-permute-start(bf16[1024,128]{1,0:T(8,128)(2,1)S(1)} %get-tuple-element.26), channel_id=1, source_target_pairs={{0,32},{16,48},{32,0},{48,16},{64,96},{80,112},{96,64},{112,80},{1... | collective-permute-start | bytes 786440 | tf_op jit(solution)/shard_map/ppermute | solution.py:16
  97.0 1.4 %collective-permute-done.25 = f32[136,256]{1,0:T(8,128)S(1)} collective-permute-done((f32[136,256]{1,0:T(8,128)S(1)}, f32[136,256]{1,0:T(8,128)S(1)}, u32[]{:S(2)}, u32[]{:S(2)}) %collective-permute-start.25) | collective-permute-done | bytes 139296 | tf_op jit(solution)/shard_map/ppermute | solution.py:16
  98.5 0.3 collective-permute-start.26
  98.8 4.8 %collective-permute-done.26 = f32[136,256]{1,0:T(8,128)S(1)} collective-permute-done((f32[136,256]{1,0:T(8,128)S(1)}, f32[136,256]{1,0:T(8,128)S(1)}, u32[]{:S(2)}, u32[]{:S(2)}) %collective-permute-start.26) | collective-permute-done | bytes 139296 | tf_op jit(solution)/shard_map/ppermute | solution.py:16
  103.6 1.8 %collective-permute-start.27 = (f32[136,256]{1,0:T(8,128)S(1)}, f32[136,256]{1,0:T(8,128)S(1)}, u32[]{:S(2)}, u32[]{:S(2)}) collective-permute-start(f32[136,256]{1,0:T(8,128)S(1)} %add.132), channel_id=1, source_target_pairs={{0,8},{1,9},{2,10},{3,11},{4,12},{5,13},{6,14},{7,15},{8,0},{9,1},... | collective-permute-start | bytes 417800 | tf_op jit(solution)/shard_map/ppermute | solution.py:16
  105.4 2.8 %collective-permute-done.19 = bf16[1024,128]{1,0:T(8,128)(2,1)S(1)} collective-permute-done((bf16[1024,128]{1,0:T(8,128)(2,1)S(1)}, bf16[1024,128]{1,0:T(8,128)(2,1)S(1)}, u32[]{:S(2)}, u32[]{:S(2)}) %collective-permute-start.19) | collective-permute-done | bytes 262176 | tf_op jit(solution)/shard_map/ppermute | solution.py:16
  108.2 0.1 convert_add_fusion.total_ref
  108.4 2.3 %collective-permute-start.20 = (bf16[512,128]{1,0:T(8,128)(2,1)S(1)}, bf16[512,128]{1,0:T(8,128)(2,1)S(1)}, u32[]{:S(2)}, u32[]{:S(2)}) collective-permute-start(bf16[512,128]{1,0:T(8,128)(2,1)S(1)} %slice.79), channel_id=1, source_target_pairs={{0,16},{16,0},{32,48},{48,32},{64,80},{80,64},{96,112},{112,96},{1... | collective-permute-start | bytes 393224 | tf_op jit(solution)/shard_map/ppermute | solution.py:16
  110.7 0.1 collective-permute-start.28
  110.8 0.9 fusion.17
  111.7 3.8 %collective-permute-done.20.away_ref = bf16[512,128]{1,0:T(8,128)(2,1)S(1)} collective-permute-done((bf16[512,128]{1,0:T(8,128)(2,1)S(1)}, bf16[512,128]{1,0:T(8,128)(2,1)S(1)}, u32[]{:S(2)}, u32[]{:S(2)}) %collective-permute-start.20) | collective-permute-done | bytes 131104 | tf_op jit(solution)/shard_map/ppermute | solution.py:16
  115.5 0.8 shard_map.114
  (37 shorter events, 0.4 us)
Async XLA Ops:
  0.6 61.1 %copy-start = (bf16[128,256]{1,0:T(8,128)(2,1)S(1)}, bf16[128,256]{1,0:T(8,128)(2,1)}, u32[]{:S(2)}) copy-start(bf16[128,256]{1,0:T(8,128)(2,1)} %param.9) | copy-start | bytes 196612
  0.6 7.7 %collective-permute-start = (bf16[512,128]{1,0:T(8,128)(2,1)}, bf16[512,128]{1,0:T(8,128)(2,1)S(1)}, u32[]{:S(2)}, u32[]{:S(2)}) collective-permute-start(bf16[512,128]{1,0:T(8,128)(2,1)} %param.8), channel_id=1, source_target_pairs={{0,16},{16,0},{32,48},{48,32},{64,80},{80,64},{96,112},{112,96},{1... | collective-permute-start | bytes 393224 | tf_op jit(solution)/shard_map/ppermute | solution.py:16
  8.4 14.4 %collective-permute-start.3 = (bf16[1024,128]{1,0:T(8,128)(2,1)S(1)}, bf16[1024,128]{1,0:T(8,128)(2,1)S(1)}, u32[]{:S(2)}, u32[]{:S(2)}) collective-permute-start(bf16[1024,128]{1,0:T(8,128)(2,1)S(1)} %constant_dynamic-update-slice_fusion._.refs_1_), channel_id=1, source_target_pairs={{0,96},{16,112},{32,64},{48,80},{64,32},{80,48},{96,0},{112,16},{1... | collective-permute-start | bytes 786440 | tf_op jit(solution)/shard_map/ppermute | solution.py:16
  11.3 11.6 %collective-permute-start.2 = (bf16[1024,128]{1,0:T(8,128)(2,1)S(1)}, bf16[1024,128]{1,0:T(8,128)(2,1)S(1)}, u32[]{:S(2)}, u32[]{:S(2)}) collective-permute-start(bf16[1024,128]{1,0:T(8,128)(2,1)S(1)} %constant_dynamic-update-slice_fusion._.refs_1_), channel_id=1, source_target_pairs={{0,64},{16,80},{32,96},{48,112},{64,0},{80,16},{96,32},{112,48},{1... | collective-permute-start | bytes 786440 | tf_op jit(solution)/shard_map/ppermute | solution.py:16
  12.1 11.4 %collective-permute-start.1 = (bf16[1024,128]{1,0:T(8,128)(2,1)S(1)}, bf16[1024,128]{1,0:T(8,128)(2,1)S(1)}, u32[]{:S(2)}, u32[]{:S(2)}) collective-permute-start(bf16[1024,128]{1,0:T(8,128)(2,1)S(1)} %constant_dynamic-update-slice_fusion._.refs_1_), channel_id=1, source_target_pairs={{0,32},{16,48},{32,0},{48,16},{64,96},{80,112},{96,64},{112,80},{1... | collective-permute-start | bytes 786440 | tf_op jit(solution)/shard_map/ppermute | solution.py:16
  12.6 0.9 copy-start.1
  13.6 6.7 %collective-permute-start.4 = (bf16[512,256]{1,0:T(8,128)(2,1)S(1)}, bf16[512,256]{1,0:T(8,128)(2,1)S(1)}, u32[]{:S(2)}, u32[]{:S(2)}) collective-permute-start(bf16[512,256]{1,0:T(8,128)(2,1)S(1)} %shard_map.111), channel_id=1, source_target_pairs={{0,2},{1,3},{2,0},{3,1},{4,6},{5,7},{6,4},{7,5},{8,10},{9,11},{10,... | collective-permute-start | bytes 786440 | tf_op jit(solution)/shard_map/ppermute | solution.py:16
  34.5 2.7 %collective-permute-start.5 = (bf16[4096,128]{1,0:T(8,128)(2,1)S(1)}, bf16[4096,128]{1,0:T(8,128)(2,1)S(1)}, u32[]{:S(2)}, u32[]{:S(2)}) collective-permute-start(bf16[4096,128]{1,0:T(8,128)(2,1)S(1)} %get-tuple-element.14), channel_id=1, source_target_pairs={{0,1},{1,0},{2,3},{3,2},{4,5},{5,4},{6,7},{7,6},{8,9},{9,8},{10,11... | collective-permute-start | bytes 3145736 | tf_op jit(solution)/shard_map/ppermute | solution.py:16
  37.5 24.2 %copy-start.2 = (bf16[512,256]{1,0:T(8,128)(2,1)S(1)}, bf16[512,256]{1,0:T(8,128)(2,1)}, u32[]{:S(2)}) copy-start(bf16[512,256]{1,0:T(8,128)(2,1)} %array_ref.1) | copy-start | bytes 786436
  37.6 24.2 %copy-start.3 = (f32[256]{0:T(256)S(1)}, f32[256]{0:T(256)}, u32[]{:S(2)}) copy-start(f32[256]{0:T(256)} %param.10) | copy-start | bytes 3076
  37.6 10.8 %collective-permute-start.6 = (bf16[1024,128]{1,0:T(8,128)(2,1)S(1)}, bf16[1024,128]{1,0:T(8,128)(2,1)S(1)}, u32[]{:S(2)}, u32[]{:S(2)}) collective-permute-start(bf16[1024,128]{1,0:T(8,128)(2,1)S(1)} %get-tuple-element.27), channel_id=1, source_target_pairs={{0,8},{1,9},{2,10},{3,11},{4,12},{5,13},{6,14},{7,15},{8,0},{9,1},... | collective-permute-start | bytes 786440 | tf_op jit(solution)/shard_map/ppermute | solution.py:16
  38.4 14.8 %collective-permute-start.8 = (bf16[1024,128]{1,0:T(8,128)(2,1)S(1)}, bf16[1024,128]{1,0:T(8,128)(2,1)S(1)}, u32[]{:S(2)}, u32[]{:S(2)}) collective-permute-start(bf16[1024,128]{1,0:T(8,128)(2,1)S(1)} %get-tuple-element.28), channel_id=1, source_target_pairs={{0,12},{1,13},{2,14},{3,15},{4,8},{5,9},{6,10},{7,11},{8,4},{9,5},... | collective-permute-start | bytes 786440 | tf_op jit(solution)/shard_map/ppermute | solution.py:16
  38.4 14.8 %collective-permute-start.7 = (bf16[1024,128]{1,0:T(8,128)(2,1)S(1)}, bf16[1024,128]{1,0:T(8,128)(2,1)S(1)}, u32[]{:S(2)}, u32[]{:S(2)}) collective-permute-start(bf16[1024,128]{1,0:T(8,128)(2,1)S(1)} %get-tuple-element.29), channel_id=1, source_target_pairs={{0,4},{1,5},{2,6},{3,7},{4,0},{5,1},{6,2},{7,3},{8,12},{9,13},{10,... | collective-permute-start | bytes 786440 | tf_op jit(solution)/shard_map/ppermute | solution.py:16
  53.3 8.3 %collective-permute-start.9 = (bf16[1024,128]{1,0:T(8,128)(2,1)S(1)}, bf16[1024,128]{1,0:T(8,128)(2,1)S(1)}, u32[]{:S(2)}, u32[]{:S(2)}) collective-permute-start(bf16[1024,128]{1,0:T(8,128)(2,1)S(1)} %pad_maximum_fusion), channel_id=1, source_target_pairs={{0,2},{1,3},{2,0},{3,1},{4,6},{5,7},{6,4},{7,5},{8,10},{9,11},{10,... | collective-permute-start | bytes 786440 | tf_op jit(solution)/shard_map/ppermute | solution.py:16
  63.0 14.3 %collective-permute-start.12 = (bf16[1024,128]{1,0:T(8,128)(2,1)S(1)}, bf16[1024,128]{1,0:T(8,128)(2,1)S(1)}, u32[]{:S(2)}, u32[]{:S(2)}) collective-permute-start(bf16[1024,128]{1,0:T(8,128)(2,1)S(1)} %bitcast.18), channel_id=1, source_target_pairs={{0,12},{1,13},{2,14},{3,15},{4,8},{5,9},{6,10},{7,11},{8,4},{9,5},... | collective-permute-start | bytes 786440 | tf_op jit(solution)/shard_map/ppermute | solution.py:16
  64.1 13.3 %collective-permute-start.11 = (bf16[1024,128]{1,0:T(8,128)(2,1)S(1)}, bf16[1024,128]{1,0:T(8,128)(2,1)S(1)}, u32[]{:S(2)}, u32[]{:S(2)}) collective-permute-start(bf16[1024,128]{1,0:T(8,128)(2,1)S(1)} %bitcast.19), channel_id=1, source_target_pairs={{0,8},{1,9},{2,10},{3,11},{4,12},{5,13},{6,14},{7,15},{8,0},{9,1},... | collective-permute-start | bytes 786440 | tf_op jit(solution)/shard_map/ppermute | solution.py:16
  64.2 13.7 %collective-permute-start.10 = (bf16[1024,128]{1,0:T(8,128)(2,1)S(1)}, bf16[1024,128]{1,0:T(8,128)(2,1)S(1)}, u32[]{:S(2)}, u32[]{:S(2)}) collective-permute-start(bf16[1024,128]{1,0:T(8,128)(2,1)S(1)} %bitcast.20), channel_id=1, source_target_pairs={{0,4},{1,5},{2,6},{3,7},{4,0},{5,1},{6,2},{7,3},{8,12},{9,13},{10,... | collective-permute-start | bytes 786440 | tf_op jit(solution)/shard_map/ppermute | solution.py:16
  67.5 6.9 %collective-permute-start.22 = (f32[136,256]{1,0:T(8,128)S(1)}, f32[136,256]{1,0:T(8,128)S(1)}, u32[]{:S(2)}, u32[]{:S(2)}) collective-permute-start(f32[136,256]{1,0:T(8,128)S(1)} %pad_maximum_fusion.1), channel_id=1, source_target_pairs={{0,64},{16,80},{32,96},{48,112},{64,0},{80,16},{96,32},{112,48},{1... | collective-permute-start | bytes 417800 | tf_op jit(solution)/shard_map/ppermute | solution.py:16
  70.6 6.3 %collective-permute-start.23 = (f32[136,256]{1,0:T(8,128)S(1)}, f32[136,256]{1,0:T(8,128)S(1)}, u32[]{:S(2)}, u32[]{:S(2)}) collective-permute-start(f32[136,256]{1,0:T(8,128)S(1)} %pad_maximum_fusion.1), channel_id=1, source_target_pairs={{0,96},{16,112},{32,64},{48,80},{64,32},{80,48},{96,0},{112,16},{1... | collective-permute-start | bytes 417800 | tf_op jit(solution)/shard_map/ppermute | solution.py:16
  74.4 5.1 %collective-permute-start.21 = (f32[136,256]{1,0:T(8,128)S(1)}, f32[136,256]{1,0:T(8,128)S(1)}, u32[]{:S(2)}, u32[]{:S(2)}) collective-permute-start(f32[136,256]{1,0:T(8,128)S(1)} %pad_maximum_fusion.1), channel_id=1, source_target_pairs={{0,32},{16,48},{32,0},{48,16},{64,96},{80,112},{96,64},{112,80},{1... | collective-permute-start | bytes 417800 | tf_op jit(solution)/shard_map/ppermute | solution.py:16
  76.9 5.4 %collective-permute-start.13 = (bf16[1024,128]{1,0:T(8,128)(2,1)S(1)}, bf16[1024,128]{1,0:T(8,128)(2,1)S(1)}, u32[]{:S(2)}, u32[]{:S(2)}) collective-permute-start(bf16[1024,128]{1,0:T(8,128)(2,1)S(1)} %bitcast.21), channel_id=1, source_target_pairs={{0,1},{1,0},{2,3},{3,2},{4,5},{5,4},{6,7},{7,6},{8,9},{9,8},{10,11... | collective-permute-start | bytes 786440 | tf_op jit(solution)/shard_map/ppermute | solution.py:16
  77.3 5.0 %collective-permute-start.16 = (bf16[1024,128]{1,0:T(8,128)(2,1)S(1)}, bf16[1024,128]{1,0:T(8,128)(2,1)S(1)}, u32[]{:S(2)}, u32[]{:S(2)}) collective-permute-start(bf16[1024,128]{1,0:T(8,128)(2,1)S(1)} %collective-permute-done.12.refs_4_), channel_id=1, source_target_pairs={{0,1},{1,0},{2,3},{3,2},{4,5},{5,4},{6,7},{7,6},{8,9},{9,8},{10,11... | collective-permute-start | bytes 786440 | tf_op jit(solution)/shard_map/ppermute | solution.py:16
  77.4 4.9 %collective-permute-start.15 = (bf16[1024,128]{1,0:T(8,128)(2,1)S(1)}, bf16[1024,128]{1,0:T(8,128)(2,1)S(1)}, u32[]{:S(2)}, u32[]{:S(2)}) collective-permute-start(bf16[1024,128]{1,0:T(8,128)(2,1)S(1)} %collective-permute-done.11.refs_3_), channel_id=1, source_target_pairs={{0,1},{1,0},{2,3},{3,2},{4,5},{5,4},{6,7},{7,6},{8,9},{9,8},{10,11... | collective-permute-start | bytes 786440 | tf_op jit(solution)/shard_map/ppermute | solution.py:16
  77.9 4.4 %collective-permute-start.14 = (bf16[1024,128]{1,0:T(8,128)(2,1)S(1)}, bf16[1024,128]{1,0:T(8,128)(2,1)S(1)}, u32[]{:S(2)}, u32[]{:S(2)}) collective-permute-start(bf16[1024,128]{1,0:T(8,128)(2,1)S(1)} %collective-permute-done.10.refs_2_), channel_id=1, source_target_pairs={{0,1},{1,0},{2,3},{3,2},{4,5},{5,4},{6,7},{7,6},{8,9},{9,8},{10,11... | collective-permute-start | bytes 786440 | tf_op jit(solution)/shard_map/ppermute | solution.py:16
  79.5 13.8 %collective-permute-start.24 = (f32[136,256]{1,0:T(8,128)S(1)}, f32[136,256]{1,0:T(8,128)S(1)}, u32[]{:S(2)}, u32[]{:S(2)}) collective-permute-start(f32[136,256]{1,0:T(8,128)S(1)} %add_add_fusion.1), channel_id=1, source_target_pairs={{0,16},{16,0},{32,48},{48,32},{64,80},{80,64},{96,112},{112,96},{1... | collective-permute-start | bytes 417800 | tf_op jit(solution)/shard_map/ppermute | solution.py:16
  93.3 5.1 %collective-permute-start.25 = (f32[136,256]{1,0:T(8,128)S(1)}, f32[136,256]{1,0:T(8,128)S(1)}, u32[]{:S(2)}, u32[]{:S(2)}) collective-permute-start(f32[136,256]{1,0:T(8,128)S(1)} %add_add_fusion), channel_id=1, source_target_pairs={{0,2},{1,3},{2,0},{3,1},{4,6},{5,7},{6,4},{7,5},{8,10},{9,11},{10,... | collective-permute-start | bytes 417800 | tf_op jit(solution)/shard_map/ppermute | solution.py:16
  93.4 12.0 %collective-permute-start.17 = (bf16[1024,128]{1,0:T(8,128)(2,1)S(1)}, bf16[1024,128]{1,0:T(8,128)(2,1)S(1)}, u32[]{:S(2)}, u32[]{:S(2)}) collective-permute-start(bf16[1024,128]{1,0:T(8,128)(2,1)S(1)} %get-tuple-element.24), channel_id=1, source_target_pairs={{0,64},{16,80},{32,96},{48,112},{64,0},{80,16},{96,32},{112,48},{1... | collective-permute-start | bytes 786440 | tf_op jit(solution)/shard_map/ppermute | solution.py:16
  93.5 14.7 %collective-permute-start.19 = (bf16[1024,128]{1,0:T(8,128)(2,1)S(1)}, bf16[1024,128]{1,0:T(8,128)(2,1)S(1)}, u32[]{:S(2)}, u32[]{:S(2)}) collective-permute-start(bf16[1024,128]{1,0:T(8,128)(2,1)S(1)} %get-tuple-element.25), channel_id=1, source_target_pairs={{0,96},{16,112},{32,64},{48,80},{64,32},{80,48},{96,0},{112,16},{1... | collective-permute-start | bytes 786440 | tf_op jit(solution)/shard_map/ppermute | solution.py:16
  95.5 12.7 %collective-permute-start.18 = (bf16[1024,128]{1,0:T(8,128)(2,1)S(1)}, bf16[1024,128]{1,0:T(8,128)(2,1)S(1)}, u32[]{:S(2)}, u32[]{:S(2)}) collective-permute-start(bf16[1024,128]{1,0:T(8,128)(2,1)S(1)} %get-tuple-element.26), channel_id=1, source_target_pairs={{0,32},{16,48},{32,0},{48,16},{64,96},{80,112},{96,64},{112,80},{1... | collective-permute-start | bytes 786440 | tf_op jit(solution)/shard_map/ppermute | solution.py:16
  98.5 5.1 %collective-permute-start.26 = (f32[136,256]{1,0:T(8,128)S(1)}, f32[136,256]{1,0:T(8,128)S(1)}, u32[]{:S(2)}, u32[]{:S(2)}) collective-permute-start(f32[136,256]{1,0:T(8,128)S(1)} %add.131), channel_id=1, source_target_pairs={{0,4},{1,5},{2,6},{3,7},{4,0},{5,1},{6,2},{7,3},{8,12},{9,13},{10,... | collective-permute-start | bytes 417800 | tf_op jit(solution)/shard_map/ppermute | solution.py:16
  103.6 7.1 %collective-permute-start.27 = (f32[136,256]{1,0:T(8,128)S(1)}, f32[136,256]{1,0:T(8,128)S(1)}, u32[]{:S(2)}, u32[]{:S(2)}) collective-permute-start(f32[136,256]{1,0:T(8,128)S(1)} %add.132), channel_id=1, source_target_pairs={{0,8},{1,9},{2,10},{3,11},{4,12},{5,13},{6,14},{7,15},{8,0},{9,1},... | collective-permute-start | bytes 417800 | tf_op jit(solution)/shard_map/ppermute | solution.py:16
  108.4 7.1 %collective-permute-start.20 = (bf16[512,128]{1,0:T(8,128)(2,1)S(1)}, bf16[512,128]{1,0:T(8,128)(2,1)S(1)}, u32[]{:S(2)}, u32[]{:S(2)}) collective-permute-start(bf16[512,128]{1,0:T(8,128)(2,1)S(1)} %slice.79), channel_id=1, source_target_pairs={{0,16},{16,0},{32,48},{48,32},{64,80},{80,64},{96,112},{112,96},{1... | collective-permute-start | bytes 393224 | tf_op jit(solution)/shard_map/ppermute | solution.py:16
  110.7 4.8 %collective-permute-start.28 = (f32[136,256]{1,0:T(8,128)S(1)}, f32[136,256]{1,0:T(8,128)S(1)}, u32[]{:S(2)}, u32[]{:S(2)}) collective-permute-start(f32[136,256]{1,0:T(8,128)S(1)} %add.133.terms_ref), channel_id=1, source_target_pairs={{0,1},{1,0},{2,3},{3,2},{4,5},{5,4},{6,7},{7,6},{8,9},{9,8},{10,11... | collective-permute-start | bytes 417800 | tf_op jit(solution)/shard_map/ppermute | solution.py:16

commit v5 on v4

--- a/solution.py
+++ b/solution.py
@@ -72,7 +72,7 @@
 
 def tile_sums(values, pieces, source_index, target_index, count, out_types, flip, zero_shape=None, ready=None):
     slots, side, _ = values.shape
-    chunk = max(d for d in range(1, 65) if slots % d == 0)
+    chunk = max(d for d in range(1, 89) if slots % d == 0)
     num_source = sum(piece.shape[0] for piece in pieces) // side
     num_out = sum(n for n, _ in out_types)
     width = pieces[0].shape[1]

time: 116 us -> 115 us (level)
  waiting for transfers between devices: 52.5 us -> 48.6 us
  starting transfers between devices: 32.6 us -> 35.5 us
    ppermute x29, waiting for transfers between devices: 52.5 us -> 48.6 us  [swap(): return lax.ppermute(array, axis, [(j, j ^ distance) for j in range(size)])]
    ppermute x29, starting transfers between devices: 32.6 us -> 35.5 us  [swap(): return lax.ppermute(array, axis, [(j, j ^ distance) for j in range(size)])]
where the time goes in v5:
time: 115 us
  waiting for transfers between devices  48.6 us (42%)
  starting transfers between devices  35.5 us (31%)
  Pallas kernels  22.4 us (19%)
  other arithmetic  3.25 us (3%)
  local copies, waits for them, and re-layouts  2.08 us (2%)
  between operations  1.59 us (1%)
  matrix products  1.47 us (1%)
    ppermute x29, waiting for transfers between devices, swap(): return lax.ppermute(array, axis, [(j, j ^ distance) for j in range(size)])  48.6 us
    ppermute x29, starting transfers between devices, swap(): return lax.ppermute(array, axis, [(j, j ^ distance) for j in range(size)])  35.5 us
    pallas_call x2, Pallas kernels, tile_sums(): pl.pallas_call(functools.partial(tile_kernel, chunk, len(pieces), len(out...  21.7 us
  transfers between devices with their start and end apart: 29, of which 17 were waited for; matrix products, arithmetic and copies ran while one was open for 3% of the time, Pallas kernels for 9%

profile of v5, /device:TPU:0, one launch (start us, length us, event | category | flops | bytes accessed | tf_op | source)
XLA Modules:
  0.0 114.8 jit_solution(1966024016588236039)
XLA Ops:
  0.6 0.0 copy-start
  0.6 4.0 %collective-permute-start = (bf16[512,128]{1,0:T(8,128)(2,1)}, bf16[512,128]{1,0:T(8,128)(2,1)S(1)}, u32[]{:S(2)}, u32[]{:S(2)}) collective-permute-start(bf16[512,128]{1,0:T(8,128)(2,1)} %param.8), channel_id=1, source_target_pairs={{0,16},{16,0},{32,48},{48,32},{64,80},{80,64},{96,112},{112,96},{1... | collective-permute-start | bytes 393224 | tf_op jit(solution)/shard_map/ppermute | solution.py:16
  5.3 0.7 reduce
  6.0 0.7 reduce.1
  6.8 0.9 constant_dynamic-update-slice_fusion.1
  7.7 0.7 collective-permute-done
  8.4 2.8 %collective-permute-start.3 = (bf16[1024,128]{1,0:T(8,128)(2,1)S(1)}, bf16[1024,128]{1,0:T(8,128)(2,1)S(1)}, u32[]{:S(2)}, u32[]{:S(2)}) collective-permute-start(bf16[1024,128]{1,0:T(8,128)(2,1)S(1)} %constant_dynamic-update-slice_fusion._.refs_1_), channel_id=1, source_target_pairs={{0,96},{16,112},{32,64},{48,80},{64,32},{80,48},{96,0},{112,16},{1... | collective-permute-start | bytes 786440 | tf_op jit(solution)/shard_map/ppermute | solution.py:16
  11.3 0.8 collective-permute-start.2
  12.1 0.5 collective-permute-start.1
  12.6 0.9 copy-done.1
  13.6 1.4 %collective-permute-start.4 = (bf16[512,256]{1,0:T(8,128)(2,1)S(1)}, bf16[512,256]{1,0:T(8,128)(2,1)S(1)}, u32[]{:S(2)}, u32[]{:S(2)}) collective-permute-start(bf16[512,256]{1,0:T(8,128)(2,1)S(1)} %shard_map.111), channel_id=1, source_target_pairs={{0,2},{1,3},{2,0},{3,1},{4,6},{5,7},{6,4},{7,5},{8,10},{9,11},{10,... | collective-permute-start | bytes 786440 | tf_op jit(solution)/shard_map/ppermute | solution.py:16
  14.9 0.1 pad_add_fusion.1.table_any
  15.0 5.3 %collective-permute-done.4.refs_5_ = bf16[512,256]{1,0:T(8,128)(2,1)S(1)} collective-permute-done((bf16[512,256]{1,0:T(8,128)(2,1)S(1)}, bf16[512,256]{1,0:T(8,128)(2,1)S(1)}, u32[]{:S(2)}, u32[]{:S(2)}) %collective-permute-start.4) | collective-permute-done | bytes 262176 | tf_op jit(solution)/shard_map/ppermute | solution.py:16
  20.3 2.5 %collective-permute-done.3.refs_4_ = bf16[1024,128]{1,0:T(8,128)(2,1)S(1)} collective-permute-done((bf16[1024,128]{1,0:T(8,128)(2,1)S(1)}, bf16[1024,128]{1,0:T(8,128)(2,1)S(1)}, u32[]{:S(2)}, u32[]{:S(2)}) %collective-permute-start.3) | collective-permute-done | bytes 262176 | tf_op jit(solution)/shard_map/ppermute | solution.py:16
  22.8 0.6 collective-permute-done.1.refs_2_
  23.4 10.9 %shard_map.112 = (f32[4096,128]{1,0:T(8,128)S(1)}, bf16[4096,128]{1,0:T(8,128)(2,1)S(1)}) custom-call(s32[705]{0:T(1024)S(1)} %pad_add_fusion.1.table_any, bf16[704,128,128]{2,1,0:T(8,128)(2,1)} %bitcast.25, bf16[1024,128]{1,0:T(8,128)(2,1)S(1)} %constant_dynamic-update-slice_fusion._.refs_1_, bf16[1024,128]{1,0:T(8,128)(2,1)S(1)} %collective-permute-done.1.refs_2_, ...), custom_call_target="tpu_custom_call" | custom-call | flops 11811160064 | bytes 23068672 | tf_op jit(solution)/shard_map/pallas_call | solution.py:82
  34.4 0.1 collective-permute-start.5
  34.4 2.6 %collective-permute-done.5 = bf16[4096,128]{1,0:T(8,128)(2,1)S(1)} collective-permute-done((bf16[4096,128]{1,0:T(8,128)(2,1)S(1)}, bf16[4096,128]{1,0:T(8,128)(2,1)S(1)}, u32[]{:S(2)}, u32[]{:S(2)}) %collective-permute-start.5) | collective-permute-done | bytes 1048608 | tf_op jit(solution)/shard_map/ppermute | solution.py:16
  37.1 0.2 add_convert_fusion
  37.3 0.1 fusion.39
  37.4 3.3 %collective-permute-start.6 = (bf16[1024,128]{1,0:T(8,128)(2,1)S(1)}, bf16[1024,128]{1,0:T(8,128)(2,1)S(1)}, u32[]{:S(2)}, u32[]{:S(2)}) collective-permute-start(bf16[1024,128]{1,0:T(8,128)(2,1)S(1)} %get-tuple-element.27), channel_id=1, source_target_pairs={{0,8},{1,9},{2,10},{3,11},{4,12},{5,13},{6,14},{7,15},{8,0},{9,1},... | collective-permute-start | bytes 786440 | tf_op jit(solution)/shard_map/ppermute | solution.py:16
  40.7 0.3 collective-permute-start.7
  41.0 7.2 %collective-permute-done.6 = bf16[1024,128]{1,0:T(8,128)(2,1)S(1)} collective-permute-done((bf16[1024,128]{1,0:T(8,128)(2,1)S(1)}, bf16[1024,128]{1,0:T(8,128)(2,1)S(1)}, u32[]{:S(2)}, u32[]{:S(2)}) %collective-permute-start.6) | collective-permute-done | bytes 262176 | tf_op jit(solution)/shard_map/ppermute | solution.py:16
  48.2 4.8 %collective-permute-done.8 = bf16[1024,128]{1,0:T(8,128)(2,1)S(1)} collective-permute-done((bf16[1024,128]{1,0:T(8,128)(2,1)S(1)}, bf16[1024,128]{1,0:T(8,128)(2,1)S(1)}, u32[]{:S(2)}, u32[]{:S(2)}) %collective-permute-start.8) | collective-permute-done | bytes 262176 | tf_op jit(solution)/shard_map/ppermute | solution.py:16
  52.9 0.1 add_convert_fusion.2
  53.1 0.3 collective-permute-start.9
  53.5 8.0 %collective-permute-done.9 = bf16[1024,128]{1,0:T(8,128)(2,1)S(1)} collective-permute-done((bf16[1024,128]{1,0:T(8,128)(2,1)S(1)}, bf16[1024,128]{1,0:T(8,128)(2,1)S(1)}, u32[]{:S(2)}, u32[]{:S(2)}) %collective-permute-start.9) | collective-permute-done | bytes 262176 | tf_op jit(solution)/shard_map/ppermute | solution.py:16
  61.4 0.1 add_convert_fusion.1
  61.6 0.9 fusion.2
  62.5 0.3 convolution_convert_fusion
  62.9 1.0 collective-permute-start.12
  63.9 2.2 %collective-permute-start.11 = (bf16[1024,128]{1,0:T(8,128)(2,1)S(1)}, bf16[1024,128]{1,0:T(8,128)(2,1)S(1)}, u32[]{:S(2)}, u32[]{:S(2)}) collective-permute-start(bf16[1024,128]{1,0:T(8,128)(2,1)S(1)} %bitcast.20), channel_id=1, source_target_pairs={{0,8},{1,9},{2,10},{3,11},{4,12},{5,13},{6,14},{7,15},{8,0},{9,1},... | collective-permute-start | bytes 786440 | tf_op jit(solution)/shard_map/ppermute | solution.py:16
  66.0 1.0 collective-permute-start.10
  67.0 0.1 convert_reduce_fusion
  67.1 0.2 fusion.41
  67.4 3.1 %collective-permute-start.22 = (f32[136,256]{1,0:T(8,128)S(1)}, f32[136,256]{1,0:T(8,128)S(1)}, u32[]{:S(2)}, u32[]{:S(2)}) collective-permute-start(f32[136,256]{1,0:T(8,128)S(1)} %pad_maximum_fusion.1), channel_id=1, source_target_pairs={{0,64},{16,80},{32,96},{48,112},{64,0},{80,16},{96,32},{112,48},{1... | collective-permute-start | bytes 417800 | tf_op jit(solution)/shard_map/ppermute | solution.py:16
  70.4 0.1 collective-permute-start.23
  70.5 3.6 %collective-permute-done.22 = f32[136,256]{1,0:T(8,128)S(1)} collective-permute-done((f32[136,256]{1,0:T(8,128)S(1)}, f32[136,256]{1,0:T(8,128)S(1)}, u32[]{:S(2)}, u32[]{:S(2)}) %collective-permute-start.22) | collective-permute-done | bytes 139296 | tf_op jit(solution)/shard_map/ppermute | solution.py:16
  74.1 0.4 collective-permute-start.21
  74.5 2.2 %collective-permute-done.23 = f32[136,256]{1,0:T(8,128)S(1)} collective-permute-done((f32[136,256]{1,0:T(8,128)S(1)}, f32[136,256]{1,0:T(8,128)S(1)}, u32[]{:S(2)}, u32[]{:S(2)}) %collective-permute-start.23) | collective-permute-done | bytes 139296 | tf_op jit(solution)/shard_map/ppermute | solution.py:16
  76.8 0.4 collective-permute-done.12.refs_4_
  77.1 0.1 collective-permute-start.16
  77.3 0.4 collective-permute-start.15
  77.7 0.1 collective-permute-done.10.refs_2_
  77.8 0.0 collective-permute-start.14
  77.8 0.1 pad_add_fusion.table_any
  77.9 1.3 %collective-permute-done.21 = f32[136,256]{1,0:T(8,128)S(1)} collective-permute-done((f32[136,256]{1,0:T(8,128)S(1)}, f32[136,256]{1,0:T(8,128)S(1)}, u32[]{:S(2)}, u32[]{:S(2)}) %collective-permute-start.21) | collective-permute-done | bytes 139296 | tf_op jit(solution)/shard_map/ppermute | solution.py:16
  79.2 2.5 %collective-permute-start.24 = (f32[136,256]{1,0:T(8,128)S(1)}, f32[136,256]{1,0:T(8,128)S(1)}, u32[]{:S(2)}, u32[]{:S(2)}) collective-permute-start(f32[136,256]{1,0:T(8,128)S(1)} %add_add_fusion.1), channel_id=1, source_target_pairs={{0,16},{16,0},{32,48},{48,32},{64,80},{80,64},{96,112},{112,96},{1... | collective-permute-start | bytes 417800 | tf_op jit(solution)/shard_map/ppermute | solution.py:16
  81.7 10.8 %shard_map.113 = (bf16[4096,128]{1,0:T(8,128)(2,1)S(1)}, f32[136,256]{1,0:T(8,128)S(1)}) custom-call(s32[705]{0:T(1024)S(1)} %pad_add_fusion.table_any, bf16[704,128,128]{2,1,0:T(8,128)(2,1)} %bitcast.26, bf16[1024,128]{1,0:T(8,128)(2,1)S(1)} %bitcast.23, bf16[1024,128]{1,0:T(8,128)(2,1)S(1)} %collective-permute-done.10.refs_2_, ...), custom_call_target="tpu_custom_call" | custom-call | flops 11811160064 | bytes 23068672 | tf_op jit(solution)/shard_map/pallas_call | solution.py:82
  92.5 0.1 collective-permute-start.25
  92.6 0.1 fusion.38
  92.7 2.6 %collective-permute-start.17 = (bf16[1024,128]{1,0:T(8,128)(2,1)S(1)}, bf16[1024,128]{1,0:T(8,128)(2,1)S(1)}, u32[]{:S(2)}, u32[]{:S(2)}) collective-permute-start(bf16[1024,128]{1,0:T(8,128)(2,1)S(1)} %get-tuple-element.24), channel_id=1, source_target_pairs={{0,64},{16,80},{32,96},{48,112},{64,0},{80,16},{96,32},{112,48},{1... | collective-permute-start | bytes 786440 | tf_op jit(solution)/shard_map/ppermute | solution.py:16
  95.3 1.9 %collective-permute-start.19 = (bf16[1024,128]{1,0:T(8,128)(2,1)S(1)}, bf16[1024,128]{1,0:T(8,128)(2,1)S(1)}, u32[]{:S(2)}, u32[]{:S(2)}) collective-permute-start(bf16[1024,128]{1,0:T(8,128)(2,1)S(1)} %get-tuple-element.25), channel_id=1, source_target_pairs={{0,96},{16,112},{32,64},{48,80},{64,32},{80,48},{96,0},{112,16},{1... | collective-permute-start | bytes 786440 | tf_op jit(solution)/shard_map/ppermute | solution.py:16
  97.2 0.5 collective-permute-done.25
  97.7 0.1 collective-permute-start.26
  97.8 5.0 %collective-permute-done.26 = f32[136,256]{1,0:T(8,128)S(1)} collective-permute-done((f32[136,256]{1,0:T(8,128)S(1)}, f32[136,256]{1,0:T(8,128)S(1)}, u32[]{:S(2)}, u32[]{:S(2)}) %collective-permute-start.26) | collective-permute-done | bytes 139296 | tf_op jit(solution)/shard_map/ppermute | solution.py:16
  102.8 3.2 %collective-permute-start.27 = (f32[136,256]{1,0:T(8,128)S(1)}, f32[136,256]{1,0:T(8,128)S(1)}, u32[]{:S(2)}, u32[]{:S(2)}) collective-permute-start(f32[136,256]{1,0:T(8,128)S(1)} %add.132), channel_id=1, source_target_pairs={{0,8},{1,9},{2,10},{3,11},{4,12},{5,13},{6,14},{7,15},{8,0},{9,1},... | collective-permute-start | bytes 417800 | tf_op jit(solution)/shard_map/ppermute | solution.py:16
  106.0 1.0 collective-permute-done.19
  107.1 0.1 convert_add_fusion.total_ref
  107.2 3.1 %collective-permute-start.20 = (bf16[512,128]{1,0:T(8,128)(2,1)S(1)}, bf16[512,128]{1,0:T(8,128)(2,1)S(1)}, u32[]{:S(2)}, u32[]{:S(2)}) collective-permute-start(bf16[512,128]{1,0:T(8,128)(2,1)S(1)} %slice.79), channel_id=1, source_target_pairs={{0,16},{16,0},{32,48},{48,32},{64,80},{80,64},{96,112},{112,96},{1... | collective-permute-start | bytes 393224 | tf_op jit(solution)/shard_map/ppermute | solution.py:16
  110.4 0.1 collective-permute-start.28
  110.5 0.9 fusion.17
  111.3 2.7 %collective-permute-done.20.away_ref = bf16[512,128]{1,0:T(8,128)(2,1)S(1)} collective-permute-done((bf16[512,128]{1,0:T(8,128)(2,1)S(1)}, bf16[512,128]{1,0:T(8,128)(2,1)S(1)}, u32[]{:S(2)}, u32[]{:S(2)}) %collective-permute-start.20) | collective-permute-done | bytes 131104 | tf_op jit(solution)/shard_map/ppermute | solution.py:16
  114.1 0.8 shard_map.114
  (37 shorter events, 0.4 us)
Async XLA Ops:
  0.6 60.9 %copy-start = (bf16[128,256]{1,0:T(8,128)(2,1)S(1)}, bf16[128,256]{1,0:T(8,128)(2,1)}, u32[]{:S(2)}) copy-start(bf16[128,256]{1,0:T(8,128)(2,1)} %param.9) | copy-start | bytes 196612
  0.6 7.7 %collective-permute-start = (bf16[512,128]{1,0:T(8,128)(2,1)}, bf16[512,128]{1,0:T(8,128)(2,1)S(1)}, u32[]{:S(2)}, u32[]{:S(2)}) collective-permute-start(bf16[512,128]{1,0:T(8,128)(2,1)} %param.8), channel_id=1, source_target_pairs={{0,16},{16,0},{32,48},{48,32},{64,80},{80,64},{96,112},{112,96},{1... | collective-permute-start | bytes 393224 | tf_op jit(solution)/shard_map/ppermute | solution.py:16
  8.4 14.4 %collective-permute-start.3 = (bf16[1024,128]{1,0:T(8,128)(2,1)S(1)}, bf16[1024,128]{1,0:T(8,128)(2,1)S(1)}, u32[]{:S(2)}, u32[]{:S(2)}) collective-permute-start(bf16[1024,128]{1,0:T(8,128)(2,1)S(1)} %constant_dynamic-update-slice_fusion._.refs_1_), channel_id=1, source_target_pairs={{0,96},{16,112},{32,64},{48,80},{64,32},{80,48},{96,0},{112,16},{1... | collective-permute-start | bytes 786440 | tf_op jit(solution)/shard_map/ppermute | solution.py:16
  11.3 11.6 %collective-permute-start.2 = (bf16[1024,128]{1,0:T(8,128)(2,1)S(1)}, bf16[1024,128]{1,0:T(8,128)(2,1)S(1)}, u32[]{:S(2)}, u32[]{:S(2)}) collective-permute-start(bf16[1024,128]{1,0:T(8,128)(2,1)S(1)} %constant_dynamic-update-slice_fusion._.refs_1_), channel_id=1, source_target_pairs={{0,64},{16,80},{32,96},{48,112},{64,0},{80,16},{96,32},{112,48},{1... | collective-permute-start | bytes 786440 | tf_op jit(solution)/shard_map/ppermute | solution.py:16
  12.1 11.4 %collective-permute-start.1 = (bf16[1024,128]{1,0:T(8,128)(2,1)S(1)}, bf16[1024,128]{1,0:T(8,128)(2,1)S(1)}, u32[]{:S(2)}, u32[]{:S(2)}) collective-permute-start(bf16[1024,128]{1,0:T(8,128)(2,1)S(1)} %constant_dynamic-update-slice_fusion._.refs_1_), channel_id=1, source_target_pairs={{0,32},{16,48},{32,0},{48,16},{64,96},{80,112},{96,64},{112,80},{1... | collective-permute-start | bytes 786440 | tf_op jit(solution)/shard_map/ppermute | solution.py:16
  12.6 0.9 copy-start.1
  13.6 6.7 %collective-permute-start.4 = (bf16[512,256]{1,0:T(8,128)(2,1)S(1)}, bf16[512,256]{1,0:T(8,128)(2,1)S(1)}, u32[]{:S(2)}, u32[]{:S(2)}) collective-permute-start(bf16[512,256]{1,0:T(8,128)(2,1)S(1)} %shard_map.111), channel_id=1, source_target_pairs={{0,2},{1,3},{2,0},{3,1},{4,6},{5,7},{6,4},{7,5},{8,10},{9,11},{10,... | collective-permute-start | bytes 786440 | tf_op jit(solution)/shard_map/ppermute | solution.py:16
  34.4 2.7 %collective-permute-start.5 = (bf16[4096,128]{1,0:T(8,128)(2,1)S(1)}, bf16[4096,128]{1,0:T(8,128)(2,1)S(1)}, u32[]{:S(2)}, u32[]{:S(2)}) collective-permute-start(bf16[4096,128]{1,0:T(8,128)(2,1)S(1)} %get-tuple-element.14), channel_id=1, source_target_pairs={{0,1},{1,0},{2,3},{3,2},{4,5},{5,4},{6,7},{7,6},{8,9},{9,8},{10,11... | collective-permute-start | bytes 3145736 | tf_op jit(solution)/shard_map/ppermute | solution.py:16
  37.4 24.2 %copy-start.2 = (bf16[512,256]{1,0:T(8,128)(2,1)S(1)}, bf16[512,256]{1,0:T(8,128)(2,1)}, u32[]{:S(2)}) copy-start(bf16[512,256]{1,0:T(8,128)(2,1)} %array_ref.1) | copy-start | bytes 786436
  37.4 24.2 %copy-start.3 = (f32[256]{0:T(256)S(1)}, f32[256]{0:T(256)}, u32[]{:S(2)}) copy-start(f32[256]{0:T(256)} %param.10) | copy-start | bytes 3076
  37.4 10.8 %collective-permute-start.6 = (bf16[1024,128]{1,0:T(8,128)(2,1)S(1)}, bf16[1024,128]{1,0:T(8,128)(2,1)S(1)}, u32[]{:S(2)}, u32[]{:S(2)}) collective-permute-start(bf16[1024,128]{1,0:T(8,128)(2,1)S(1)} %get-tuple-element.27), channel_id=1, source_target_pairs={{0,8},{1,9},{2,10},{3,11},{4,12},{5,13},{6,14},{7,15},{8,0},{9,1},... | collective-permute-start | bytes 786440 | tf_op jit(solution)/shard_map/ppermute | solution.py:16
  40.7 12.3 %collective-permute-start.8 = (bf16[1024,128]{1,0:T(8,128)(2,1)S(1)}, bf16[1024,128]{1,0:T(8,128)(2,1)S(1)}, u32[]{:S(2)}, u32[]{:S(2)}) collective-permute-start(bf16[1024,128]{1,0:T(8,128)(2,1)S(1)} %get-tuple-element.28), channel_id=1, source_target_pairs={{0,12},{1,13},{2,14},{3,15},{4,8},{5,9},{6,10},{7,11},{8,4},{9,5},... | collective-permute-start | bytes 786440 | tf_op jit(solution)/shard_map/ppermute | solution.py:16
  40.7 12.3 %collective-permute-start.7 = (bf16[1024,128]{1,0:T(8,128)(2,1)S(1)}, bf16[1024,128]{1,0:T(8,128)(2,1)S(1)}, u32[]{:S(2)}, u32[]{:S(2)}) collective-permute-start(bf16[1024,128]{1,0:T(8,128)(2,1)S(1)} %get-tuple-element.29), channel_id=1, source_target_pairs={{0,4},{1,5},{2,6},{3,7},{4,0},{5,1},{6,2},{7,3},{8,12},{9,13},{10,... | collective-permute-start | bytes 786440 | tf_op jit(solution)/shard_map/ppermute | solution.py:16
  53.1 8.3 %collective-permute-start.9 = (bf16[1024,128]{1,0:T(8,128)(2,1)S(1)}, bf16[1024,128]{1,0:T(8,128)(2,1)S(1)}, u32[]{:S(2)}, u32[]{:S(2)}) collective-permute-start(bf16[1024,128]{1,0:T(8,128)(2,1)S(1)} %pad_maximum_fusion), channel_id=1, source_target_pairs={{0,2},{1,3},{2,0},{3,1},{4,6},{5,7},{6,4},{7,5},{8,10},{9,11},{10,... | collective-permute-start | bytes 786440 | tf_op jit(solution)/shard_map/ppermute | solution.py:16
  62.9 14.3 %collective-permute-start.12 = (bf16[1024,128]{1,0:T(8,128)(2,1)S(1)}, bf16[1024,128]{1,0:T(8,128)(2,1)S(1)}, u32[]{:S(2)}, u32[]{:S(2)}) collective-permute-start(bf16[1024,128]{1,0:T(8,128)(2,1)S(1)} %bitcast.19), channel_id=1, source_target_pairs={{0,12},{1,13},{2,14},{3,15},{4,8},{5,9},{6,10},{7,11},{8,4},{9,5},... | collective-permute-start | bytes 786440 | tf_op jit(solution)/shard_map/ppermute | solution.py:16
  63.9 13.4 %collective-permute-start.11 = (bf16[1024,128]{1,0:T(8,128)(2,1)S(1)}, bf16[1024,128]{1,0:T(8,128)(2,1)S(1)}, u32[]{:S(2)}, u32[]{:S(2)}) collective-permute-start(bf16[1024,128]{1,0:T(8,128)(2,1)S(1)} %bitcast.20), channel_id=1, source_target_pairs={{0,8},{1,9},{2,10},{3,11},{4,12},{5,13},{6,14},{7,15},{8,0},{9,1},... | collective-permute-start | bytes 786440 | tf_op jit(solution)/shard_map/ppermute | solution.py:16
  66.0 11.7 %collective-permute-start.10 = (bf16[1024,128]{1,0:T(8,128)(2,1)S(1)}, bf16[1024,128]{1,0:T(8,128)(2,1)S(1)}, u32[]{:S(2)}, u32[]{:S(2)}) collective-permute-start(bf16[1024,128]{1,0:T(8,128)(2,1)S(1)} %bitcast.21), channel_id=1, source_target_pairs={{0,4},{1,5},{2,6},{3,7},{4,0},{5,1},{6,2},{7,3},{8,12},{9,13},{10,... | collective-permute-start | bytes 786440 | tf_op jit(solution)/shard_map/ppermute | solution.py:16
  67.4 6.7 %collective-permute-start.22 = (f32[136,256]{1,0:T(8,128)S(1)}, f32[136,256]{1,0:T(8,128)S(1)}, u32[]{:S(2)}, u32[]{:S(2)}) collective-permute-start(f32[136,256]{1,0:T(8,128)S(1)} %pad_maximum_fusion.1), channel_id=1, source_target_pairs={{0,64},{16,80},{32,96},{48,112},{64,0},{80,16},{96,32},{112,48},{1... | collective-permute-start | bytes 417800 | tf_op jit(solution)/shard_map/ppermute | solution.py:16
  70.4 6.3 %collective-permute-start.23 = (f32[136,256]{1,0:T(8,128)S(1)}, f32[136,256]{1,0:T(8,128)S(1)}, u32[]{:S(2)}, u32[]{:S(2)}) collective-permute-start(f32[136,256]{1,0:T(8,128)S(1)} %pad_maximum_fusion.1), channel_id=1, source_target_pairs={{0,96},{16,112},{32,64},{48,80},{64,32},{80,48},{96,0},{112,16},{1... | collective-permute-start | bytes 417800 | tf_op jit(solution)/shard_map/ppermute | solution.py:16
  74.1 5.1 %collective-permute-start.21 = (f32[136,256]{1,0:T(8,128)S(1)}, f32[136,256]{1,0:T(8,128)S(1)}, u32[]{:S(2)}, u32[]{:S(2)}) collective-permute-start(f32[136,256]{1,0:T(8,128)S(1)} %pad_maximum_fusion.1), channel_id=1, source_target_pairs={{0,32},{16,48},{32,0},{48,16},{64,96},{80,112},{96,64},{112,80},{1... | collective-permute-start | bytes 417800 | tf_op jit(solution)/shard_map/ppermute | solution.py:16
  76.8 4.9 %collective-permute-start.13 = (bf16[1024,128]{1,0:T(8,128)(2,1)S(1)}, bf16[1024,128]{1,0:T(8,128)(2,1)S(1)}, u32[]{:S(2)}, u32[]{:S(2)}) collective-permute-start(bf16[1024,128]{1,0:T(8,128)(2,1)S(1)} %bitcast.22), channel_id=1, source_target_pairs={{0,1},{1,0},{2,3},{3,2},{4,5},{5,4},{6,7},{7,6},{8,9},{9,8},{10,11... | collective-permute-start | bytes 786440 | tf_op jit(solution)/shard_map/ppermute | solution.py:16
  77.1 4.5 %collective-permute-start.16 = (bf16[1024,128]{1,0:T(8,128)(2,1)S(1)}, bf16[1024,128]{1,0:T(8,128)(2,1)S(1)}, u32[]{:S(2)}, u32[]{:S(2)}) collective-permute-start(bf16[1024,128]{1,0:T(8,128)(2,1)S(1)} %collective-permute-done.12.refs_4_), channel_id=1, source_target_pairs={{0,1},{1,0},{2,3},{3,2},{4,5},{5,4},{6,7},{7,6},{8,9},{9,8},{10,11... | collective-permute-start | bytes 786440 | tf_op jit(solution)/shard_map/ppermute | solution.py:16
  77.3 4.4 %collective-permute-start.15 = (bf16[1024,128]{1,0:T(8,128)(2,1)S(1)}, bf16[1024,128]{1,0:T(8,128)(2,1)S(1)}, u32[]{:S(2)}, u32[]{:S(2)}) collective-permute-start(bf16[1024,128]{1,0:T(8,128)(2,1)S(1)} %collective-permute-done.11.refs_3_), channel_id=1, source_target_pairs={{0,1},{1,0},{2,3},{3,2},{4,5},{5,4},{6,7},{7,6},{8,9},{9,8},{10,11... | collective-permute-start | bytes 786440 | tf_op jit(solution)/shard_map/ppermute | solution.py:16
  77.8 3.9 %collective-permute-start.14 = (bf16[1024,128]{1,0:T(8,128)(2,1)S(1)}, bf16[1024,128]{1,0:T(8,128)(2,1)S(1)}, u32[]{:S(2)}, u32[]{:S(2)}) collective-permute-start(bf16[1024,128]{1,0:T(8,128)(2,1)S(1)} %collective-permute-done.10.refs_2_), channel_id=1, source_target_pairs={{0,1},{1,0},{2,3},{3,2},{4,5},{5,4},{6,7},{7,6},{8,9},{9,8},{10,11... | collective-permute-start | bytes 786440 | tf_op jit(solution)/shard_map/ppermute | solution.py:16
  79.2 13.3 %collective-permute-start.24 = (f32[136,256]{1,0:T(8,128)S(1)}, f32[136,256]{1,0:T(8,128)S(1)}, u32[]{:S(2)}, u32[]{:S(2)}) collective-permute-start(f32[136,256]{1,0:T(8,128)S(1)} %add_add_fusion.1), channel_id=1, source_target_pairs={{0,16},{16,0},{32,48},{48,32},{64,80},{80,64},{96,112},{112,96},{1... | collective-permute-start | bytes 417800 | tf_op jit(solution)/shard_map/ppermute | solution.py:16
  92.5 5.1 %collective-permute-start.25 = (f32[136,256]{1,0:T(8,128)S(1)}, f32[136,256]{1,0:T(8,128)S(1)}, u32[]{:S(2)}, u32[]{:S(2)}) collective-permute-start(f32[136,256]{1,0:T(8,128)S(1)} %add_add_fusion), channel_id=1, source_target_pairs={{0,2},{1,3},{2,0},{3,1},{4,6},{5,7},{6,4},{7,5},{8,10},{9,11},{10,... | collective-permute-start | bytes 417800 | tf_op jit(solution)/shard_map/ppermute | solution.py:16
  92.7 13.4 %collective-permute-start.17 = (bf16[1024,128]{1,0:T(8,128)(2,1)S(1)}, bf16[1024,128]{1,0:T(8,128)(2,1)S(1)}, u32[]{:S(2)}, u32[]{:S(2)}) collective-permute-start(bf16[1024,128]{1,0:T(8,128)(2,1)S(1)} %get-tuple-element.24), channel_id=1, source_target_pairs={{0,64},{16,80},{32,96},{48,112},{64,0},{80,16},{96,32},{112,48},{1... | collective-permute-start | bytes 786440 | tf_op jit(solution)/shard_map/ppermute | solution.py:16
  95.3 11.8 %collective-permute-start.19 = (bf16[1024,128]{1,0:T(8,128)(2,1)S(1)}, bf16[1024,128]{1,0:T(8,128)(2,1)S(1)}, u32[]{:S(2)}, u32[]{:S(2)}) collective-permute-start(bf16[1024,128]{1,0:T(8,128)(2,1)S(1)} %get-tuple-element.25), channel_id=1, source_target_pairs={{0,96},{16,112},{32,64},{48,80},{64,32},{80,48},{96,0},{112,16},{1... | collective-permute-start | bytes 786440 | tf_op jit(solution)/shard_map/ppermute | solution.py:16
  97.2 9.9 %collective-permute-start.18 = (bf16[1024,128]{1,0:T(8,128)(2,1)S(1)}, bf16[1024,128]{1,0:T(8,128)(2,1)S(1)}, u32[]{:S(2)}, u32[]{:S(2)}) collective-permute-start(bf16[1024,128]{1,0:T(8,128)(2,1)S(1)} %get-tuple-element.26), channel_id=1, source_target_pairs={{0,32},{16,48},{32,0},{48,16},{64,96},{80,112},{96,64},{112,80},{1... | collective-permute-start | bytes 786440 | tf_op jit(solution)/shard_map/ppermute | solution.py:16
  97.7 5.1 %collective-permute-start.26 = (f32[136,256]{1,0:T(8,128)S(1)}, f32[136,256]{1,0:T(8,128)S(1)}, u32[]{:S(2)}, u32[]{:S(2)}) collective-permute-start(f32[136,256]{1,0:T(8,128)S(1)} %add.131), channel_id=1, source_target_pairs={{0,4},{1,5},{2,6},{3,7},{4,0},{5,1},{6,2},{7,3},{8,12},{9,13},{10,... | collective-permute-start | bytes 417800 | tf_op jit(solution)/shard_map/ppermute | solution.py:16
  102.8 7.5 %collective-permute-start.27 = (f32[136,256]{1,0:T(8,128)S(1)}, f32[136,256]{1,0:T(8,128)S(1)}, u32[]{:S(2)}, u32[]{:S(2)}) collective-permute-start(f32[136,256]{1,0:T(8,128)S(1)} %add.132), channel_id=1, source_target_pairs={{0,8},{1,9},{2,10},{3,11},{4,12},{5,13},{6,14},{7,15},{8,0},{9,1},... | collective-permute-start | bytes 417800 | tf_op jit(solution)/shard_map/ppermute | solution.py:16
  107.2 6.8 %collective-permute-start.20 = (bf16[512,128]{1,0:T(8,128)(2,1)S(1)}, bf16[512,128]{1,0:T(8,128)(2,1)S(1)}, u32[]{:S(2)}, u32[]{:S(2)}) collective-permute-start(bf16[512,128]{1,0:T(8,128)(2,1)S(1)} %slice.79), channel_id=1, source_target_pairs={{0,16},{16,0},{32,48},{48,32},{64,80},{80,64},{96,112},{112,96},{1... | collective-permute-start | bytes 393224 | tf_op jit(solution)/shard_map/ppermute | solution.py:16
  110.4 3.7 %collective-permute-start.28 = (f32[136,256]{1,0:T(8,128)S(1)}, f32[136,256]{1,0:T(8,128)S(1)}, u32[]{:S(2)}, u32[]{:S(2)}) collective-permute-start(f32[136,256]{1,0:T(8,128)S(1)} %add.133.terms_ref), channel_id=1, source_target_pairs={{0,1},{1,0},{2,3},{3,2},{4,5},{5,4},{6,7},{7,6},{8,9},{9,8},{10,11... | collective-permute-start | bytes 417800 | tf_op jit(solution)/shard_map/ppermute | solution.py:16
